TPU v7x, 32 devices: a whole 2x2x4 slice. The times are simulated.
32 devices in a mesh: groups: 2 (over x), visit: 16 (over z, y, core).
Axes of the slice: x: 2, y: 2, z: 4, core: 2. Of those that a mesh axis runs over, the one named last changes fastest.
Arguments:
- visit_image: bfloat16 [32, 256, 1024], P(('groups', 'visit')), parts along dimension 0, may hold values from -6 to 6
- band_offset: int32 [32, 2], P(('groups', 'visit')), parts along dimension 0, may hold values from -8 to 8
- shift_frac: float32 [32, 2], P(('groups', 'visit')), parts along dimension 0, may hold values from 0 to 1
- weights: bfloat16 [32], P(('groups', 'visit')), parts along dimension 0, may hold values from 0.29882812 to 3
- box_owner: int32 [32, 128, 1], P(('groups', 'visit')), parts along dimension 0, may hold values from 0 to 15; in each aligned block of 128 rows (0 to 127, 128 to 255, ..., all dimensions but the last counted through in order) at most 16 rows name the same one
- box_slot: int32 [32, 128], P(('groups', 'visit')), parts along dimension 0, may hold values from 0 to 15
- basis_index: int32 [32, 6], P(('groups', 'visit')), parts along dimension 0, may hold values from 0 to 11
- basis_coef: float32 [32, 6], P(('groups', 'visit')), parts along dimension 0, may hold values from 0.1 to 0.3
- basis_width: float32 [12], replicated, may hold values from 0.7 to 4
Outputs:
- template_coadd: bfloat16 [512, 16, 128], P(('groups', 'visit')), parts along dimension 0
- difference_coadd: float32 [512, 16, 128], P(('groups', 'visit')), parts along dimension 0
There are 2 independent parts, one for each index of `groups`. A program takes and returns all parts, laid end to end along the dimension named above; an argument that names none is the same for every part. Nothing has to cross between parts.
Inputs may be any that keep to these rules, and one draw needn't show every extreme that they name: `box_owner`: among the 128 boxes of one visit no owner is named more than 16 times, and in every draw some visit names some owner exactly 16 times.
All inputs are finite; a program needn't handle non-finite values.
Results may differ from a plain program's by a relative error of at most 0.012.
The roundings to bfloat16 on the way count: a program that leaves them out, or rounds other values in their place, can miss the bound.
Values may be sent and summed in bfloat16 or wider, within the bound.
No kernel may reach another device: no remote copies, remote signals or barrier semaphores. Data moves between devices by JAX's collectives and lax.ppermute only.
A program may use at most 64 MiB of HBM per device.

v0:
```python
import jax
import jax.numpy as jnp
from jax import lax
from jax.sharding import PartitionSpec as P

BH = 16
BW = 128
PS = 16


band_reach = 8.0


def lanczos_band(extent, shift_by, by_rows):
    out_index = jnp.arange(extent, dtype=jnp.float32)[:, None]
    in_index = jnp.arange(extent, dtype=jnp.float32)[None, :]
    if by_rows:
        offset = in_index - out_index - shift_by
    else:
        offset = out_index - in_index - shift_by
    kernel_value = jnp.sinc(offset) * jnp.sinc(offset / 3.0)
    return jnp.where(jnp.abs(offset) < 3.0, kernel_value, 0.0).astype(jnp.bfloat16)


def gauss_band(extent, blur_width):
    out_index = jnp.arange(extent, dtype=jnp.float32)[:, None]
    in_index = jnp.arange(extent, dtype=jnp.float32)[None, :]
    pixel_gap = out_index - in_index
    tap_offsets = jnp.arange(17, dtype=jnp.float32) - 8.0
    spread = 2.0 * blur_width * blur_width
    tap_total = jnp.sum(jnp.exp(-tap_offsets * tap_offsets / spread))
    kernel_value = jnp.where(
        jnp.abs(pixel_gap) <= band_reach, jnp.exp(-pixel_gap * pixel_gap / spread), 0.0
    )
    return (kernel_value / tap_total).astype(jnp.bfloat16)


def to_boxes(picture, box_rows, box_cols):
    pix_rows, pix_cols = picture.shape
    split = picture.reshape(pix_rows // box_rows, box_rows, pix_cols // box_cols, box_cols)
    return split.transpose(0, 2, 1, 3).reshape(-1, box_rows * box_cols)


def from_boxes(flat_boxes, pix_rows, pix_cols, box_rows, box_cols):
    split = flat_boxes.reshape(pix_rows // box_rows, pix_cols // box_cols, box_rows, box_cols)
    return split.transpose(0, 2, 1, 3).reshape(pix_rows, pix_cols)


def tag_product(tag_rows, box_data):
    return lax.dot_general(
        tag_rows, box_data, (((0,), (0,)), ((), ())), preferred_element_type=jnp.float32
    )


def shards(
    visit_image,
    band_offset,
    shift_frac,
    weights,
    box_owner,
    box_slot,
    basis_index,
    basis_coef,
    basis_width,
):
    picture = visit_image[0]
    pix_rows, pix_cols = picture.shape
    shifts = band_offset[0].astype(jnp.float32) + shift_frac[0]
    row_warp = lanczos_band(pix_rows, shifts[0], True)
    col_warp = lanczos_band(pix_cols, shifts[1], False)
    col_pass = jnp.dot(picture, col_warp, preferred_element_type=jnp.float32).astype(jnp.bfloat16)
    warped = jnp.dot(row_warp, col_pass, preferred_element_type=jnp.float32).astype(jnp.bfloat16)
    box_data = to_boxes(warped, BH, BW)
    box_count = box_data.shape[0]
    peer_count = lax.axis_size("visit")
    capacity = max(2, 2 * box_count // peer_count)
    dest_ids = box_owner[0, :, 0]
    slot_ids = box_slot[0]
    dest_hits = (dest_ids[:, None] == jnp.arange(peer_count, dtype=jnp.int32)[None, :]).astype(
        jnp.int32
    )
    earlier = jnp.cumsum(dest_hits, axis=0) - dest_hits
    dest_rank = jnp.sum(earlier * dest_hits, axis=1)
    buffer_row = dest_ids * capacity + dest_rank
    visit_weight = weights[0]
    slot_hits = slot_ids[:, None] == jnp.arange(PS, dtype=jnp.int32)[None, :]
    tag_rows = jnp.where(slot_hits, visit_weight, jnp.zeros((), jnp.bfloat16))
    sent_boxes = (
        jnp.zeros((peer_count * capacity, box_data.shape[1]), jnp.bfloat16)
        .at[buffer_row]
        .set(box_data)
    )
    sent_tags = jnp.zeros((peer_count * capacity, PS), jnp.bfloat16).at[buffer_row].set(tag_rows)
    received, received_tags = (
        lax.all_to_all(sent_boxes, "visit", split_axis=0, concat_axis=0, tiled=True),
        lax.all_to_all(sent_tags, "visit", split_axis=0, concat_axis=0, tiled=True),
    )
    summed = tag_product(received_tags, received)
    weight_sum = 1.0 + jnp.sum(received_tags.astype(jnp.float32), axis=0)
    template = (summed / weight_sum[:, None]).astype(jnp.bfloat16)
    chosen = (received_tags > 0).astype(jnp.bfloat16)
    reply_rows = jnp.dot(chosen, template, preferred_element_type=jnp.float32).astype(jnp.bfloat16)
    came_back = lax.all_to_all(reply_rows, "visit", split_axis=0, concat_axis=0, tiled=True)
    returned_boxes = came_back[buffer_row]
    template_image = from_boxes(returned_boxes, pix_rows, pix_cols, BH, BW)
    basis_ids = jnp.arange(basis_width.shape[0], dtype=jnp.int32)
    matched = jnp.zeros((pix_rows, pix_cols), jnp.float32)
    for member in range(basis_index.shape[1]):
        blur_width = jnp.sum(jnp.where(basis_ids == basis_index[0, member], basis_width, 0.0))
        across = gauss_band(pix_cols, blur_width)
        down_band = gauss_band(pix_rows, blur_width)
        blurred = jnp.dot(template_image, across, preferred_element_type=jnp.float32).astype(
            jnp.bfloat16
        )
        matched = matched + basis_coef[0, member] * jnp.dot(
            down_band, blurred, preferred_element_type=jnp.float32
        )
    difference = (warped.astype(jnp.float32) - matched).astype(jnp.bfloat16)
    diff_boxes = to_boxes(difference, BH, BW)
    sent_diff = (
        jnp.zeros((peer_count * capacity, diff_boxes.shape[1]), jnp.bfloat16)
        .at[buffer_row]
        .set(diff_boxes)
    )
    received_diff = lax.all_to_all(sent_diff, "visit", split_axis=0, concat_axis=0, tiled=True)
    difference_coadd = tag_product(received_tags, received_diff) / weight_sum[:, None]
    return (template.reshape(PS, BH, BW), difference_coadd.reshape(PS, BH, BW))


def solution(mesh):
    placed = (
        P(("groups", "visit"), None, None),
        P(("groups", "visit"), None),
        P(("groups", "visit"), None),
        P(("groups", "visit")),
        P(("groups", "visit"), None, None),
        P(("groups", "visit"), None),
        P(("groups", "visit"), None),
        P(("groups", "visit"), None),
        P(),
    )
    return jax.shard_map(
        shards,
        mesh=mesh,
        in_specs=placed,
        out_specs=(P(("groups", "visit"), None, None), P(("groups", "visit"), None, None)),
        check_vma=False,
    )
```

profile of v0, /device:TPU:0, one launch (start us, length us, event | category | flops | bytes accessed | tf_op | source)
XLA Modules:
  0.0 153.3 jit_solution(590456195435126809)
XLA Ops:
  0.6 0.8 fusion.171
  1.6 0.8 select_reduce_fusion
  2.4 0.7 fusion.185
  3.8 1.1 scatter_custom_fusion
  5.0 0.7 reshape.125
  5.7 7.4 %all-to-all-start = ((bf16[16,2,128]{2,1,0:T(2,128)(2,1)}), bf16[16,2,128]{2,1,0:T(2,128)(2,1)S(1)}, u32[]{:S(2)}, u32[]{:S(2)}) async-start(bf16[16,2,128]{2,1,0:T(2,128)(2,1)} %reshape.125), calls=%async_computation | async-start | bytes 16384 | tf_op jit(solution)/shard_map/all_to_all | solution.py:96
  13.1 0.7 convert_add_fusion
  13.8 0.7 fusion.238
  14.4 12.7 %convolution_convert_fusion.1 = bf16[256,1024]{1,0:T(8,128)(2,1)S(1)} fusion(f32[]{:T(128)} %bitcast.8, bf16[1,256,1024]{2,1,0:T(8,128)(2,1)S(1)} %copy-done, f32[]{:T(128)} %bitcast.7), kind=kOutput, calls=%fused_computation.112 | convolution fusion | flops 752943104 | bytes 1048584 | tf_op jit(solution)/shard_map/dot_general | solution.py:72
  27.3 2.6 %scatter_custom_fusion.1 = bf16[256,2048]{1,0:T(8,128)(2,1)} fusion(s32[128]{0:T(128)S(1)} %fusion.185, bf16[]{:T(256)} %constant.11.clone.1, bf16[16,16,8,128]{3,2,1,0:T(8,128)(2,1)S(1)} %bitcast.117), kind=kCustom, calls=%fused_computation.126 | custom fusion | bytes 1572866 | tf_op jit(solution)/shard_map/scatter | solution.py:91
  29.9 6.0 %all-to-all-start.1 = ((bf16[16,16,2048]{2,1,0:T(8,128)(2,1)}), bf16[16,16,2048]{2,1,0:T(8,128)(2,1)S(1)}, u32[]{:S(2)}, u32[]{:S(2)}) async-start(bf16[16,16,2048]{2,1,0:T(8,128)(2,1)} %bitcast.12), calls=%async_computation.1 | async-start | bytes 2097152 | tf_op jit(solution)/shard_map/all_to_all | solution.py:95
  36.3 22.5 %all-to-all-done.1 = bf16[16,16,2048]{2,1,0:T(8,128)(2,1)S(1)} async-done(((bf16[16,16,2048]{2,1,0:T(8,128)(2,1)}), bf16[16,16,2048]{2,1,0:T(8,128)(2,1)S(1)}, u32[]{:S(2)}, u32[]{:S(2)}) %all-to-all-start.1) | async-done | bytes 1048608 | tf_op jit(solution)/shard_map/all_to_all | solution.py:95
  59.3 1.5 convolution_convert_fusion
  60.8 7.0 %all-to-all-start.2 = ((bf16[16,16,2048]{2,1,0:T(8,128)(2,1)}), bf16[16,16,2048]{2,1,0:T(8,128)(2,1)S(1)}, u32[]{:S(2)}, u32[]{:S(2)}) async-start(bf16[16,16,2048]{2,1,0:T(8,128)(2,1)} %bitcast.16), calls=%async_computation.2 | async-start | bytes 2097152 | tf_op jit(solution)/shard_map/all_to_all | solution.py:103
  67.8 0.7 fusion.237
  68.5 4.5 %fusion.184 = (f32[]{:T(128)}, f32[]{:T(128)}, f32[]{:T(128)}, f32[]{:T(128)}, f32[]{:T(128)}, /*index=5*/f32[]{:T(128)}) fusion(f32[12]{0:T(128)S(1)} %copy-done.3, s32[]{:T(128)} %bitcast.29, s32[]{:T(128)} %bitcast.25, s32[]{:T(128)} %bitcast.23, s32[]{:T(128)} %bitcast.21, s32[]{:T(128)} %bitcast.15, s32[]{:T(128)} %bitcast.27), kind=kLoop, calls=%fused_computation.257 | loop fusion | flops 210 | bytes 96 | tf_op jit(solution)/shard_map/reduce_sum | solution.py:109
  81.0 0.7 exponential_reduce_fusion.4
  81.7 0.7 exponential_reduce_fusion.3
  83.7 0.7 exponential_reduce_fusion
  84.4 0.7 fusion.236
  85.0 5.7 %all-to-all-done.2 = bf16[16,16,2048]{2,1,0:T(8,128)(2,1)S(1)} async-done(((bf16[16,16,2048]{2,1,0:T(8,128)(2,1)}), bf16[16,16,2048]{2,1,0:T(8,128)(2,1)S(1)}, u32[]{:S(2)}, u32[]{:S(2)}) %all-to-all-start.2) | async-done | bytes 1048608 | tf_op jit(solution)/shard_map/all_to_all | solution.py:103
  90.7 0.9 gather_fusion
  91.6 4.5 %convolution_multiply_fusion.5 = f32[256,1024]{1,0:T(8,128)} fusion(f32[]{:T(128)} %exponential_reduce_fusion.5, f32[]{:T(128)S(6)} %mul.256, f32[]{:T(128)} %bitcast.14, bf16[32,8,8,128]{3,2,1,0:T(8,128)(2,1)S(1)} %bitcast.118), kind=kOutput, calls=%fused_computation.105 | convolution fusion | flops 681639936 | bytes 1572876 | tf_op jit(solution)/shard_map/dot_general | solution.py:115
  96.2 4.8 %fusion.62 = f32[256,1024]{1,0:T(8,128)S(1)} fusion(f32[256,1024]{1,0:T(8,128)} %convolution_multiply_fusion.5, f32[]{:T(128)} %exponential_reduce_fusion.4, f32[]{:T(128)S(6)} %mul.262, f32[]{:T(128)} %bitcast.20, bf16[32,8,8,128]{3,2,1,0:T(8,128)(2,1)S(1)} %bitcast.119), kind=kOutput, calls=%fused_computation.104 | convolution fusion | flops 681902080 | bytes 2621452 | tf_op jit(solution)/shard_map/dot_general | solution.py:115
  101.0 4.5 %fusion.61 = f32[256,1024]{1,0:T(8,128)} fusion(f32[256,1024]{1,0:T(8,128)S(1)} %fusion.62, f32[]{:T(128)} %exponential_reduce_fusion.3, f32[]{:T(128)S(6)} %mul.266, f32[]{:T(128)} %bitcast.22, bf16[32,8,8,128]{3,2,1,0:T(8,128)(2,1)S(1)} %bitcast.120), kind=kOutput, calls=%fused_computation.102 | convolution fusion | flops 681902080 | bytes 2621452 | tf_op jit(solution)/shard_map/dot_general | solution.py:115
  105.6 4.8 %fusion.60 = f32[256,1024]{1,0:T(8,128)S(1)} fusion(f32[256,1024]{1,0:T(8,128)} %fusion.61, f32[]{:T(128)} %exponential_reduce_fusion.2, f32[]{:T(128)S(6)} %mul.270, f32[]{:T(128)} %bitcast.24, bf16[32,8,8,128]{3,2,1,0:T(8,128)(2,1)S(1)} %bitcast.121), kind=kOutput, calls=%fused_computation.100 | convolution fusion | flops 681902080 | bytes 2621452 | tf_op jit(solution)/shard_map/dot_general | solution.py:115
  110.3 4.4 %fusion.59 = f32[256,1024]{1,0:T(8,128)} fusion(f32[256,1024]{1,0:T(8,128)S(1)} %fusion.60, f32[]{:T(128)} %exponential_reduce_fusion.1, f32[]{:T(128)S(6)} %mul.274, f32[]{:T(128)} %bitcast.26, bf16[32,8,8,128]{3,2,1,0:T(8,128)(2,1)S(1)} %bitcast.122), kind=kOutput, calls=%fused_computation.98 | convolution fusion | flops 681902080 | bytes 2621452 | tf_op jit(solution)/shard_map/dot_general | solution.py:115
  114.7 5.1 %fusion.73 = bf16[32,8,8,128]{3,1,2,0:T(8,128)(2,1)S(1)} fusion(f32[256,1024]{1,0:T(8,128)} %fusion.59, bf16[256,1024]{1,0:T(8,128)(2,1)S(1)} %convolution_convert_fusion.1, f32[]{:T(128)} %exponential_reduce_fusion, f32[]{:T(128)S(6)} %mul.278, f32[]{:T(128)} %bitcast.28, bf16[32,8,8,128]{3,2,1,0:T(8,128)(2,1)S(1)} %bitcast.123), kind=kOutput, calls=%fused_computation.115 | convolution fusion | flops 682688512 | bytes 2621452 | tf_op jit(solution)/shard_map/dot_general | solution.py:115
  119.9 2.5 %scatter_custom_fusion.2 = bf16[256,2048]{1,0:T(8,128)(2,1)} fusion(s32[128]{0:T(128)S(1)} %fusion.185, bf16[]{:T(256)} %constant.11.clone.1, bf16[16,16,8,128]{3,2,1,0:T(8,128)(2,1)S(1)} %bitcast.116), kind=kCustom, calls=%fused_computation.118 | custom fusion | bytes 1572866 | tf_op jit(solution)/shard_map/scatter | solution.py:123
  122.4 6.9 %all-to-all-start.3 = ((bf16[16,16,2048]{2,1,0:T(8,128)(2,1)}), bf16[16,16,2048]{2,1,0:T(8,128)(2,1)S(1)}, u32[]{:S(2)}, u32[]{:S(2)}) async-start(bf16[16,16,2048]{2,1,0:T(8,128)(2,1)} %bitcast.32), calls=%async_computation.3 | async-start | bytes 2097152 | tf_op jit(solution)/shard_map/all_to_all | solution.py:125
  129.9 22.3 %all-to-all-done.3 = bf16[16,16,2048]{2,1,0:T(8,128)(2,1)S(1)} async-done(((bf16[16,16,2048]{2,1,0:T(8,128)(2,1)}), bf16[16,16,2048]{2,1,0:T(8,128)(2,1)S(1)}, u32[]{:S(2)}, u32[]{:S(2)}) %all-to-all-start.3) | async-done | bytes 1048608 | tf_op jit(solution)/shard_map/all_to_all | solution.py:125
  152.6 0.7 copy.22
  (26 shorter events, 4.2 us)
Async XLA Ops:
  0.6 13.8 %copy-start = (bf16[1,256,1024]{2,1,0:T(8,128)(2,1)S(1)}, bf16[1,256,1024]{2,1,0:T(8,128)(2,1)}, u32[]{:S(2)}) copy-start(bf16[1,256,1024]{2,1,0:T(8,128)(2,1)} %param.11) | copy-start | bytes 1572868
  5.7 24.2 %all-to-all-start = ((bf16[16,2,128]{2,1,0:T(2,128)(2,1)}), bf16[16,2,128]{2,1,0:T(2,128)(2,1)S(1)}, u32[]{:S(2)}, u32[]{:S(2)}) async-start(bf16[16,2,128]{2,1,0:T(2,128)(2,1)} %reshape.125), calls=%async_computation | async-start | bytes 16384 | tf_op jit(solution)/shard_map/all_to_all | solution.py:96
  29.9 29.0 %all-to-all-start.1 = ((bf16[16,16,2048]{2,1,0:T(8,128)(2,1)}), bf16[16,16,2048]{2,1,0:T(8,128)(2,1)S(1)}, u32[]{:S(2)}, u32[]{:S(2)}) async-start(bf16[16,16,2048]{2,1,0:T(8,128)(2,1)} %bitcast.12), calls=%async_computation.1 | async-start | bytes 2097152 | tf_op jit(solution)/shard_map/all_to_all | solution.py:95
  60.8 7.0 %copy-start.1 = (s32[1,6]{1,0:T(1,128)S(1)}, s32[1,6]{1,0:T(1,128)}, u32[]{:S(2)}) copy-start(s32[1,6]{1,0:T(1,128)} %param.17) | copy-start | bytes 76
  60.8 7.7 %copy-start.3 = (f32[12]{0:T(128)S(1)}, f32[12]{0:T(128)}, u32[]{:S(2)}) copy-start(f32[12]{0:T(128)} %param.19) | copy-start | bytes 148
  60.8 23.6 %copy-start.2 = (f32[1,6]{1,0:T(1,128)S(1)}, f32[1,6]{1,0:T(1,128)}, u32[]{:S(2)}) copy-start(f32[1,6]{1,0:T(1,128)} %param.18) | copy-start | bytes 76
  60.8 29.9 %all-to-all-start.2 = ((bf16[16,16,2048]{2,1,0:T(8,128)(2,1)}), bf16[16,16,2048]{2,1,0:T(8,128)(2,1)S(1)}, u32[]{:S(2)}, u32[]{:S(2)}) async-start(bf16[16,16,2048]{2,1,0:T(8,128)(2,1)} %bitcast.16), calls=%async_computation.2 | async-start | bytes 2097152 | tf_op jit(solution)/shard_map/all_to_all | solution.py:103
  122.4 29.8 %all-to-all-start.3 = ((bf16[16,16,2048]{2,1,0:T(8,128)(2,1)}), bf16[16,16,2048]{2,1,0:T(8,128)(2,1)S(1)}, u32[]{:S(2)}, u32[]{:S(2)}) async-start(bf16[16,16,2048]{2,1,0:T(8,128)(2,1)} %bitcast.32), calls=%async_computation.3 | async-start | bytes 2097152 | tf_op jit(solution)/shard_map/all_to_all | solution.py:125
where the time goes:
time: 155 us; the launch traced here: 153 us
  waiting for transfers between devices  50.5 us (33%)
  matrix products  43.2 us (28%)
  starting transfers between devices  27.2 us (18%)
  other arithmetic  12.8 us (8%)
  local copies, waits for them, and re-layouts  10.6 us (7%)
  between operations  8.94 us (6%)
    dot_general x6, matrix products, shards(): jnp.dot(down_band, blurred, preferred_element_type=jnp.float32)  28.1 us
    all_to_all x1, waiting for transfers between devices, shards(): lax.all_to_all(sent_boxes, 'visit', split_axis=0, concat_axis=0, tiled=True)  22.5 us
    all_to_all x1, waiting for transfers between devices, shards(): lax.all_to_all(sent_diff, 'visit', split_axis=0, concat_axis=0, tiled=True)  22.3 us
    dot_general x1, matrix products, shards(): jnp.dot(row_warp, col_pass, preferred_element_type=jnp.float32)  12.7 us
    all_to_all x1, starting transfers between devices, shards(): lax.all_to_all(sent_tags, 'visit', split_axis=0, concat_axis=0, tiled=True)  7.39 us
    all_to_all x1, starting transfers between devices, shards(): lax.all_to_all(reply_rows, 'visit', split_axis=0, concat_axis=0, tiled=True)  7 us
    all_to_all x1, starting transfers between devices, shards(): lax.all_to_all(sent_diff, 'visit', split_axis=0, concat_axis=0, tiled=True)  6.86 us
    all_to_all x1, starting transfers between devices, shards(): lax.all_to_all(sent_boxes, 'visit', split_axis=0, concat_axis=0, tiled=True)  6.01 us
  transfers between devices with their start and end apart: 4, of which 3 were waited for; matrix products, arithmetic and copies ran while one was open for 18% of the time, Pallas kernels for 0%

commit v1 on v0

v1 whole, which is shorter than its diff:
```python
import functools

import jax
import jax.numpy as jnp
from jax import lax
from jax.experimental import pallas as pl
from jax.experimental.pallas import tpu as pltpu
from jax.sharding import PartitionSpec as P

BH = 16
BW = 128
PS = 16
SIDE = 128
WIDE = 256

band_reach = 8.0

VMEM = pl.BlockSpec(memory_space=pltpu.VMEM)
SMEM = pl.BlockSpec(memory_space=pltpu.SMEM)
ANY = pl.BlockSpec(memory_space=pl.ANY)


def params():
    return pltpu.CompilerParams(vmem_limit_bytes=48 * 1024 * 1024)


def place(owner, me, peers):
    away = jnp.bitwise_xor(owner, me)
    return (away & 1) * (peers // 2) + ((away >> 1) & 1) * (peers // 4) + (away >> 2)


def windows(width):
    found = []
    for first in range(0, width, WIDE):
        low, high = max(first - SIDE, 0), min(first + WIDE + SIDE, width)
        found.append((low, high, low - first + SIDE, high - first + SIDE))
    return found


def lanczos_taps(gap, whole, part):
    shift = whole.astype(jnp.float32) + part
    band = jnp.zeros(gap.shape, jnp.float32)
    for tap in range(-2, 5):
        spot = (whole + tap).astype(jnp.float32)
        x = jnp.full((8, 128), spot - shift, jnp.float32)

        def sinc(v):
            angle = jnp.pi * v
            return jnp.where(v == 0.0, 1.0, jnp.sin(angle) / jnp.where(v == 0.0, 1.0, angle))

        value = jnp.where(jnp.abs(x) < 3.0, sinc(x) * sinc(x / 3.0), 0.0)
        band = jnp.where(gap == spot, value[0:1, 0:1], band)
    return band.astype(jnp.bfloat16)


def warp_kernel(
    peers, picture, band_offset, shift_frac, weight, owner, slot, me_ref, warped, keep, send, total, wide_band
):
    rows, width = warped.shape
    me = me_ref[0]
    gap = (
        lax.broadcasted_iota(jnp.int32, (WIDE + 2 * SIDE, WIDE), 0)
        - lax.broadcasted_iota(jnp.int32, (WIDE + 2 * SIDE, WIDE), 1)
        - SIDE
    ).astype(jnp.float32)
    wide_band[...] = lanczos_taps(gap, band_offset[0, 1], shift_frac[0, 1])
    gap = (
        lax.broadcasted_iota(jnp.int32, (rows, rows), 1) - lax.broadcasted_iota(jnp.int32, (rows, rows), 0)
    ).astype(jnp.float32)
    row_warp = lanczos_taps(gap, band_offset[0, 0], shift_frac[0, 0])
    total[...] = jnp.zeros_like(total)
    heavy = weight[...].astype(jnp.float32)
    for block, (low, high, top, bottom) in enumerate(windows(width)):
        col_pass = jnp.dot(
            picture[:, low:high], wide_band[top:bottom, :], preferred_element_type=jnp.float32
        ).astype(jnp.bfloat16)
        done = jnp.dot(row_warp, col_pass, preferred_element_type=jnp.float32).astype(jnp.bfloat16)
        warped[:, block * WIDE : (block + 1) * WIDE] = done
        add_boxes(peers, me, total, done.astype(jnp.float32) * heavy, owner, slot, block, width)
    store_slots(peers, total, keep, send)


def add_boxes(peers, me, total, scaled, owner, slot, block, width):
    across = WIDE // BW
    for down in range(scaled.shape[0] // BH):
        for col in range(across):
            box = down * (width // BW) + block * across + col
            spot = place(owner[0, box], me, peers) * PS + slot[0, box]
            piece = pl.ds(pl.multiple_of(spot * BH, BH), BH)
            total[piece, :] += scaled[down * BH : (down + 1) * BH, col * BW : (col + 1) * BW]


def store_slots(peers, total, keep, send):
    half = peers // 2 * PS * BH
    step = 1024

    @pl.loop(0, half // step)
    def _(i):
        here = pl.ds(pl.multiple_of(i * step, step), step)
        there = pl.ds(pl.multiple_of(i * step + half, step), step)
        keep[here, :] = total[here, :].astype(jnp.bfloat16)
        send[here, :] = total[there, :].astype(jnp.bfloat16)


def add_kernel(parts, ours, theirs, *outs):
    length = ours.shape[0] // parts
    for i, out in enumerate(outs):
        here = pl.ds(i * length, length)
        out[...] = (ours[here, :].astype(jnp.float32) + theirs[here, :].astype(jnp.float32)).astype(jnp.bfloat16)


def add_parts(ours, theirs, parts):
    length = ours.shape[0] // parts
    return pl.pallas_call(
        functools.partial(add_kernel, parts),
        out_shape=[jax.ShapeDtypeStruct((length, BW), jnp.bfloat16)] * parts,
        in_specs=[VMEM, VMEM],
        out_specs=[VMEM] * parts,
        compiler_params=params(),
        name="add_parts",
    )(ours, theirs)


def swap(x, axis_size, bit):
    return lax.ppermute(x, "visit", [(i, i ^ bit) for i in range(axis_size)])


def scatter_sum(keep, send, peers):
    near = swap(send, peers, 1)
    ours, theirs = add_parts(keep, near, 2)
    near = swap(theirs, peers, 2)
    terms = add_parts(ours, near, peers // 4)
    return [terms[0]] + [swap(terms[far], peers, 4 * far) for far in reversed(range(1, peers // 4))]


def gather_slots(own, peers):
    far = [own] + [swap(own, peers, 4 * away) for away in range(1, peers // 4)]
    line = jnp.concatenate(far, axis=0)
    pair = jnp.concatenate([line, swap(line, peers, 2)], axis=0)
    return pair, swap(pair, peers, 1)


def weight_kernel(tags, me_ref, weight_sum):
    visits = tags.shape[0] // 2
    named = tags[0:visits, :]
    heavy = tags[visits:, :]
    lines = []
    for i in range(PS):
        target = (me_ref[0] * PS + i).astype(jnp.float32)
        hit = jnp.where(named == target, heavy, 0.0)
        lines.append(jnp.sum(jnp.sum(hit, axis=0, keepdims=True), axis=1, keepdims=True))
    weight_sum[...] = jnp.broadcast_to(1.0 + jnp.concatenate(lines, axis=0), weight_sum.shape)


def coadd_kernel(weight_sum, *refs):
    *terms, out = refs
    for i in range(PS):
        here = slice(i * BH, (i + 1) * BH)
        summed = terms[0][here, :].astype(jnp.float32)
        for term in terms[1:]:
            summed = summed + term[here, :].astype(jnp.float32)
        out[here, :] = (summed / weight_sum[i : i + 1, :]).astype(out.dtype)


def coadd(weight_sum, terms, dtype):
    return pl.pallas_call(
        coadd_kernel,
        out_shape=jax.ShapeDtypeStruct((PS * BH, BW), dtype),
        in_specs=[VMEM] * (1 + len(terms)),
        out_specs=VMEM,
        compiler_params=params(),
        name="coadd",
    )(weight_sum, *terms)


def gauss_kernel(basis_index, basis_width, bands):
    bases = bands.shape[0]
    tap = lax.broadcasted_iota(jnp.int32, (8, 128), 1).astype(jnp.float32) - band_reach
    gaps = []
    for shift in (SIDE, 0, -SIDE):
        gap = (
            lax.broadcasted_iota(jnp.int32, (SIDE, SIDE), 0) - lax.broadcasted_iota(jnp.int32, (SIDE, SIDE), 1) - shift
        ).astype(jnp.float32)
        gaps.append(gap)
    for member in range(bases):
        blur_width = basis_width[basis_index[0, member]]
        spread = 2.0 * blur_width * blur_width
        total = jnp.sum(jnp.where(tap <= band_reach, jnp.exp(-tap * tap / spread), 0.0), axis=1, keepdims=True)[0:1]
        blocks = []
        for gap in gaps:
            value = jnp.where(jnp.abs(gap) <= band_reach, jnp.exp(-gap * gap / spread), 0.0)
            blocks.append((value / total).astype(jnp.bfloat16))
        above, middle, below = blocks
        nothing = jnp.zeros_like(middle)
        for place_, pieces in enumerate(((above, nothing), (middle, above), (below, middle), (nothing, below))):
            for col, piece in enumerate(pieces):
                bands[member, place_ * SIDE : (place_ + 1) * SIDE, col * SIDE : (col + 1) * SIDE] = piece


def match_kernel(
    peers,
    warped,
    bands,
    near,
    other,
    weight,
    coef,
    owner,
    slot,
    me_ref,
    keep,
    send,
    table,
    image,
    total,
    sems,
):
    rows, width = warped.shape
    me = me_ref[0]
    half = peers // 2 * PS * BH
    copies = [
        pltpu.make_async_copy(near, table.at[pl.ds(0, half)], sems.at[0]),
        pltpu.make_async_copy(other, table.at[pl.ds(half, half)], sems.at[1]),
    ]
    for copy in copies:
        copy.start()
    total[...] = jnp.zeros_like(total)
    heavy = weight[...].astype(jnp.float32)
    for copy in copies:
        copy.wait()
    for box in range(rows // BH * (width // BW)):
        down, col = divmod(box, width // BW)
        spot = place(owner[0, box], me, peers) * PS + slot[0, box]
        piece = table[pl.ds(pl.multiple_of(spot * BH, BH), BH), :]
        image[down * BH : (down + 1) * BH, col * BW : (col + 1) * BW] = piece
    for block, (low, high, top, bottom) in enumerate(windows(width)):
        matched = jnp.zeros((rows, WIDE), jnp.float32)
        for member in range(bands.shape[0]):
            blurred = jnp.dot(
                image[:, low:high], bands[member, top:bottom, :], preferred_element_type=jnp.float32
            ).astype(jnp.bfloat16)
            matched = matched + coef[0, member] * jnp.dot(
                bands[member, SIDE : SIDE + rows, :], blurred, preferred_element_type=jnp.float32
            )
        ours = warped[:, block * WIDE : (block + 1) * WIDE].astype(jnp.float32)
        difference = (ours - matched).astype(jnp.bfloat16)
        add_boxes(peers, me, total, difference.astype(jnp.float32) * heavy, owner, slot, block, width)
    store_slots(peers, total, keep, send)


def shards(
    visit_image,
    band_offset,
    shift_frac,
    weights,
    box_owner,
    box_slot,
    basis_index,
    basis_coef,
    basis_width,
):
    peers = lax.axis_size("visit")
    rows, width = visit_image.shape[1:]
    bases = basis_index.shape[1]
    lines = peers * PS * BH
    owner = box_owner.reshape(1, -1)
    me = lax.axis_index("visit").astype(jnp.int32).reshape(1)
    weight = weights.reshape(1, 1)

    named = (owner * PS + box_slot).astype(jnp.float32)
    tag = jnp.concatenate([named, jnp.broadcast_to(weight.astype(jnp.float32), named.shape)], axis=0)
    tags = lax.all_gather(tag, "visit", axis=1, tiled=False).reshape(2 * peers, -1)

    half = jax.ShapeDtypeStruct((lines // 2, BW), jnp.bfloat16)
    warped, keep, send = pl.pallas_call(
        functools.partial(warp_kernel, peers),
        out_shape=[jax.ShapeDtypeStruct((rows, width), jnp.bfloat16), half, half],
        in_specs=[VMEM, SMEM, SMEM, VMEM, SMEM, SMEM, SMEM],
        out_specs=[VMEM] * 3,
        scratch_shapes=[
            pltpu.VMEM((lines, BW), jnp.float32),
            pltpu.VMEM((WIDE + 2 * SIDE, WIDE), jnp.bfloat16),
        ],
        compiler_params=params(),
        name="warp",
    )(visit_image[0], band_offset, shift_frac, weight, owner, box_slot, me)

    bands = pl.pallas_call(
        gauss_kernel,
        out_shape=jax.ShapeDtypeStruct((bases, WIDE + 2 * SIDE, WIDE), jnp.bfloat16),
        in_specs=[SMEM, SMEM],
        out_specs=VMEM,
        compiler_params=params(),
        name="gauss_bands",
    )(basis_index, basis_width)

    terms = scatter_sum(keep, send, peers)
    weight_sum = pl.pallas_call(
        weight_kernel,
        out_shape=jax.ShapeDtypeStruct((PS, BW), jnp.float32),
        in_specs=[VMEM, SMEM],
        out_specs=VMEM,
        compiler_params=params(),
        name="weight_sum",
    )(tags, me)
    template = coadd(weight_sum, terms, jnp.bfloat16)
    near, other = gather_slots(template, peers)

    keep, send = pl.pallas_call(
        functools.partial(match_kernel, peers),
        out_shape=[half, half],
        in_specs=[VMEM, VMEM, ANY, ANY, VMEM, SMEM, SMEM, SMEM, SMEM],
        out_specs=[VMEM] * 2,
        scratch_shapes=[
            pltpu.VMEM((lines, BW), jnp.bfloat16),
            pltpu.VMEM((rows, width), jnp.bfloat16),
            pltpu.VMEM((lines, BW), jnp.float32),
            pltpu.SemaphoreType.DMA((2,)),
        ],
        compiler_params=params(),
        name="match",
    )(warped, bands, near, other, weight, basis_coef, owner, box_slot, me)
    terms = scatter_sum(keep, send, peers)
    difference_coadd = coadd(weight_sum, terms, jnp.float32)
    return (template.reshape(PS, BH, BW), difference_coadd.reshape(PS, BH, BW))


def solution(mesh):
    placed = (
        P(("groups", "visit"), None, None),
        P(("groups", "visit"), None),
        P(("groups", "visit"), None),
        P(("groups", "visit")),
        P(("groups", "visit"), None, None),
        P(("groups", "visit"), None),
        P(("groups", "visit"), None),
        P(("groups", "visit"), None),
        P(),
    )
    return jax.shard_map(
        shards,
        mesh=mesh,
        in_specs=placed,
        out_specs=(P(("groups", "visit"), None, None), P(("groups", "visit"), None, None)),
        check_vma=False,
    )
```

time: 155 us -> 94.6 us (0.61)
  matrix products: 43.2 us -> 0 us
  blocking collectives: 0 us -> 21.8 us
  waiting for transfers between devices: 50.5 us -> 33.2 us
  Pallas kernels: 0 us -> 14.9 us
  other arithmetic: 12.8 us -> 0.86 us
  starting transfers between devices: 27.2 us -> 17.5 us
  between operations: 8.94 us -> 1.43 us
  local copies, waits for them, and re-layouts: 10.6 us -> 4.65 us
    all_to_all x4 -> x0, waiting for transfers between devices: 50.5 us -> none  [the longest x1 22.5 us: shards(): lax.all_to_all(sent_boxes, 'visit', split_axis=0, concat_axis=0, tiled=True)]
    dot_general x10 -> x0, matrix products: 43.2 us -> none  [the longest x6 28.1 us: shards(): jnp.dot(down_band, blurred, preferred_element_type=jnp.float32)]
    ppermute x0 -> x15, waiting for transfers between devices: none -> 33.2 us  [swap(): return lax.ppermute(x, 'visit', [(i, i ^ bit) for i in range(axis_size)])]
    all_to_all x4 -> x0, starting transfers between devices: 27.2 us -> none  [the longest x1 7.39 us: shards(): lax.all_to_all(sent_tags, 'visit', split_axis=0, concat_axis=0, tiled=True)]
    all_gather x0 -> x1, blocking collectives: none -> 21.8 us  [shards(): lax.all_gather(tag, 'visit', axis=1, tiled=False).reshape(2 * peers, -1)]
    ppermute x0 -> x15, starting transfers between devices: none -> 17.5 us  [swap(): return lax.ppermute(x, 'visit', [(i, i ^ bit) for i in range(axis_size)])]
    pallas_call x0 -> x10, Pallas kernels: none -> 14.9 us  [the longest x1 9.03 us: shards(): pl.pallas_call(functools.partial(match_kernel, peers), out_shape=[half, h...]
    reduce_sum x9 -> x0, other arithmetic: 9.35 us -> none  [the longest x1 4.48 us: shards(): jnp.sum(jnp.where(basis_ids == basis_index[0, member], basis_width, 0.0))]
  transfers between devices with their start and end apart: 4 -> 15, of which waited for: 3 -> 11; matrix products, arithmetic and copies ran while one was open for 18% -> 1% of each run, Pallas kernels for 0% -> 1%
where the time goes in v1:
time: 94.6 us; the launch traced here: 94.3 us
  waiting for transfers between devices  33.2 us (35%)
  blocking collectives  21.8 us (23%)
  starting transfers between devices  17.5 us (18%)
  Pallas kernels  14.9 us (16%)
  local copies, waits for them, and re-layouts  4.65 us (5%)
  between operations  1.43 us (2%)
    ppermute x15, waiting for transfers between devices, swap(): return lax.ppermute(x, 'visit', [(i, i ^ bit) for i in range(axis_size)])  33.2 us
    all_gather x1, blocking collectives, shards(): lax.all_gather(tag, 'visit', axis=1, tiled=False).reshape(2 * peers, -1)  21.8 us
    ppermute x15, starting transfers between devices, swap(): return lax.ppermute(x, 'visit', [(i, i ^ bit) for i in range(axis_size)])  17.5 us
    pallas_call x1, Pallas kernels, shards(): pl.pallas_call(functools.partial(match_kernel, peers), out_shape=[half, h...  9.03 us
    unnamed x24, local copies, waits for them, and re-layouts  4.59 us
    pallas_call x1, Pallas kernels, shards(): pl.pallas_call(functools.partial(warp_kernel, peers), out_shape=[jax.Shap...  2.93 us
  transfers between devices with their start and end apart: 15, of which 11 were waited for; matrix products, arithmetic and copies ran while one was open for 1% of the time, Pallas kernels for 1%

profile of v1, /device:TPU:0, one launch (start us, length us, event | category | flops | bytes accessed | tf_op | source)
XLA Modules:
  0.0 94.3 jit_solution(17755913978845170737)
XLA Ops:
  1.3 1.0 %copy-done = bf16[1,256,1024]{2,1,0:T(8,128)(2,1)S(1)} copy-done((bf16[1,256,1024]{2,1,0:T(8,128)(2,1)S(1)}, bf16[1,256,1024]{2,1,0:T(8,128)(2,1)}, u32[]{:S(2)}) %copy-start) | copy-done | bytes 524312
  2.3 0.7 copy-done.1
  3.0 0.7 copy-done.3
  3.6 0.7 copy-done.8
  4.3 0.7 copy-done.9
  5.0 2.9 %warp.1 = (bf16[256,1024]{1,0:T(8,128)(2,1)S(1)}, bf16[2048,128]{1,0:T(8,128)(2,1)S(1)}, bf16[2048,128]{1,0:T(8,128)(2,1)S(1)}) custom-call(bf16[256,1024]{1,0:T(8,128)(2,1)S(1)} %bitcast.12, s32[1,2]{1,0:T(1,128)S(1)} %copy-done.8, f32[1,2]{1,0:T(1,128)S(1)} %copy-done.9, bf16[1,1]{1,0:T(2,128)(2,1)} %bitcast.9.weight, s32[1,128]{1,0:T(1,128)S(1)} %bitcast.13, ...), custom_call_target="tpu_custom_call" | custom-call | tf_op jit(solution)/shard_map/warp/pallas_call | solution.py:275
  7.9 0.5 collective-permute-start
  8.4 1.5 %collective-permute-done.theirs = bf16[2048,128]{1,0:T(8,128)(2,1)S(1)} collective-permute-done((bf16[2048,128]{1,0:T(8,128)(2,1)S(1)}, bf16[2048,128]{1,0:T(8,128)(2,1)S(1)}, u32[]{:S(2)}, u32[]{:S(2)}) %collective-permute-start) | collective-permute-done | bytes 524320 | tf_op jit(solution)/shard_map/ppermute | solution.py:125
  10.1 3.0 %collective-permute-start.1 = (bf16[1024,128]{1,0:T(8,128)(2,1)S(1)}, bf16[1024,128]{1,0:T(8,128)(2,1)S(1)}, u32[]{:S(2)}, u32[]{:S(2)}) collective-permute-start(bf16[1024,128]{1,0:T(8,128)(2,1)S(1)} %get-tuple-element.22), channel_id=1, source_target_pairs={{0,2},{1,3},{2,0},{3,1},{4,6},{5,7},{6,4},{7,5},{8,10},{9,11},{10,... | collective-permute-start | bytes 786440 | tf_op jit(solution)/shard_map/ppermute | solution.py:125
  13.0 6.6 %collective-permute-done.1.theirs = bf16[1024,128]{1,0:T(8,128)(2,1)S(1)} collective-permute-done((bf16[1024,128]{1,0:T(8,128)(2,1)S(1)}, bf16[1024,128]{1,0:T(8,128)(2,1)S(1)}, u32[]{:S(2)}, u32[]{:S(2)}) %collective-permute-start.1) | collective-permute-done | bytes 262176 | tf_op jit(solution)/shard_map/ppermute | solution.py:125
  19.7 3.9 %collective-permute-start.2 = (bf16[256,128]{1,0:T(8,128)(2,1)S(1)}, bf16[256,128]{1,0:T(8,128)(2,1)S(1)}, u32[]{:S(2)}, u32[]{:S(2)}) collective-permute-start(bf16[256,128]{1,0:T(8,128)(2,1)S(1)} %get-tuple-element.24), channel_id=1, source_target_pairs={{0,12},{1,13},{2,14},{3,15},{4,8},{5,9},{6,10},{7,11},{8,4},{9,5},... | collective-permute-start | bytes 196616 | tf_op jit(solution)/shard_map/ppermute | solution.py:125
  23.6 0.6 collective-permute-start.4
  24.2 21.8 %all-gather = f32[2,2048]{1,0:T(2,128)S(1)} all-gather(f32[2,128]{1,0:T(2,128)S(1)} %concatenate.10), channel_id=2, replica_groups=mesh['groups'=2,'visit'=16] {'visit'}, dimensions={1}, use_global_device_ids=true | all-gather | bytes 17408 | tf_op jit(solution)/shard_map/all_gather | solution.py:272
  46.3 0.7 coadd.2
  47.2 4.2 %collective-permute-start.5 = (bf16[256,128]{1,0:T(8,128)(2,1)}, bf16[256,128]{1,0:T(8,128)(2,1)S(1)}, u32[]{:S(2)}, u32[]{:S(2)}) collective-permute-start(bf16[256,128]{1,0:T(8,128)(2,1)} %coadd.2), channel_id=1, source_target_pairs={{0,4},{1,5},{2,6},{3,7},{4,0},{5,1},{6,2},{7,3},{8,12},{9,13},{10,... | collective-permute-start | bytes 196616 | tf_op jit(solution)/shard_map/ppermute | solution.py:125
  51.3 0.9 constant_dynamic-update-slice_fusion.4
  52.2 1.8 %collective-permute-done.7 = bf16[256,128]{1,0:T(8,128)(2,1)S(1)} collective-permute-done((bf16[256,128]{1,0:T(8,128)(2,1)}, bf16[256,128]{1,0:T(8,128)(2,1)S(1)}, u32[]{:S(2)}, u32[]{:S(2)}) %collective-permute-start.7) | collective-permute-done | bytes 65568 | tf_op jit(solution)/shard_map/ppermute | solution.py:125
  54.0 1.2 %collective-permute-done.6 = bf16[256,128]{1,0:T(8,128)(2,1)S(1)} collective-permute-done((bf16[256,128]{1,0:T(8,128)(2,1)}, bf16[256,128]{1,0:T(8,128)(2,1)S(1)}, u32[]{:S(2)}, u32[]{:S(2)}) %collective-permute-start.6) | collective-permute-done | bytes 65568 | tf_op jit(solution)/shard_map/ppermute | solution.py:125
  55.3 0.9 pad_maximum_fusion
  56.3 8.0 %collective-permute-done.8 = bf16[1024,128]{1,0:T(8,128)(2,1)S(1)} collective-permute-done((bf16[1024,128]{1,0:T(8,128)(2,1)S(1)}, bf16[1024,128]{1,0:T(8,128)(2,1)S(1)}, u32[]{:S(2)}, u32[]{:S(2)}) %collective-permute-start.8) | collective-permute-done | bytes 262176 | tf_op jit(solution)/shard_map/ppermute | solution.py:125
  64.4 1.0 %gauss_bands.1.bands = bf16[6,512,256]{2,1,0:T(8,128)(2,1)S(1)} custom-call(s32[1,6]{1,0:T(1,128)S(1)} %copy-done.5, f32[12]{0:T(128)S(1)} %copy-done.6), custom_call_target="tpu_custom_call" | custom-call | tf_op jit(solution)/shard_map/gauss_bands/pallas_call | solution.py:288
  65.4 0.9 collective-permute-done.9.other
  66.3 9.0 %match.1 = (bf16[2048,128]{1,0:T(8,128)(2,1)S(1)}, bf16[2048,128]{1,0:T(8,128)(2,1)S(1)}) custom-call(bf16[256,1024]{1,0:T(8,128)(2,1)S(1)} %get-tuple-element.27.warped, bf16[6,512,256]{2,1,0:T(8,128)(2,1)S(1)} %gauss_bands.1.bands, bf16[2048,128]{1,0:T(8,128)(2,1)S(1)} %constant_dynamic-update-slice_fusion.near, ...), custom_call_target="tpu_custom_call" | custom-call | tf_op jit(solution)/shard_map/match/pallas_call | solution.py:309
  75.5 1.8 %collective-permute-done.10.theirs = bf16[2048,128]{1,0:T(8,128)(2,1)S(1)} collective-permute-done((bf16[2048,128]{1,0:T(8,128)(2,1)S(1)}, bf16[2048,128]{1,0:T(8,128)(2,1)S(1)}, u32[]{:S(2)}, u32[]{:S(2)}) %collective-permute-start.10) | collective-permute-done | bytes 524320 | tf_op jit(solution)/shard_map/ppermute | solution.py:125
  77.4 0.4 collective-permute-start.11
  77.8 8.1 %collective-permute-done.11.theirs = bf16[1024,128]{1,0:T(8,128)(2,1)S(1)} collective-permute-done((bf16[1024,128]{1,0:T(8,128)(2,1)S(1)}, bf16[1024,128]{1,0:T(8,128)(2,1)S(1)}, u32[]{:S(2)}, u32[]{:S(2)}) %collective-permute-start.11) | collective-permute-done | bytes 262176 | tf_op jit(solution)/shard_map/ppermute | solution.py:125
  85.9 1.0 %collective-permute-start.12 = (bf16[256,128]{1,0:T(8,128)(2,1)S(1)}, bf16[256,128]{1,0:T(8,128)(2,1)S(1)}, u32[]{:S(2)}, u32[]{:S(2)}) collective-permute-start(bf16[256,128]{1,0:T(8,128)(2,1)S(1)} %get-tuple-element.33), channel_id=1, source_target_pairs={{0,12},{1,13},{2,14},{3,15},{4,8},{5,9},{6,10},{7,11},{8,4},{9,5},... | collective-permute-start | bytes 196616 | tf_op jit(solution)/shard_map/ppermute | solution.py:125
  86.9 0.3 collective-permute-start.13
  87.1 3.2 %collective-permute-start.14 = (bf16[256,128]{1,0:T(8,128)(2,1)S(1)}, bf16[256,128]{1,0:T(8,128)(2,1)S(1)}, u32[]{:S(2)}, u32[]{:S(2)}) collective-permute-start(bf16[256,128]{1,0:T(8,128)(2,1)S(1)} %get-tuple-element.35), channel_id=1, source_target_pairs={{0,4},{1,5},{2,6},{3,7},{4,0},{5,1},{6,2},{7,3},{8,12},{9,13},{10,... | collective-permute-start | bytes 196616 | tf_op jit(solution)/shard_map/ppermute | solution.py:125
  90.3 2.2 %collective-permute-done.12.refs_1_ = bf16[256,128]{1,0:T(8,128)(2,1)S(1)} collective-permute-done((bf16[256,128]{1,0:T(8,128)(2,1)S(1)}, bf16[256,128]{1,0:T(8,128)(2,1)S(1)}, u32[]{:S(2)}, u32[]{:S(2)}) %collective-permute-start.12) | collective-permute-done | bytes 65568 | tf_op jit(solution)/shard_map/ppermute | solution.py:125
  92.6 1.0 %collective-permute-done.13.refs_2_ = bf16[256,128]{1,0:T(8,128)(2,1)S(1)} collective-permute-done((bf16[256,128]{1,0:T(8,128)(2,1)S(1)}, bf16[256,128]{1,0:T(8,128)(2,1)S(1)}, u32[]{:S(2)}, u32[]{:S(2)}) %collective-permute-start.13) | collective-permute-done | bytes 65568 | tf_op jit(solution)/shard_map/ppermute | solution.py:125
  93.6 0.7 coadd.3
  (38 shorter events, 1.4 us)
Async XLA Ops:
  1.3 1.0 %copy-start = (bf16[1,256,1024]{2,1,0:T(8,128)(2,1)S(1)}, bf16[1,256,1024]{2,1,0:T(8,128)(2,1)}, u32[]{:S(2)}) copy-start(bf16[1,256,1024]{2,1,0:T(8,128)(2,1)} %param.9) | copy-start | bytes 1572868
  2.3 0.7 copy-start.1
  3.0 0.7 copy-start.3
  3.6 0.7 copy-start.8
  4.3 0.7 copy-start.9
  7.9 2.1 %collective-permute-start = (bf16[2048,128]{1,0:T(8,128)(2,1)S(1)}, bf16[2048,128]{1,0:T(8,128)(2,1)S(1)}, u32[]{:S(2)}, u32[]{:S(2)}) collective-permute-start(bf16[2048,128]{1,0:T(8,128)(2,1)S(1)} %get-tuple-element.20), channel_id=1, source_target_pairs={{0,1},{1,0},{2,3},{3,2},{4,5},{5,4},{6,7},{7,6},{8,9},{9,8},{10,11... | collective-permute-start | bytes 1572872 | tf_op jit(solution)/shard_map/ppermute | solution.py:125
  9.9 54.4 %copy-start.5 = (s32[1,6]{1,0:T(1,128)S(1)}, s32[1,6]{1,0:T(1,128)}, u32[]{:S(2)}) copy-start(s32[1,6]{1,0:T(1,128)} %basis_index.1) | copy-start | bytes 76
  9.9 54.4 %copy-start.6 = (f32[12]{0:T(128)S(1)}, f32[12]{0:T(128)}, u32[]{:S(2)}) copy-start(f32[12]{0:T(128)} %basis_width.1) | copy-start | bytes 148
  10.1 9.6 %collective-permute-start.1 = (bf16[1024,128]{1,0:T(8,128)(2,1)S(1)}, bf16[1024,128]{1,0:T(8,128)(2,1)S(1)}, u32[]{:S(2)}, u32[]{:S(2)}) collective-permute-start(bf16[1024,128]{1,0:T(8,128)(2,1)S(1)} %get-tuple-element.22), channel_id=1, source_target_pairs={{0,2},{1,3},{2,0},{3,1},{4,6},{5,7},{6,4},{7,5},{8,10},{9,11},{10,... | collective-permute-start | bytes 786440 | tf_op jit(solution)/shard_map/ppermute | solution.py:125
  19.7 26.6 %collective-permute-start.2 = (bf16[256,128]{1,0:T(8,128)(2,1)S(1)}, bf16[256,128]{1,0:T(8,128)(2,1)S(1)}, u32[]{:S(2)}, u32[]{:S(2)}) collective-permute-start(bf16[256,128]{1,0:T(8,128)(2,1)S(1)} %get-tuple-element.24), channel_id=1, source_target_pairs={{0,12},{1,13},{2,14},{3,15},{4,8},{5,9},{6,10},{7,11},{8,4},{9,5},... | collective-permute-start | bytes 196616 | tf_op jit(solution)/shard_map/ppermute | solution.py:125
  23.6 22.7 %collective-permute-start.3 = (bf16[256,128]{1,0:T(8,128)(2,1)S(1)}, bf16[256,128]{1,0:T(8,128)(2,1)S(1)}, u32[]{:S(2)}, u32[]{:S(2)}) collective-permute-start(bf16[256,128]{1,0:T(8,128)(2,1)S(1)} %get-tuple-element.25), channel_id=1, source_target_pairs={{0,8},{1,9},{2,10},{3,11},{4,12},{5,13},{6,14},{7,15},{8,0},{9,1},... | collective-permute-start | bytes 196616 | tf_op jit(solution)/shard_map/ppermute | solution.py:125
  23.6 22.7 %collective-permute-start.4 = (bf16[256,128]{1,0:T(8,128)(2,1)S(1)}, bf16[256,128]{1,0:T(8,128)(2,1)S(1)}, u32[]{:S(2)}, u32[]{:S(2)}) collective-permute-start(bf16[256,128]{1,0:T(8,128)(2,1)S(1)} %get-tuple-element.26), channel_id=1, source_target_pairs={{0,4},{1,5},{2,6},{3,7},{4,0},{5,1},{6,2},{7,3},{8,12},{9,13},{10,... | collective-permute-start | bytes 196616 | tf_op jit(solution)/shard_map/ppermute | solution.py:125
  47.0 19.3 %copy-start.2 = (s32[1,128]{1,0:T(1,128)S(1)}, s32[1,128]{1,0:T(1,128)}, u32[]{:S(2)}) copy-start(s32[1,128]{1,0:T(1,128)} %slot.3) | copy-start | bytes 1540
  47.0 19.3 %copy-start.4 = (s32[1,128,1]{1,2,0:T(1,128)S(1)}, s32[1,128,1]{1,2,0:T(1,128)}, u32[]{:S(2)}) copy-start(s32[1,128,1]{1,2,0:T(1,128)} %param.13) | copy-start | bytes 1540
  47.0 19.3 %copy-start.7 = (f32[1,6]{1,0:T(1,128)S(1)}, f32[1,6]{1,0:T(1,128)}, u32[]{:S(2)}) copy-start(f32[1,6]{1,0:T(1,128)} %coef.1) | copy-start | bytes 76
  47.0 7.0 %collective-permute-start.7 = (bf16[256,128]{1,0:T(8,128)(2,1)}, bf16[256,128]{1,0:T(8,128)(2,1)S(1)}, u32[]{:S(2)}, u32[]{:S(2)}) collective-permute-start(bf16[256,128]{1,0:T(8,128)(2,1)} %coadd.2), channel_id=1, source_target_pairs={{0,12},{1,13},{2,14},{3,15},{4,8},{5,9},{6,10},{7,11},{8,4},{9,5},... | collective-permute-start | bytes 196616 | tf_op jit(solution)/shard_map/ppermute | solution.py:125
  47.0 8.2 %collective-permute-start.6 = (bf16[256,128]{1,0:T(8,128)(2,1)}, bf16[256,128]{1,0:T(8,128)(2,1)S(1)}, u32[]{:S(2)}, u32[]{:S(2)}) collective-permute-start(bf16[256,128]{1,0:T(8,128)(2,1)} %coadd.2), channel_id=1, source_target_pairs={{0,8},{1,9},{2,10},{3,11},{4,12},{5,13},{6,14},{7,15},{8,0},{9,1},... | collective-permute-start | bytes 196616 | tf_op jit(solution)/shard_map/ppermute | solution.py:125
  47.2 8.1 %collective-permute-start.5 = (bf16[256,128]{1,0:T(8,128)(2,1)}, bf16[256,128]{1,0:T(8,128)(2,1)S(1)}, u32[]{:S(2)}, u32[]{:S(2)}) collective-permute-start(bf16[256,128]{1,0:T(8,128)(2,1)} %coadd.2), channel_id=1, source_target_pairs={{0,4},{1,5},{2,6},{3,7},{4,0},{5,1},{6,2},{7,3},{8,12},{9,13},{10,... | collective-permute-start | bytes 196616 | tf_op jit(solution)/shard_map/ppermute | solution.py:125
  56.1 8.1 %collective-permute-start.8 = (bf16[1024,128]{1,0:T(8,128)(2,1)S(1)}, bf16[1024,128]{1,0:T(8,128)(2,1)S(1)}, u32[]{:S(2)}, u32[]{:S(2)}) collective-permute-start(bf16[1024,128]{1,0:T(8,128)(2,1)S(1)} %pad_maximum_fusion), channel_id=1, source_target_pairs={{0,2},{1,3},{2,0},{3,1},{4,6},{5,7},{6,4},{7,5},{8,10},{9,11},{10,... | collective-permute-start | bytes 786440 | tf_op jit(solution)/shard_map/ppermute | solution.py:125
  64.3 2.0 %collective-permute-start.9 = (bf16[2048,128]{1,0:T(8,128)(2,1)S(1)}, bf16[2048,128]{1,0:T(8,128)(2,1)S(1)}, u32[]{:S(2)}, u32[]{:S(2)}) collective-permute-start(bf16[2048,128]{1,0:T(8,128)(2,1)S(1)} %constant_dynamic-update-slice_fusion.near), channel_id=1, source_target_pairs={{0,1},{1,0},{2,3},{3,2},{4,5},{5,4},{6,7},{7,6},{8,9},{9,8},{10,11... | collective-permute-start | bytes 1572872 | tf_op jit(solution)/shard_map/ppermute | solution.py:125
  75.3 2.0 %collective-permute-start.10 = (bf16[2048,128]{1,0:T(8,128)(2,1)S(1)}, bf16[2048,128]{1,0:T(8,128)(2,1)S(1)}, u32[]{:S(2)}, u32[]{:S(2)}) collective-permute-start(bf16[2048,128]{1,0:T(8,128)(2,1)S(1)} %get-tuple-element.29), channel_id=1, source_target_pairs={{0,1},{1,0},{2,3},{3,2},{4,5},{5,4},{6,7},{7,6},{8,9},{9,8},{10,11... | collective-permute-start | bytes 1572872 | tf_op jit(solution)/shard_map/ppermute | solution.py:125
  77.4 8.4 %collective-permute-start.11 = (bf16[1024,128]{1,0:T(8,128)(2,1)S(1)}, bf16[1024,128]{1,0:T(8,128)(2,1)S(1)}, u32[]{:S(2)}, u32[]{:S(2)}) collective-permute-start(bf16[1024,128]{1,0:T(8,128)(2,1)S(1)} %get-tuple-element.31), channel_id=1, source_target_pairs={{0,2},{1,3},{2,0},{3,1},{4,6},{5,7},{6,4},{7,5},{8,10},{9,11},{10,... | collective-permute-start | bytes 786440 | tf_op jit(solution)/shard_map/ppermute | solution.py:125
  85.9 6.7 %collective-permute-start.12 = (bf16[256,128]{1,0:T(8,128)(2,1)S(1)}, bf16[256,128]{1,0:T(8,128)(2,1)S(1)}, u32[]{:S(2)}, u32[]{:S(2)}) collective-permute-start(bf16[256,128]{1,0:T(8,128)(2,1)S(1)} %get-tuple-element.33), channel_id=1, source_target_pairs={{0,12},{1,13},{2,14},{3,15},{4,8},{5,9},{6,10},{7,11},{8,4},{9,5},... | collective-permute-start | bytes 196616 | tf_op jit(solution)/shard_map/ppermute | solution.py:125
  86.9 6.7 %collective-permute-start.13 = (bf16[256,128]{1,0:T(8,128)(2,1)S(1)}, bf16[256,128]{1,0:T(8,128)(2,1)S(1)}, u32[]{:S(2)}, u32[]{:S(2)}) collective-permute-start(bf16[256,128]{1,0:T(8,128)(2,1)S(1)} %get-tuple-element.34), channel_id=1, source_target_pairs={{0,8},{1,9},{2,10},{3,11},{4,12},{5,13},{6,14},{7,15},{8,0},{9,1},... | collective-permute-start | bytes 196616 | tf_op jit(solution)/shard_map/ppermute | solution.py:125
  87.1 6.5 %collective-permute-start.14 = (bf16[256,128]{1,0:T(8,128)(2,1)S(1)}, bf16[256,128]{1,0:T(8,128)(2,1)S(1)}, u32[]{:S(2)}, u32[]{:S(2)}) collective-permute-start(bf16[256,128]{1,0:T(8,128)(2,1)S(1)} %get-tuple-element.35), channel_id=1, source_target_pairs={{0,4},{1,5},{2,6},{3,7},{4,0},{5,1},{6,2},{7,3},{8,12},{9,13},{10,... | collective-permute-start | bytes 196616 | tf_op jit(solution)/shard_map/ppermute | solution.py:125

commit v2 on v1

v2 whole, which is shorter than its diff:
```python
import functools

import jax
import jax.numpy as jnp
from jax import lax
from jax.experimental import pallas as pl
from jax.experimental.pallas import tpu as pltpu
from jax.sharding import PartitionSpec as P

BH = 16
BW = 128
PS = 16
SIDE = 128
WIDE = 256

band_reach = 8.0

VMEM = pl.BlockSpec(memory_space=pltpu.VMEM)
SMEM = pl.BlockSpec(memory_space=pltpu.SMEM)
HBM = pl.BlockSpec(memory_space=pltpu.HBM)


def params():
    return pltpu.CompilerParams(vmem_limit_bytes=48 * 1024 * 1024)


def tag_rows(peers):
    return PS * pl.cdiv(2 * peers, BW)


def place(owner, me, peers):
    away = jnp.bitwise_xor(owner, me)
    return (away & 1) * (peers // 2) + ((away >> 1) & 1) * (peers // 4) + (away >> 2)


def windows(width):
    found = []
    for first in range(0, width, WIDE):
        low, high = max(first - SIDE, 0), min(first + WIDE + SIDE, width)
        found.append((low, high, low - first + SIDE, high - first + SIDE))
    return found


def lanczos_taps(gap, whole, part):
    shift = whole.astype(jnp.float32) + part
    band = jnp.zeros(gap.shape, jnp.float32)
    for tap in range(-2, 5):
        spot = (whole + tap).astype(jnp.float32)
        x = jnp.full((8, 128), spot - shift, jnp.float32)

        def sinc(v):
            angle = jnp.pi * v
            return jnp.where(v == 0.0, 1.0, jnp.sin(angle) / jnp.where(v == 0.0, 1.0, angle))

        value = jnp.where(jnp.abs(x) < 3.0, sinc(x) * sinc(x / 3.0), 0.0)
        band = jnp.where(gap == spot, value[0:1, 0:1], band)
    return band.astype(jnp.bfloat16)


def warp_kernel(
    peers,
    picture,
    weight,
    me_ref,
    band_offset_in,
    shift_frac_in,
    owner_in,
    slot_in,
    warped,
    keep,
    send,
    total,
    wide_band,
    band_offset,
    shift_frac,
    owner,
    slot,
    sems,
):
    rows, width = warped.shape
    me = me_ref[0]
    copies = [
        pltpu.make_async_copy(source, target, sems.at[i])
        for i, (source, target) in enumerate(
            (
                (band_offset_in, band_offset),
                (shift_frac_in, shift_frac),
                (owner_in, owner),
                (slot_in, slot),
            )
        )
    ]
    for copy in copies:
        copy.start()
    total[...] = jnp.zeros_like(total)
    heavy = weight[...].astype(jnp.float32)
    for copy in copies:
        copy.wait()
    gap = (
        lax.broadcasted_iota(jnp.int32, (WIDE + 2 * SIDE, WIDE), 0)
        - lax.broadcasted_iota(jnp.int32, (WIDE + 2 * SIDE, WIDE), 1)
        - SIDE
    ).astype(jnp.float32)
    wide_band[...] = lanczos_taps(gap, band_offset[0, 1], shift_frac[0, 1])
    gap = (
        lax.broadcasted_iota(jnp.int32, (rows, rows), 1) - lax.broadcasted_iota(jnp.int32, (rows, rows), 0)
    ).astype(jnp.float32)
    row_warp = lanczos_taps(gap, band_offset[0, 0], shift_frac[0, 0])
    chunk = PS * BH + tag_rows(peers)
    lane = lax.broadcasted_iota(jnp.int32, (1, BW), 1)
    mark = jnp.where(lane == me, heavy, 0.0)
    for box in range(owner.shape[1]):
        spot = place(owner[0, box], me, peers) * chunk + PS * BH + slot[0, box]
        total[pl.ds(spot, 1), :] += mark
    passes = [
        jnp.dot(
            picture[:, low:high], wide_band[top:bottom, :], preferred_element_type=jnp.float32
        ).astype(jnp.bfloat16)
        for low, high, top, bottom in windows(width)
    ]
    for block, col_pass in enumerate(passes):
        done = jnp.dot(row_warp, col_pass, preferred_element_type=jnp.float32).astype(jnp.bfloat16)
        warped[:, block * WIDE : (block + 1) * WIDE] = done
        add_boxes(peers, chunk, me, total, done.astype(jnp.float32) * heavy, owner, slot, block, width)
    store_slots(peers, chunk, total, keep, send)


def add_boxes(peers, chunk, me, total, scaled, owner, slot, block, width):
    across = WIDE // BW
    for down in range(scaled.shape[0] // BH):
        for col in range(across):
            box = down * (width // BW) + block * across + col
            spot = place(owner[0, box], me, peers) * chunk + slot[0, box] * BH
            piece = pl.ds(pl.multiple_of(spot, BH), BH)
            total[piece, :] += scaled[down * BH : (down + 1) * BH, col * BW : (col + 1) * BW]


def store_slots(peers, chunk, total, keep, send):
    half = peers // 2 * chunk
    boxes = PS * BH

    @pl.loop(0, peers // 2)
    def _(i):
        for out, base in ((keep, 0), (send, half)):
            start = pl.multiple_of(i * chunk, PS)
            out[pl.ds(start, boxes), :] = total[pl.ds(base + start, boxes), :].astype(jnp.bfloat16)
            if chunk > boxes:
                tags = total[pl.ds(base + start + boxes, PS), :]
                high = tags.astype(jnp.bfloat16)
                low = tags - high.astype(jnp.float32)
                if chunk == boxes + PS:
                    both = high.astype(jnp.float32) + pltpu.roll(low, peers, 1)
                    out[pl.ds(start + boxes, PS), :] = both.astype(jnp.bfloat16)
                else:
                    out[pl.ds(start + boxes, PS), :] = high
                    out[pl.ds(start + boxes + PS, PS), :] = low.astype(jnp.bfloat16)


def add_kernel(parts, ours, theirs, *outs):
    length = ours.shape[0] // parts
    for i, out in enumerate(outs):
        here = pl.ds(i * length, length)
        out[...] = (ours[here, :].astype(jnp.float32) + theirs[here, :].astype(jnp.float32)).astype(jnp.bfloat16)


def add_parts(ours, theirs, parts):
    length = ours.shape[0] // parts
    return pl.pallas_call(
        functools.partial(add_kernel, parts),
        out_shape=[jax.ShapeDtypeStruct((length, BW), jnp.bfloat16)] * parts,
        in_specs=[VMEM, VMEM],
        out_specs=[VMEM] * parts,
        compiler_params=params(),
        name="add_parts",
    )(ours, theirs)


def swap(x, axis_size, bit):
    return lax.ppermute(x, "visit", [(i, i ^ bit) for i in range(axis_size)])


def scatter_sum(keep, send, peers):
    near = swap(send, peers, 1)
    ours, theirs = add_parts(keep, near, 2)
    near = swap(theirs, peers, 2)
    terms = add_parts(ours, near, peers // 4)
    return [terms[0]] + [swap(terms[far], peers, 4 * far) for far in reversed(range(1, peers // 4))]


def join_kernel(*refs):
    *parts, out = refs
    length = parts[0].shape[0]
    for i, part in enumerate(parts):
        out[i * length : (i + 1) * length, :] = part[...]


def join(*parts):
    rows, lanes = parts[0].shape
    return pl.pallas_call(
        join_kernel,
        out_shape=jax.ShapeDtypeStruct((rows * len(parts), lanes), parts[0].dtype),
        in_specs=[VMEM] * len(parts),
        out_specs=VMEM,
        compiler_params=params(),
        name="join",
    )(*parts)


def gather_slots(own, peers):
    line = join(own, *[swap(own, peers, 4 * away) for away in range(1, peers // 4)])
    pair = join(line, swap(line, peers, 2))
    return pair, swap(pair, peers, 1)


def summed_terms(terms, here):
    total = terms[0][here, :].astype(jnp.float32)
    for term in terms[1:]:
        total = total + term[here, :].astype(jnp.float32)
    return total


def template_kernel(*refs):
    *terms, template, weight_sum = refs
    tags = summed_terms(terms, slice(PS * BH, PS * BH + PS))
    for i in range(1, (terms[0].shape[0] - PS * BH) // PS):
        tags = tags + summed_terms(terms, slice(PS * BH + i * PS, PS * BH + (i + 1) * PS))
    weight_sum[...] = jnp.broadcast_to(1.0 + jnp.sum(tags, axis=1, keepdims=True), weight_sum.shape)
    for i in range(PS):
        here = slice(i * BH, (i + 1) * BH)
        template[here, :] = (summed_terms(terms, here) / weight_sum[i : i + 1, :]).astype(template.dtype)


def difference_kernel(weight_sum, *refs):
    *terms, out = refs
    for i in range(PS):
        here = slice(i * BH, (i + 1) * BH)
        out[here, :] = summed_terms(terms, here) / weight_sum[i : i + 1, :]


def gauss_kernel(basis_index, basis_width, bands):
    bases = bands.shape[0]
    tap = lax.broadcasted_iota(jnp.int32, (8, 128), 1).astype(jnp.float32) - band_reach
    gaps = []
    for shift in (SIDE, 0, -SIDE):
        gap = (
            lax.broadcasted_iota(jnp.int32, (SIDE, SIDE), 0) - lax.broadcasted_iota(jnp.int32, (SIDE, SIDE), 1) - shift
        ).astype(jnp.float32)
        gaps.append(gap)
    for member in range(bases):
        blur_width = basis_width[basis_index[0, member]]
        spread = 2.0 * blur_width * blur_width
        total = jnp.sum(jnp.where(tap <= band_reach, jnp.exp(-tap * tap / spread), 0.0), axis=1, keepdims=True)[0:1]
        blocks = []
        for gap in gaps:
            value = jnp.where(jnp.abs(gap) <= band_reach, jnp.exp(-gap * gap / spread), 0.0)
            blocks.append((value / total).astype(jnp.bfloat16))
        above, middle, below = blocks
        nothing = jnp.zeros_like(middle)
        for place_, pieces in enumerate(((above, nothing), (middle, above), (below, middle), (nothing, below))):
            for col, piece in enumerate(pieces):
                bands[member, place_ * SIDE : (place_ + 1) * SIDE, col * SIDE : (col + 1) * SIDE] = piece


def match_kernel(
    peers, warped, bands, near, other, weight, coef, owner, slot, me_ref, keep, send, image, total
):
    rows, width = warped.shape
    me = me_ref[0]
    boxes = PS * BH
    total[...] = jnp.zeros_like(total)
    heavy = weight[...].astype(jnp.float32)
    for box in range(rows // BH * (width // BW)):
        down, col = divmod(box, width // BW)
        spot = place(owner[0, box], me, peers)
        far = spot // (peers // 2)
        here = (spot - far * (peers // 2)) * boxes + slot[0, box] * BH
        piece = pl.ds(pl.multiple_of(here, BH), BH)
        image[down * BH : (down + 1) * BH, col * BW : (col + 1) * BW] = jnp.where(
            far == 0, near[piece, :], other[piece, :]
        )
    for block, (low, high, top, bottom) in enumerate(windows(width)):
        blurred = [
            jnp.dot(image[:, low:high], bands[member, top:bottom, :], preferred_element_type=jnp.float32).astype(
                jnp.bfloat16
            )
            for member in range(bands.shape[0])
        ]
        matched = jnp.zeros((rows, WIDE), jnp.float32)
        for member in range(bands.shape[0]):
            matched = matched + coef[0, member] * jnp.dot(
                bands[member, SIDE : SIDE + rows, :], blurred[member], preferred_element_type=jnp.float32
            )
        ours = warped[:, block * WIDE : (block + 1) * WIDE].astype(jnp.float32)
        difference = (ours - matched).astype(jnp.bfloat16)
        add_boxes(peers, boxes, me, total, difference.astype(jnp.float32) * heavy, owner, slot, block, width)
    store_slots(peers, boxes, total, keep, send)


def shards(
    visit_image,
    band_offset,
    shift_frac,
    weights,
    box_owner,
    box_slot,
    basis_index,
    basis_coef,
    basis_width,
):
    peers = lax.axis_size("visit")
    rows, width = visit_image.shape[1:]
    bases = basis_index.shape[1]
    owner = box_owner.reshape(1, -1)
    me = lax.axis_index("visit").astype(jnp.int32).reshape(1)
    weight = weights.reshape(1, 1)
    boxes = PS * BH
    chunk = boxes + tag_rows(peers)

    half = jax.ShapeDtypeStruct((peers // 2 * chunk, BW), jnp.bfloat16)
    warped, keep, send = pl.pallas_call(
        functools.partial(warp_kernel, peers),
        out_shape=[jax.ShapeDtypeStruct((rows, width), jnp.bfloat16), half, half],
        in_specs=[VMEM, VMEM, SMEM, HBM, HBM, HBM, HBM],
        out_specs=[VMEM] * 3,
        scratch_shapes=[
            pltpu.VMEM((peers * chunk, BW), jnp.float32),
            pltpu.VMEM((WIDE + 2 * SIDE, WIDE), jnp.bfloat16),
            pltpu.SMEM(band_offset.shape, jnp.int32),
            pltpu.SMEM(shift_frac.shape, jnp.float32),
            pltpu.SMEM(owner.shape, jnp.int32),
            pltpu.SMEM(box_slot.shape, jnp.int32),
            pltpu.SemaphoreType.DMA((4,)),
        ],
        compiler_params=params(),
        name="warp",
    )(visit_image[0], weight, me, band_offset, shift_frac, owner, box_slot)

    bands = pl.pallas_call(
        gauss_kernel,
        out_shape=jax.ShapeDtypeStruct((bases, WIDE + 2 * SIDE, WIDE), jnp.bfloat16),
        in_specs=[SMEM, SMEM],
        out_specs=VMEM,
        compiler_params=params(),
        name="gauss_bands",
    )(basis_index, basis_width)

    terms = scatter_sum(keep, send, peers)
    template, weight_sum = pl.pallas_call(
        template_kernel,
        out_shape=[
            jax.ShapeDtypeStruct((boxes, BW), jnp.bfloat16),
            jax.ShapeDtypeStruct((PS, BW), jnp.float32),
        ],
        in_specs=[VMEM] * len(terms),
        out_specs=[VMEM] * 2,
        compiler_params=params(),
        name="template",
    )(*terms)
    near, other = gather_slots(template, peers)

    half = jax.ShapeDtypeStruct((peers // 2 * boxes, BW), jnp.bfloat16)
    keep, send = pl.pallas_call(
        functools.partial(match_kernel, peers),
        out_shape=[half, half],
        in_specs=[VMEM] * 5 + [SMEM] * 4,
        out_specs=[VMEM] * 2,
        scratch_shapes=[
            pltpu.VMEM((rows, width), jnp.bfloat16),
            pltpu.VMEM((peers * boxes, BW), jnp.float32),
        ],
        compiler_params=params(),
        name="match",
    )(warped, bands, near, other, weight, basis_coef, owner, box_slot, me)
    terms = scatter_sum(keep, send, peers)
    difference_coadd = pl.pallas_call(
        difference_kernel,
        out_shape=jax.ShapeDtypeStruct((boxes, BW), jnp.float32),
        in_specs=[VMEM] * (1 + len(terms)),
        out_specs=VMEM,
        compiler_params=params(),
        name="difference_coadd",
    )(weight_sum, *terms)
    return (template.reshape(PS, BH, BW), difference_coadd.reshape(PS, BH, BW))


def solution(mesh):
    placed = (
        P(("groups", "visit"), None, None),
        P(("groups", "visit"), None),
        P(("groups", "visit"), None),
        P(("groups", "visit")),
        P(("groups", "visit"), None, None),
        P(("groups", "visit"), None),
        P(("groups", "visit"), None),
        P(("groups", "visit"), None),
        P(),
    )
    return jax.shard_map(
        shards,
        mesh=mesh,
        in_specs=placed,
        out_specs=(P(("groups", "visit"), None, None), P(("groups", "visit"), None, None)),
        check_vma=False,
    )
```

time: 94.6 us -> 73.1 us (0.77)
  blocking collectives: 21.8 us -> 0 us
  Pallas kernels: 14.9 us -> 10.9 us
  starting transfers between devices: 17.5 us -> 20.4 us
  waiting for transfers between devices: 33.2 us -> 35.7 us
    all_gather x1 -> x0, blocking collectives: 21.8 us -> none  [shards(): lax.all_gather(tag, 'visit', axis=1, tiled=False).reshape(2 * peers, -1)]
    pallas_call x1, Pallas kernels: 9.03 us -> 4.58 us  [shards(): pl.pallas_call(functools.partial(match_kernel, peers), out_shape=[half, h...]
    ppermute x15, starting transfers between devices: 17.5 us -> 20.4 us  [swap(): return lax.ppermute(x, 'visit', [(i, i ^ bit) for i in range(axis_size)])]
    ppermute x15, waiting for transfers between devices: 33.2 us -> 35.7 us  [swap(): return lax.ppermute(x, 'visit', [(i, i ^ bit) for i in range(axis_size)])]
    unnamed x24 -> x22, local copies, waits for them, and re-layouts: 4.59 us -> 4.51 us
  transfers between devices with their start and end apart: 15 -> 15, of which waited for: 11 -> 13; matrix products, arithmetic and copies ran while one was open for 1% -> 0% of each run, Pallas kernels for 1% -> 1%
where the time goes in v2:
time: 73.1 us; the launch traced here: 72.9 us
  waiting for transfers between devices  35.7 us (49%)
  starting transfers between devices  20.4 us (28%)
  Pallas kernels  10.9 us (15%)
  local copies, waits for them, and re-layouts  4.51 us (6%)
  between operations  1.39 us (2%)
    ppermute x15, waiting for transfers between devices, swap(): return lax.ppermute(x, 'visit', [(i, i ^ bit) for i in range(axis_size)])  35.7 us
    ppermute x15, starting transfers between devices, swap(): return lax.ppermute(x, 'visit', [(i, i ^ bit) for i in range(axis_size)])  20.4 us
    pallas_call x1, Pallas kernels, shards(): pl.pallas_call(functools.partial(match_kernel, peers), out_shape=[half, h...  4.58 us
    unnamed x22, local copies, waits for them, and re-layouts  4.51 us
    pallas_call x1, Pallas kernels, shards(): pl.pallas_call(functools.partial(warp_kernel, peers), out_shape=[jax.Shap...  3.5 us
  transfers between devices with their start and end apart: 15, of which 13 were waited for; matrix products, arithmetic and copies ran while one was open for 0% of the time, Pallas kernels for 1%

profile of v2, /device:TPU:0, one launch (start us, length us, event | category | flops | bytes accessed | tf_op | source)
XLA Modules:
  0.0 72.9 jit_solution(8101828316628020115)
XLA Ops:
  1.3 1.0 %copy-done = bf16[1,256,1024]{2,1,0:T(8,128)(2,1)S(1)} copy-done((bf16[1,256,1024]{2,1,0:T(8,128)(2,1)S(1)}, bf16[1,256,1024]{2,1,0:T(8,128)(2,1)}, u32[]{:S(2)}) %copy-start) | copy-done | bytes 524312
  2.3 0.7 copy-done.2
  3.0 0.7 copy-done.4
  3.6 0.7 copy-done.9
  4.3 0.7 copy-done.10
  5.0 3.5 %warp.1 = (bf16[256,1024]{1,0:T(8,128)(2,1)S(1)}, bf16[2176,128]{1,0:T(8,128)(2,1)S(1)}, bf16[2176,128]{1,0:T(8,128)(2,1)S(1)}) custom-call(bf16[256,1024]{1,0:T(8,128)(2,1)S(1)} %bitcast.8, bf16[1,1]{1,0:T(2,128)(2,1)} %bitcast.6.weight, s32[1]{0:T(128)} %bitcast.2.me_ref, s32[1,2]{1,0:T(1,128)S(1)} %copy-done.9, f32[1,2]{1,0:T(1,128)S(1)} %copy-done.10, ...), custom_call_target="tpu_custom_call" | custom-call | tf_op jit(solution)/shard_map/warp/pallas_call | solution.py:320
  9.0 1.6 %collective-permute-done.theirs = bf16[2176,128]{1,0:T(8,128)(2,1)S(1)} collective-permute-done((bf16[2176,128]{1,0:T(8,128)(2,1)S(1)}, bf16[2176,128]{1,0:T(8,128)(2,1)S(1)}, u32[]{:S(2)}, u32[]{:S(2)}) %collective-permute-start) | collective-permute-done | bytes 557088 | tf_op jit(solution)/shard_map/ppermute | solution.py:179
  10.7 3.0 %collective-permute-start.1 = (bf16[1088,128]{1,0:T(8,128)(2,1)S(1)}, bf16[1088,128]{1,0:T(8,128)(2,1)S(1)}, u32[]{:S(2)}, u32[]{:S(2)}) collective-permute-start(bf16[1088,128]{1,0:T(8,128)(2,1)S(1)} %get-tuple-element.24), channel_id=1, source_target_pairs={{0,2},{1,3},{2,0},{3,1},{4,6},{5,7},{6,4},{7,5},{8,10},{9,11},{10,... | collective-permute-start | bytes 835592 | tf_op jit(solution)/shard_map/ppermute | solution.py:179
  13.7 7.0 %collective-permute-done.1.theirs = bf16[1088,128]{1,0:T(8,128)(2,1)S(1)} collective-permute-done((bf16[1088,128]{1,0:T(8,128)(2,1)S(1)}, bf16[1088,128]{1,0:T(8,128)(2,1)S(1)}, u32[]{:S(2)}, u32[]{:S(2)}) %collective-permute-start.1) | collective-permute-done | bytes 278560 | tf_op jit(solution)/shard_map/ppermute | solution.py:179
  20.7 3.9 %collective-permute-start.2 = (bf16[272,128]{1,0:T(8,128)(2,1)S(1)}, bf16[272,128]{1,0:T(8,128)(2,1)S(1)}, u32[]{:S(2)}, u32[]{:S(2)}) collective-permute-start(bf16[272,128]{1,0:T(8,128)(2,1)S(1)} %get-tuple-element.26), channel_id=1, source_target_pairs={{0,12},{1,13},{2,14},{3,15},{4,8},{5,9},{6,10},{7,11},{8,4},{9,5},... | collective-permute-start | bytes 208904 | tf_op jit(solution)/shard_map/ppermute | solution.py:179
  24.6 0.6 collective-permute-start.4
  25.2 2.5 %collective-permute-done.2.refs_1_ = bf16[272,128]{1,0:T(8,128)(2,1)S(1)} collective-permute-done((bf16[272,128]{1,0:T(8,128)(2,1)S(1)}, bf16[272,128]{1,0:T(8,128)(2,1)S(1)}, u32[]{:S(2)}, u32[]{:S(2)}) %collective-permute-start.2) | collective-permute-done | bytes 69664 | tf_op jit(solution)/shard_map/ppermute | solution.py:179
  27.7 2.4 %collective-permute-done.3.refs_2_ = bf16[272,128]{1,0:T(8,128)(2,1)S(1)} collective-permute-done((bf16[272,128]{1,0:T(8,128)(2,1)S(1)}, bf16[272,128]{1,0:T(8,128)(2,1)S(1)}, u32[]{:S(2)}, u32[]{:S(2)}) %collective-permute-start.3) | collective-permute-done | bytes 69664 | tf_op jit(solution)/shard_map/ppermute | solution.py:179
  30.1 0.7 %template.1 = (bf16[256,128]{1,0:T(8,128)(2,1)}, f32[16,128]{1,0:T(8,128)S(1)}) custom-call(bf16[272,128]{1,0:T(8,128)(2,1)S(1)} %get-tuple-element.25.refs_0_, bf16[272,128]{1,0:T(8,128)(2,1)S(1)} %collective-permute-done.2.refs_1_, bf16[272,128]{1,0:T(8,128)(2,1)S(1)} %collective-permute-done.3.refs_2_, bf16[272,128]{1,0:T(8,128)(2,1)S(1)} %collective-permute-done.4.refs_3_), custom_call_target="tpu_custom_call" | custom-call | tf_op jit(solution)/shard_map/template/pallas_call | solution.py:348
  30.9 2.5 %collective-permute-start.7 = (bf16[256,128]{1,0:T(8,128)(2,1)}, bf16[256,128]{1,0:T(8,128)(2,1)S(1)}, u32[]{:S(2)}, u32[]{:S(2)}) collective-permute-start(bf16[256,128]{1,0:T(8,128)(2,1)} %get-tuple-element.29.refs_0_), channel_id=1, source_target_pairs={{0,12},{1,13},{2,14},{3,15},{4,8},{5,9},{6,10},{7,11},{8,4},{9,5},... | collective-permute-start | bytes 196616 | tf_op jit(solution)/shard_map/ppermute | solution.py:179
  33.4 1.8 %collective-permute-start.5 = (bf16[256,128]{1,0:T(8,128)(2,1)}, bf16[256,128]{1,0:T(8,128)(2,1)S(1)}, u32[]{:S(2)}, u32[]{:S(2)}) collective-permute-start(bf16[256,128]{1,0:T(8,128)(2,1)} %get-tuple-element.29.refs_0_), channel_id=1, source_target_pairs={{0,4},{1,5},{2,6},{3,7},{4,0},{5,1},{6,2},{7,3},{8,12},{9,13},{10,... | collective-permute-start | bytes 196616 | tf_op jit(solution)/shard_map/ppermute | solution.py:179
  35.3 2.4 %collective-permute-done.7.refs_3_ = bf16[256,128]{1,0:T(8,128)(2,1)S(1)} collective-permute-done((bf16[256,128]{1,0:T(8,128)(2,1)}, bf16[256,128]{1,0:T(8,128)(2,1)S(1)}, u32[]{:S(2)}, u32[]{:S(2)}) %collective-permute-start.7) | collective-permute-done | bytes 65568 | tf_op jit(solution)/shard_map/ppermute | solution.py:179
  37.7 1.3 %collective-permute-done.6.refs_2_ = bf16[256,128]{1,0:T(8,128)(2,1)S(1)} collective-permute-done((bf16[256,128]{1,0:T(8,128)(2,1)}, bf16[256,128]{1,0:T(8,128)(2,1)S(1)}, u32[]{:S(2)}, u32[]{:S(2)}) %collective-permute-start.6) | collective-permute-done | bytes 65568 | tf_op jit(solution)/shard_map/ppermute | solution.py:179
  39.0 0.8 %copy-done.1 = bf16[256,128]{1,0:T(8,128)(2,1)S(1)} copy-done((bf16[256,128]{1,0:T(8,128)(2,1)S(1)}, bf16[256,128]{1,0:T(8,128)(2,1)}, u32[]{:S(2)}) %copy-start.1) | copy-done | bytes 65560
  39.9 1.6 %collective-permute-start.8 = (bf16[1024,128]{1,0:T(8,128)(2,1)S(1)}, bf16[1024,128]{1,0:T(8,128)(2,1)S(1)}, u32[]{:S(2)}, u32[]{:S(2)}) collective-permute-start(bf16[1024,128]{1,0:T(8,128)(2,1)S(1)} %join.2.refs_0_), channel_id=1, source_target_pairs={{0,2},{1,3},{2,0},{3,1},{4,6},{5,7},{6,4},{7,5},{8,10},{9,11},{10,... | collective-permute-start | bytes 786440 | tf_op jit(solution)/shard_map/ppermute | solution.py:179
  41.5 4.8 %collective-permute-done.8.refs_1_ = bf16[1024,128]{1,0:T(8,128)(2,1)S(1)} collective-permute-done((bf16[1024,128]{1,0:T(8,128)(2,1)S(1)}, bf16[1024,128]{1,0:T(8,128)(2,1)S(1)}, u32[]{:S(2)}, u32[]{:S(2)}) %collective-permute-start.8) | collective-permute-done | bytes 262176 | tf_op jit(solution)/shard_map/ppermute | solution.py:179
  46.4 1.0 %gauss_bands.1.bands = bf16[6,512,256]{2,1,0:T(8,128)(2,1)S(1)} custom-call(s32[1,6]{1,0:T(1,128)S(1)} %copy-done.6, f32[12]{0:T(128)S(1)} %copy-done.7), custom_call_target="tpu_custom_call" | custom-call | tf_op jit(solution)/shard_map/gauss_bands/pallas_call | solution.py:338
  47.4 0.9 %collective-permute-done.9.other = bf16[2048,128]{1,0:T(8,128)(2,1)S(1)} collective-permute-done((bf16[2048,128]{1,0:T(8,128)(2,1)S(1)}, bf16[2048,128]{1,0:T(8,128)(2,1)S(1)}, u32[]{:S(2)}, u32[]{:S(2)}) %collective-permute-start.9) | collective-permute-done | bytes 524320 | tf_op jit(solution)/shard_map/ppermute | solution.py:179
  48.3 4.6 %match.1 = (bf16[2048,128]{1,0:T(8,128)(2,1)S(1)}, bf16[2048,128]{1,0:T(8,128)(2,1)S(1)}) custom-call(bf16[256,1024]{1,0:T(8,128)(2,1)S(1)} %get-tuple-element.31.warped, bf16[6,512,256]{2,1,0:T(8,128)(2,1)S(1)} %gauss_bands.1.bands, bf16[2048,128]{1,0:T(8,128)(2,1)S(1)} %join.3.near, bf16[2048,128]{1,0:T(8,128)(2,1)S(1)} %collective-permute-done.9.other, ...), custom_call_target="tpu_custom_call" | custom-call | tf_op jit(solution)/shard_map/match/pallas_call | solution.py:362
  53.1 1.8 %collective-permute-done.10.theirs = bf16[2048,128]{1,0:T(8,128)(2,1)S(1)} collective-permute-done((bf16[2048,128]{1,0:T(8,128)(2,1)S(1)}, bf16[2048,128]{1,0:T(8,128)(2,1)S(1)}, u32[]{:S(2)}, u32[]{:S(2)}) %collective-permute-start.10) | collective-permute-done | bytes 524320 | tf_op jit(solution)/shard_map/ppermute | solution.py:179
  55.0 1.6 %collective-permute-start.11 = (bf16[1024,128]{1,0:T(8,128)(2,1)S(1)}, bf16[1024,128]{1,0:T(8,128)(2,1)S(1)}, u32[]{:S(2)}, u32[]{:S(2)}) collective-permute-start(bf16[1024,128]{1,0:T(8,128)(2,1)S(1)} %get-tuple-element.35), channel_id=1, source_target_pairs={{0,2},{1,3},{2,0},{3,1},{4,6},{5,7},{6,4},{7,5},{8,10},{9,11},{10,... | collective-permute-start | bytes 786440 | tf_op jit(solution)/shard_map/ppermute | solution.py:179
  56.7 6.8 %collective-permute-done.11.theirs = bf16[1024,128]{1,0:T(8,128)(2,1)S(1)} collective-permute-done((bf16[1024,128]{1,0:T(8,128)(2,1)S(1)}, bf16[1024,128]{1,0:T(8,128)(2,1)S(1)}, u32[]{:S(2)}, u32[]{:S(2)}) %collective-permute-start.11) | collective-permute-done | bytes 262176 | tf_op jit(solution)/shard_map/ppermute | solution.py:179
  63.5 2.3 %collective-permute-start.12 = (bf16[256,128]{1,0:T(8,128)(2,1)S(1)}, bf16[256,128]{1,0:T(8,128)(2,1)S(1)}, u32[]{:S(2)}, u32[]{:S(2)}) collective-permute-start(bf16[256,128]{1,0:T(8,128)(2,1)S(1)} %get-tuple-element.37), channel_id=1, source_target_pairs={{0,12},{1,13},{2,14},{3,15},{4,8},{5,9},{6,10},{7,11},{8,4},{9,5},... | collective-permute-start | bytes 196616 | tf_op jit(solution)/shard_map/ppermute | solution.py:179
  65.8 2.1 %collective-permute-start.14 = (bf16[256,128]{1,0:T(8,128)(2,1)S(1)}, bf16[256,128]{1,0:T(8,128)(2,1)S(1)}, u32[]{:S(2)}, u32[]{:S(2)}) collective-permute-start(bf16[256,128]{1,0:T(8,128)(2,1)S(1)} %get-tuple-element.39), channel_id=1, source_target_pairs={{0,4},{1,5},{2,6},{3,7},{4,0},{5,1},{6,2},{7,3},{8,12},{9,13},{10,... | collective-permute-start | bytes 196616 | tf_op jit(solution)/shard_map/ppermute | solution.py:179
  68.0 1.8 %collective-permute-done.12.refs_1_ = bf16[256,128]{1,0:T(8,128)(2,1)S(1)} collective-permute-done((bf16[256,128]{1,0:T(8,128)(2,1)S(1)}, bf16[256,128]{1,0:T(8,128)(2,1)S(1)}, u32[]{:S(2)}, u32[]{:S(2)}) %collective-permute-start.12) | collective-permute-done | bytes 65568 | tf_op jit(solution)/shard_map/ppermute | solution.py:179
  69.8 2.4 %collective-permute-done.13.refs_2_ = bf16[256,128]{1,0:T(8,128)(2,1)S(1)} collective-permute-done((bf16[256,128]{1,0:T(8,128)(2,1)S(1)}, bf16[256,128]{1,0:T(8,128)(2,1)S(1)}, u32[]{:S(2)}, u32[]{:S(2)}) %collective-permute-start.13) | collective-permute-done | bytes 65568 | tf_op jit(solution)/shard_map/ppermute | solution.py:179
  72.2 0.7 difference_coadd.1
  (31 shorter events, 1.3 us)
Async XLA Ops:
  1.3 1.0 %copy-start = (bf16[1,256,1024]{2,1,0:T(8,128)(2,1)S(1)}, bf16[1,256,1024]{2,1,0:T(8,128)(2,1)}, u32[]{:S(2)}) copy-start(bf16[1,256,1024]{2,1,0:T(8,128)(2,1)} %param.9) | copy-start | bytes 1572868
  2.3 0.7 copy-start.2
  3.0 0.7 copy-start.4
  3.6 0.7 copy-start.9
  4.3 0.7 copy-start.10
  8.5 2.1 %collective-permute-start = (bf16[2176,128]{1,0:T(8,128)(2,1)S(1)}, bf16[2176,128]{1,0:T(8,128)(2,1)S(1)}, u32[]{:S(2)}, u32[]{:S(2)}) collective-permute-start(bf16[2176,128]{1,0:T(8,128)(2,1)S(1)} %get-tuple-element.22), channel_id=1, source_target_pairs={{0,1},{1,0},{2,3},{3,2},{4,5},{5,4},{6,7},{7,6},{8,9},{9,8},{10,11... | collective-permute-start | bytes 1671176 | tf_op jit(solution)/shard_map/ppermute | solution.py:179
  10.6 35.9 %copy-start.6 = (s32[1,6]{1,0:T(1,128)S(1)}, s32[1,6]{1,0:T(1,128)}, u32[]{:S(2)}) copy-start(s32[1,6]{1,0:T(1,128)} %basis_index.1) | copy-start | bytes 76
  10.6 35.9 %copy-start.7 = (f32[12]{0:T(128)S(1)}, f32[12]{0:T(128)}, u32[]{:S(2)}) copy-start(f32[12]{0:T(128)} %basis_width.1) | copy-start | bytes 148
  10.7 9.9 %collective-permute-start.1 = (bf16[1088,128]{1,0:T(8,128)(2,1)S(1)}, bf16[1088,128]{1,0:T(8,128)(2,1)S(1)}, u32[]{:S(2)}, u32[]{:S(2)}) collective-permute-start(bf16[1088,128]{1,0:T(8,128)(2,1)S(1)} %get-tuple-element.24), channel_id=1, source_target_pairs={{0,2},{1,3},{2,0},{3,1},{4,6},{5,7},{6,4},{7,5},{8,10},{9,11},{10,... | collective-permute-start | bytes 835592 | tf_op jit(solution)/shard_map/ppermute | solution.py:179
  20.7 7.0 %collective-permute-start.2 = (bf16[272,128]{1,0:T(8,128)(2,1)S(1)}, bf16[272,128]{1,0:T(8,128)(2,1)S(1)}, u32[]{:S(2)}, u32[]{:S(2)}) collective-permute-start(bf16[272,128]{1,0:T(8,128)(2,1)S(1)} %get-tuple-element.26), channel_id=1, source_target_pairs={{0,12},{1,13},{2,14},{3,15},{4,8},{5,9},{6,10},{7,11},{8,4},{9,5},... | collective-permute-start | bytes 208904 | tf_op jit(solution)/shard_map/ppermute | solution.py:179
  24.6 5.5 %collective-permute-start.3 = (bf16[272,128]{1,0:T(8,128)(2,1)S(1)}, bf16[272,128]{1,0:T(8,128)(2,1)S(1)}, u32[]{:S(2)}, u32[]{:S(2)}) collective-permute-start(bf16[272,128]{1,0:T(8,128)(2,1)S(1)} %get-tuple-element.27), channel_id=1, source_target_pairs={{0,8},{1,9},{2,10},{3,11},{4,12},{5,13},{6,14},{7,15},{8,0},{9,1},... | collective-permute-start | bytes 208904 | tf_op jit(solution)/shard_map/ppermute | solution.py:179
  24.6 5.6 %collective-permute-start.4 = (bf16[272,128]{1,0:T(8,128)(2,1)S(1)}, bf16[272,128]{1,0:T(8,128)(2,1)S(1)}, u32[]{:S(2)}, u32[]{:S(2)}) collective-permute-start(bf16[272,128]{1,0:T(8,128)(2,1)S(1)} %get-tuple-element.28), channel_id=1, source_target_pairs={{0,4},{1,5},{2,6},{3,7},{4,0},{5,1},{6,2},{7,3},{8,12},{9,13},{10,... | collective-permute-start | bytes 208904 | tf_op jit(solution)/shard_map/ppermute | solution.py:179
  30.9 17.4 %copy-start.3 = (s32[1,128,1]{1,2,0:T(1,128)S(1)}, s32[1,128,1]{1,2,0:T(1,128)}, u32[]{:S(2)}) copy-start(s32[1,128,1]{1,2,0:T(1,128)} %param.13) | copy-start | bytes 1540
  30.9 17.4 %copy-start.5 = (s32[1,128]{1,0:T(1,128)S(1)}, s32[1,128]{1,0:T(1,128)}, u32[]{:S(2)}) copy-start(s32[1,128]{1,0:T(1,128)} %slot.1) | copy-start | bytes 1540
  30.9 17.4 %copy-start.8 = (f32[1,6]{1,0:T(1,128)S(1)}, f32[1,6]{1,0:T(1,128)}, u32[]{:S(2)}) copy-start(f32[1,6]{1,0:T(1,128)} %coef.1) | copy-start | bytes 76
  30.9 6.8 %collective-permute-start.7 = (bf16[256,128]{1,0:T(8,128)(2,1)}, bf16[256,128]{1,0:T(8,128)(2,1)S(1)}, u32[]{:S(2)}, u32[]{:S(2)}) collective-permute-start(bf16[256,128]{1,0:T(8,128)(2,1)} %get-tuple-element.29.refs_0_), channel_id=1, source_target_pairs={{0,12},{1,13},{2,14},{3,15},{4,8},{5,9},{6,10},{7,11},{8,4},{9,5},... | collective-permute-start | bytes 196616 | tf_op jit(solution)/shard_map/ppermute | solution.py:179
  33.4 5.6 %collective-permute-start.6 = (bf16[256,128]{1,0:T(8,128)(2,1)}, bf16[256,128]{1,0:T(8,128)(2,1)S(1)}, u32[]{:S(2)}, u32[]{:S(2)}) collective-permute-start(bf16[256,128]{1,0:T(8,128)(2,1)} %get-tuple-element.29.refs_0_), channel_id=1, source_target_pairs={{0,8},{1,9},{2,10},{3,11},{4,12},{5,13},{6,14},{7,15},{8,0},{9,1},... | collective-permute-start | bytes 196616 | tf_op jit(solution)/shard_map/ppermute | solution.py:179
  33.4 5.6 %collective-permute-start.5 = (bf16[256,128]{1,0:T(8,128)(2,1)}, bf16[256,128]{1,0:T(8,128)(2,1)S(1)}, u32[]{:S(2)}, u32[]{:S(2)}) collective-permute-start(bf16[256,128]{1,0:T(8,128)(2,1)} %get-tuple-element.29.refs_0_), channel_id=1, source_target_pairs={{0,4},{1,5},{2,6},{3,7},{4,0},{5,1},{6,2},{7,3},{8,12},{9,13},{10,... | collective-permute-start | bytes 196616 | tf_op jit(solution)/shard_map/ppermute | solution.py:179
  39.0 0.8 %copy-start.1 = (bf16[256,128]{1,0:T(8,128)(2,1)S(1)}, bf16[256,128]{1,0:T(8,128)(2,1)}, u32[]{:S(2)}) copy-start(bf16[256,128]{1,0:T(8,128)(2,1)} %get-tuple-element.29.refs_0_) | copy-start | bytes 196612
  39.9 6.4 %collective-permute-start.8 = (bf16[1024,128]{1,0:T(8,128)(2,1)S(1)}, bf16[1024,128]{1,0:T(8,128)(2,1)S(1)}, u32[]{:S(2)}, u32[]{:S(2)}) collective-permute-start(bf16[1024,128]{1,0:T(8,128)(2,1)S(1)} %join.2.refs_0_), channel_id=1, source_target_pairs={{0,2},{1,3},{2,0},{3,1},{4,6},{5,7},{6,4},{7,5},{8,10},{9,11},{10,... | collective-permute-start | bytes 786440 | tf_op jit(solution)/shard_map/ppermute | solution.py:179
  46.3 2.0 %collective-permute-start.9 = (bf16[2048,128]{1,0:T(8,128)(2,1)S(1)}, bf16[2048,128]{1,0:T(8,128)(2,1)S(1)}, u32[]{:S(2)}, u32[]{:S(2)}) collective-permute-start(bf16[2048,128]{1,0:T(8,128)(2,1)S(1)} %join.3.near), channel_id=1, source_target_pairs={{0,1},{1,0},{2,3},{3,2},{4,5},{5,4},{6,7},{7,6},{8,9},{9,8},{10,11... | collective-permute-start | bytes 1572872 | tf_op jit(solution)/shard_map/ppermute | solution.py:179
  52.9 2.0 %collective-permute-start.10 = (bf16[2048,128]{1,0:T(8,128)(2,1)S(1)}, bf16[2048,128]{1,0:T(8,128)(2,1)S(1)}, u32[]{:S(2)}, u32[]{:S(2)}) collective-permute-start(bf16[2048,128]{1,0:T(8,128)(2,1)S(1)} %get-tuple-element.33), channel_id=1, source_target_pairs={{0,1},{1,0},{2,3},{3,2},{4,5},{5,4},{6,7},{7,6},{8,9},{9,8},{10,11... | collective-permute-start | bytes 1572872 | tf_op jit(solution)/shard_map/ppermute | solution.py:179
  55.0 8.4 %collective-permute-start.11 = (bf16[1024,128]{1,0:T(8,128)(2,1)S(1)}, bf16[1024,128]{1,0:T(8,128)(2,1)S(1)}, u32[]{:S(2)}, u32[]{:S(2)}) collective-permute-start(bf16[1024,128]{1,0:T(8,128)(2,1)S(1)} %get-tuple-element.35), channel_id=1, source_target_pairs={{0,2},{1,3},{2,0},{3,1},{4,6},{5,7},{6,4},{7,5},{8,10},{9,11},{10,... | collective-permute-start | bytes 786440 | tf_op jit(solution)/shard_map/ppermute | solution.py:179
  63.5 6.3 %collective-permute-start.12 = (bf16[256,128]{1,0:T(8,128)(2,1)S(1)}, bf16[256,128]{1,0:T(8,128)(2,1)S(1)}, u32[]{:S(2)}, u32[]{:S(2)}) collective-permute-start(bf16[256,128]{1,0:T(8,128)(2,1)S(1)} %get-tuple-element.37), channel_id=1, source_target_pairs={{0,12},{1,13},{2,14},{3,15},{4,8},{5,9},{6,10},{7,11},{8,4},{9,5},... | collective-permute-start | bytes 196616 | tf_op jit(solution)/shard_map/ppermute | solution.py:179
  65.8 6.4 %collective-permute-start.13 = (bf16[256,128]{1,0:T(8,128)(2,1)S(1)}, bf16[256,128]{1,0:T(8,128)(2,1)S(1)}, u32[]{:S(2)}, u32[]{:S(2)}) collective-permute-start(bf16[256,128]{1,0:T(8,128)(2,1)S(1)} %get-tuple-element.38), channel_id=1, source_target_pairs={{0,8},{1,9},{2,10},{3,11},{4,12},{5,13},{6,14},{7,15},{8,0},{9,1},... | collective-permute-start | bytes 196616 | tf_op jit(solution)/shard_map/ppermute | solution.py:179
  65.8 6.4 %collective-permute-start.14 = (bf16[256,128]{1,0:T(8,128)(2,1)S(1)}, bf16[256,128]{1,0:T(8,128)(2,1)S(1)}, u32[]{:S(2)}, u32[]{:S(2)}) collective-permute-start(bf16[256,128]{1,0:T(8,128)(2,1)S(1)} %get-tuple-element.39), channel_id=1, source_target_pairs={{0,4},{1,5},{2,6},{3,7},{4,0},{5,1},{6,2},{7,3},{8,12},{9,13},{10,... | collective-permute-start | bytes 196616 | tf_op jit(solution)/shard_map/ppermute | solution.py:179

commit v3 on v2

v3 whole, which is shorter than its diff:
```python
import functools

import jax
import jax.numpy as jnp
from jax import lax
from jax.experimental import pallas as pl
from jax.experimental.pallas import tpu as pltpu
from jax.sharding import PartitionSpec as P

BH = 16
BW = 128
PS = 16
BOXES = PS * BH
SIDE = 128
WIDE = 256
LEAN = 64
TALL = 2 * BH
GROUP = 8

band_reach = 8.0

VMEM = pl.BlockSpec(memory_space=pltpu.VMEM)
SMEM = pl.BlockSpec(memory_space=pltpu.SMEM)


def params():
    return pltpu.CompilerParams(vmem_limit_bytes=48 * 1024 * 1024)


def place(owner, me, peers):
    away = jnp.bitwise_xor(owner, me)
    return (away & 1) * (peers // 2) + ((away >> 1) & 1) * (peers // 4) + (away >> 2)


def name_tiles(peers):
    return 1 if peers * PS <= 256 else 2


def chunk_rows(peers):
    return BOXES + (name_tiles(peers) + 1) * peers


def windows(width):
    found = []
    for first in range(0, width, WIDE):
        low, high = max(first - SIDE, 0), min(first + WIDE + SIDE, width)
        found.append((low, high, low - first + SIDE, high - first + SIDE))
    return found


def turned(x, by):
    return pltpu.roll(x, by % BW, 1)


def lanczos_taps(gap, whole, part):
    shift = whole + part
    band = jnp.zeros(gap.shape, jnp.float32)
    for tap in range(-2, 5):
        spot = whole + tap
        x = jnp.full((8, 128), spot - shift, jnp.float32)

        def sinc(v):
            angle = jnp.pi * v
            return jnp.where(v == 0.0, 1.0, jnp.sin(angle) / jnp.where(v == 0.0, 1.0, angle))

        value = jnp.where(jnp.abs(x) < 3.0, sinc(x) * sinc(x / 3.0), 0.0)
        band = jnp.where(gap == spot, value[0:1, 0:1], band)
    return band.astype(jnp.bfloat16)


OWNER, SLOT, MISC = 0, 1, 2
OFFSET, FRACTION, WEIGHT, BASES = 0, 2, 4, 5


def pack(owner, slot, band_offset, shift_frac, weight, basis_index, basis_coef):
    def line(x):
        return x.astype(jnp.float32).reshape(1, -1)

    misc = jnp.concatenate([line(x) for x in (band_offset, shift_frac, weight, basis_index, basis_coef)], axis=1)
    misc = jnp.pad(misc, ((0, 0), (0, BW - misc.shape[1])))
    return jnp.concatenate([line(owner), line(slot), misc, jnp.zeros((5, BW), jnp.float32)], axis=0)


def warp_kernel(peers, bases, picture, packed, scalars, me_ref, keep, send, total, wide_band, spots, starts, sem):
    rows, width = picture.shape
    me = me_ref[0]
    chunk = chunk_rows(peers)
    half = peers // 2 * chunk
    named = packed[OWNER : OWNER + 1, :].astype(jnp.int32)
    slots = packed[SLOT : SLOT + 1, :].astype(jnp.int32)
    spots[...] = (place(named, me, peers) * PS + slots) * BH
    copy = pltpu.make_async_copy(spots, starts, sem)
    copy.start()
    total[...] = jnp.zeros_like(total)

    heavy = packed[MISC : MISC + 1, WEIGHT : WEIGHT + 1]
    mean = jnp.sum(jnp.sum(picture[...].astype(jnp.float32), axis=0, keepdims=True), axis=1, keepdims=True)
    mean = (mean * (1.0 / (rows * width))).astype(jnp.bfloat16).astype(jnp.float32)

    if name_tiles(peers) == 1:
        names = [packed[OWNER : OWNER + 1, :] * PS + packed[SLOT : SLOT + 1, :]]
    else:
        names = [packed[OWNER : OWNER + 1, :], packed[SLOT : SLOT + 1, :]]
    misc = packed[MISC : MISC + 1, :]
    lane = lax.broadcasted_iota(jnp.int32, (1, BW), 1)

    def lanes(x, first, count, to):
        moved = turned(jnp.broadcast_to(x, (8, BW)), to - first)[0:1]
        return jnp.where((lane >= to) & (lane < to + count), moved, 0.0)

    high = misc.astype(jnp.bfloat16).astype(jnp.float32)
    middle = (misc - high).astype(jnp.bfloat16).astype(jnp.float32)
    low = misc - high - middle
    numbers = lanes(misc, BASES, bases, 0)
    for i, piece in enumerate((high, middle, low)):
        numbers = numbers + lanes(piece, BASES + bases, bases, (1 + i) * bases)
    numbers = numbers + jnp.where(lane == 4 * bases, heavy, 0.0) + jnp.where(lane == 4 * bases + 1, mean, 0.0)
    row = lax.broadcasted_iota(jnp.int32, (peers, BW), 0)
    tags = jnp.concatenate(
        [jnp.where(row == me, x, 0.0).astype(jnp.bfloat16) for x in (*names, numbers)], axis=0
    )

    gap = (
        lax.broadcasted_iota(jnp.int32, (WIDE + 2 * SIDE, WIDE), 0)
        - lax.broadcasted_iota(jnp.int32, (WIDE + 2 * SIDE, WIDE), 1)
        - SIDE
    ).astype(jnp.float32)
    wide_band[...] = lanczos_taps(gap, scalars[MISC, OFFSET + 1], scalars[MISC, FRACTION + 1])
    gap = (
        lax.broadcasted_iota(jnp.int32, (rows, rows), 1) - lax.broadcasted_iota(jnp.int32, (rows, rows), 0)
    ).astype(jnp.float32)
    row_warp = lanczos_taps(gap, scalars[MISC, OFFSET], scalars[MISC, FRACTION])
    passes = [
        jnp.dot(
            picture[:, low:high], wide_band[top:bottom, :], preferred_element_type=jnp.float32
        ).astype(jnp.bfloat16)
        for low, high, top, bottom in windows(width)
    ]
    copy.wait()
    across = WIDE // BW
    for block, col_pass in enumerate(passes):
        done = jnp.dot(row_warp, col_pass, preferred_element_type=jnp.float32).astype(jnp.bfloat16)
        scaled = (done.astype(jnp.float32) - mean) * heavy
        for down in range(rows // BH):
            for col in range(across):
                box = down * (width // BW) + block * across + col
                piece = pl.ds(pl.multiple_of(starts[0, box], BH), BH)
                total[piece, :] += scaled[down * BH : (down + 1) * BH, col * BW : (col + 1) * BW]

    @pl.loop(0, peers // 2)
    def _(i):
        start = pl.multiple_of(i * chunk, PS)
        for out, base in ((keep, 0), (send, peers // 2 * BOXES)):
            source = pl.multiple_of(base + i * BOXES, BOXES)
            out[pl.ds(start, BOXES), :] = total[pl.ds(source, BOXES), :].astype(jnp.bfloat16)
            out[pl.ds(start + BOXES, chunk - BOXES), :] = tags


def add_kernel(parts, ours, theirs, *outs):
    length = ours.shape[0] // parts
    for i, out in enumerate(outs):
        here = pl.ds(i * length, length)
        out[...] = (ours[here, :].astype(jnp.float32) + theirs[here, :].astype(jnp.float32)).astype(jnp.bfloat16)


def add_parts(ours, theirs, parts):
    length = ours.shape[0] // parts
    return pl.pallas_call(
        functools.partial(add_kernel, parts),
        out_shape=[jax.ShapeDtypeStruct((length, BW), jnp.bfloat16)] * parts,
        in_specs=[VMEM, VMEM],
        out_specs=[VMEM] * parts,
        compiler_params=params(),
        name="add_parts",
    )(ours, theirs)


def swap(x, axis_size, bit):
    return lax.ppermute(x, "visit", [(i, i ^ bit) for i in range(axis_size)])


def scatter_sum(keep, send, peers):
    near = swap(send, peers, 1)
    ours, theirs = add_parts(keep, near, 2)
    near = swap(theirs, peers, 2)
    terms = add_parts(ours, near, peers // 4)
    return [terms[0]] + [swap(terms[far], peers, 4 * far) for far in reversed(range(1, peers // 4))]


def join_kernel(*refs):
    *parts, out = refs
    length = parts[0].shape[0]
    for i, part in enumerate(parts):
        out[i * length : (i + 1) * length, :] = part[...]


def join(*parts):
    rows, lanes = parts[0].shape
    return pl.pallas_call(
        join_kernel,
        out_shape=jax.ShapeDtypeStruct((rows * len(parts), lanes), parts[0].dtype),
        in_specs=[VMEM] * len(parts),
        out_specs=VMEM,
        compiler_params=params(),
        name="join",
    )(*parts)


def gather_slots(own, peers):
    line = join(own, *[swap(own, peers, 4 * away) for away in range(1, peers // 4)])
    pair = join(line, swap(line, peers, 2))
    return pair, swap(pair, peers, 1)


def summed_terms(terms, here):
    total = terms[0][here, :].astype(jnp.float32)
    for term in terms[1:]:
        total = total + term[here, :].astype(jnp.float32)
    return total


def read_tags(peers, terms):
    tiles = [
        summed_terms(terms, slice(BOXES + i * peers, BOXES + (i + 1) * peers)) for i in range(name_tiles(peers) + 1)
    ]
    if name_tiles(peers) == 1:
        name = tiles[0].astype(jnp.int32)
        owner, slot = name >> 4, name & (PS - 1)
    else:
        owner, slot = tiles[0].astype(jnp.int32), tiles[1].astype(jnp.int32)
    return owner, slot, tiles[-1]


def template_kernel(peers, bases, me_ref, *refs):
    *terms, template, leaning, coadd, weight_sum = refs
    me = me_ref[0]
    owner, slot, numbers = read_tags(peers, terms)
    heavy = numbers[:, 4 * bases : 4 * bases + 1]
    level = heavy * numbers[:, 4 * bases + 1 : 4 * bases + 2]
    mine = owner == me
    for i in range(PS):
        hit = mine & (slot == i)

        def over(x):
            found = jnp.sum(jnp.where(hit, x, 0.0), axis=0, keepdims=True)
            return jnp.sum(found, axis=1, keepdims=True)

        total = 1.0 + over(heavy)
        here = slice(i * BH, (i + 1) * BH)
        mean = (summed_terms(terms, here) + over(level)) / total
        rounded = mean.astype(jnp.bfloat16)
        template[here, :] = rounded
        leaning[here, :] = turned(rounded.astype(jnp.float32), LEAN).astype(jnp.bfloat16)
        coadd[here, :] = mean
        weight_sum[i : i + 1, :] = jnp.broadcast_to(total, (1, BW))


AROUND = [(down, across) for down in (-1, 0, 1) for across in (-1, 0, 1)]


def plan_kernel(peers, bases, most, rows_of_boxes, me_ref, *refs):
    *terms, spots, scales = refs
    me = me_ref[0]
    owner, slot, numbers = read_tags(peers, terms)
    nothing = peers * PS
    tile = place(owner, me, peers) * PS + slot
    boxes = owner.shape[1]
    cols = boxes // rows_of_boxes
    box = lax.broadcasted_iota(jnp.int32, (peers, BW), 1)
    lane = lax.broadcasted_iota(jnp.int32, (peers, BW), 1)
    mine = owner == me
    before = (
        lax.broadcasted_iota(jnp.int32, (boxes, boxes), 0) < lax.broadcasted_iota(jnp.int32, (boxes, boxes), 1)
    )
    rank = jnp.dot(
        jnp.where(mine, 1.0, 0.0).astype(jnp.bfloat16),
        jnp.where(before, 1.0, 0.0).astype(jnp.bfloat16),
        preferred_element_type=jnp.float32,
    ).astype(jnp.int32)
    tables = []
    for down, across in AROUND:
        row, col = box // cols + down, box % cols + across
        inside = (row >= 0) & (row < rows_of_boxes) & (col >= 0) & (col < cols)
        moved = turned(tile, -(down * cols + across)) if (down, across) != (0, 0) else tile
        tables.append(jnp.where(inside, moved - nothing, 0).astype(jnp.float32))
    tables.append((slot - PS).astype(jnp.float32))
    first = jnp.zeros((peers, BW), jnp.float32)
    second = jnp.zeros((peers, BW), jnp.float32)
    for j in range(most):
        chosen = mine & (rank == j)
        for i, table in enumerate(tables):
            value = jnp.sum(jnp.where(chosen, table, 0.0), axis=1, keepdims=True)
            value = value + (nothing if i < 9 else PS)
            if i < 8:
                first = jnp.where(lane == i * most + j, value, first)
            else:
                second = jnp.where(lane == (i - 8) * most + j, value, second)
    index = turned(numbers, 2 * most)
    second = jnp.where((lane >= 2 * most) & (lane < 2 * most + bases), index, second)
    spots[0:peers, :] = (first * BH).astype(jnp.int32)
    spots[peers : 2 * peers, :] = (jnp.where(lane < 2 * most, second * BH, second)).astype(jnp.int32)
    coef = turned(numbers, -bases) + turned(numbers, -2 * bases) + turned(numbers, -3 * bases)
    heavy = numbers[:, 4 * bases : 4 * bases + 1]
    scales[...] = jnp.where(lane < bases, coef * heavy, 0.0)


def gauss_kernel(basis_width, across_bands, down_bands):
    tap = lax.broadcasted_iota(jnp.int32, (8, 128), 1).astype(jnp.float32) - band_reach
    shape = across_bands.shape[1:]
    across_gap = (
        lax.broadcasted_iota(jnp.int32, shape, 0) - lax.broadcasted_iota(jnp.int32, shape, 1) - LEAN
    ).astype(jnp.float32)
    shape = down_bands.shape[1:]
    out_row = lax.broadcasted_iota(jnp.int32, shape, 0)
    in_row = lax.broadcasted_iota(jnp.int32, shape, 1)
    inner = in_row % TALL
    down_gap = jnp.where(inner < BH + BH // 2, inner, inner - TALL) - out_row % BH
    down_gap = jnp.where(out_row // BH == in_row // TALL, down_gap, 1024).astype(jnp.float32)
    for member in range(across_bands.shape[0]):
        blur_width = basis_width[member]
        spread = 2.0 * blur_width * blur_width
        total = jnp.sum(jnp.where(tap <= band_reach, jnp.exp(-tap * tap / spread), 0.0), axis=1, keepdims=True)[0:1]
        for gap, out in ((across_gap, across_bands), (down_gap, down_bands)):
            value = jnp.where(jnp.abs(gap) <= band_reach, jnp.exp(-gap * gap / spread), 0.0)
            out[member] = (value / total).astype(jnp.bfloat16)


def match_kernel(
    peers,
    bases,
    most,
    steps,
    near,
    other,
    across_bands,
    down_bands,
    coadd,
    weight_sum,
    spots,
    scales,
    out,
    table,
    window,
    blurred,
    matched,
):
    groups = pl.cdiv(most, GROUP)
    high = GROUP * TALL
    half = near.shape[0]
    table[0:half, :] = near[...]
    table[half : 2 * half, :] = other[...]
    table[2 * half :, :] = jnp.zeros((BH, BW), jnp.bfloat16)
    matched[...] = jnp.zeros_like(matched)
    if most % GROUP:
        window[...] = jnp.zeros_like(window)
    lane = lax.broadcasted_iota(jnp.int32, (BH, BW), 1)
    row = lax.broadcasted_iota(jnp.int32, (BH, BW), 0)
    left = lane < LEAN
    upper = row < BH // 2

    @pl.loop(0, peers // steps)
    def _(turn):
        for step in range(steps):
            visit = turn * steps + step
            for j in range(most):

                def tile(i):
                    at = spots[visit, i * most + j] if i < 8 else spots[peers + visit, j]
                    return table[pl.ds(pl.multiple_of(at, BH), BH), :]

                tiles = [tile(i) for i in range(9)]
                mixed = [jnp.where(upper, tiles[6 + i], tiles[i]) for i in range(3)]
                start = (step * groups * GROUP + j) * TALL
                for base, (west, middle, east) in ((0, tiles[3:6]), (BH, mixed)):
                    window[start + base : start + base + BH, 0:BW] = jnp.where(left, west, middle)
                    window[start + base : start + base + BH, BW:] = jnp.where(left, middle, east)
        for step in range(steps):
            visit = turn * steps + step
            here = slice(step * groups * high, (step + 1) * groups * high)
            for member in range(0, bases, 2):
                pair = range(member, min(member + 2, bases))
                band = [across_bands[spots[peers + visit, 2 * most + k]] for k in pair]
                band = jnp.concatenate(band, axis=1) if len(band) > 1 else band[0]
                blurred[here, member * BW : member * BW + band.shape[1]] = jnp.dot(
                    window[here, :], band, preferred_element_type=jnp.float32
                ).astype(jnp.bfloat16)
        for step in range(steps):
            visit = turn * steps + step
            for group in range(groups):
                here = slice((step * groups + group) * high, (step * groups + group + 1) * high)
                total = jnp.zeros((GROUP * BH, BW), jnp.float32)
                for k in range(bases):
                    total = total + scales[visit, k] * jnp.dot(
                        down_bands[spots[peers + visit, 2 * most + k]],
                        blurred[here, k * BW : (k + 1) * BW],
                        preferred_element_type=jnp.float32,
                    )
                for i in range(min(GROUP, most - group * GROUP)):
                    at = spots[peers + visit, most + group * GROUP + i]
                    matched[pl.ds(pl.multiple_of(at, BH), BH), :] += total[i * BH : (i + 1) * BH]

    for i in range(PS):
        here = slice(i * BH, (i + 1) * BH)
        out[here, :] = coadd[here, :] - matched[here, :] / weight_sum[i : i + 1, :]


def shards(
    visit_image,
    band_offset,
    shift_frac,
    weights,
    box_owner,
    box_slot,
    basis_index,
    basis_coef,
    basis_width,
):
    peers = lax.axis_size("visit")
    rows, width = visit_image.shape[1:]
    bases = basis_index.shape[1]
    table_size = basis_width.shape[0]
    most = max(2, 2 * box_slot.shape[1] // peers)
    me = lax.axis_index("visit").astype(jnp.int32).reshape(1)
    chunk = chunk_rows(peers)
    packed = pack(box_owner, box_slot, band_offset, shift_frac, weights, basis_index, basis_coef)

    half = jax.ShapeDtypeStruct((peers // 2 * chunk, BW), jnp.bfloat16)
    keep, send = pl.pallas_call(
        functools.partial(warp_kernel, peers, bases),
        out_shape=[half, half],
        in_specs=[VMEM, VMEM, SMEM, SMEM],
        out_specs=[VMEM] * 2,
        scratch_shapes=[
            pltpu.VMEM((peers * BOXES, BW), jnp.float32),
            pltpu.VMEM((WIDE + 2 * SIDE, WIDE), jnp.bfloat16),
            pltpu.VMEM((1, BW), jnp.int32),
            pltpu.SMEM((1, BW), jnp.int32),
            pltpu.SemaphoreType.DMA,
        ],
        compiler_params=params(),
        name="warp",
    )(visit_image[0], packed, packed, me)

    across_bands, down_bands = pl.pallas_call(
        gauss_kernel,
        out_shape=[
            jax.ShapeDtypeStruct((table_size, BW + 2 * LEAN, BW), jnp.bfloat16),
            jax.ShapeDtypeStruct((table_size, GROUP * BH, GROUP * TALL), jnp.bfloat16),
        ],
        in_specs=[SMEM],
        out_specs=[VMEM] * 2,
        compiler_params=params(),
        name="gauss_bands",
    )(basis_width)

    terms = scatter_sum(keep, send, peers)
    square = jax.ShapeDtypeStruct((BOXES, BW), jnp.bfloat16)
    template, leaning, coadd, weight_sum = pl.pallas_call(
        functools.partial(template_kernel, peers, bases),
        out_shape=[
            square,
            square,
            jax.ShapeDtypeStruct((BOXES, BW), jnp.float32),
            jax.ShapeDtypeStruct((PS, BW), jnp.float32),
        ],
        in_specs=[SMEM] + [VMEM] * len(terms),
        out_specs=[VMEM] * 4,
        compiler_params=params(),
        name="template",
    )(me, *terms)
    near, other = gather_slots(leaning, peers)
    spots, scales = pl.pallas_call(
        functools.partial(plan_kernel, peers, bases, most, rows // BH),
        out_shape=[
            jax.ShapeDtypeStruct((2 * peers, BW), jnp.int32),
            jax.ShapeDtypeStruct((peers, BW), jnp.float32),
        ],
        in_specs=[SMEM] + [VMEM] * len(terms),
        out_specs=[VMEM] * 2,
        compiler_params=params(),
        name="plan",
    )(me, *terms)

    steps = 4
    tall = steps * pl.cdiv(most, GROUP) * GROUP * TALL
    difference_coadd = pl.pallas_call(
        functools.partial(match_kernel, peers, bases, most, steps),
        out_shape=jax.ShapeDtypeStruct((BOXES, BW), jnp.float32),
        in_specs=[VMEM] * 6 + [SMEM] * 2,
        out_specs=VMEM,
        scratch_shapes=[
            pltpu.VMEM(((peers * PS + 1) * BH, BW), jnp.bfloat16),
            pltpu.VMEM((tall, BW + 2 * LEAN), jnp.bfloat16),
            pltpu.VMEM((tall, bases * BW), jnp.bfloat16),
            pltpu.VMEM(((PS + 1) * BH, BW), jnp.float32),
        ],
        compiler_params=params(),
        name="match",
    )(near, other, across_bands, down_bands, coadd, weight_sum, spots, scales)
    return (template.reshape(PS, BH, BW), difference_coadd.reshape(PS, BH, BW))


def solution(mesh):
    placed = (
        P(("groups", "visit"), None, None),
        P(("groups", "visit"), None),
        P(("groups", "visit"), None),
        P(("groups", "visit")),
        P(("groups", "visit"), None, None),
        P(("groups", "visit"), None),
        P(("groups", "visit"), None),
        P(("groups", "visit"), None),
        P(),
    )
    return jax.shard_map(
        shards,
        mesh=mesh,
        in_specs=placed,
        out_specs=(P(("groups", "visit"), None, None), P(("groups", "visit"), None, None)),
        check_vma=False,
    )
```

time: 73.1 us -> 59.6 us (0.82)
  waiting for transfers between devices: 35.7 us -> 22.8 us
  starting transfers between devices: 20.4 us -> 14 us
  Pallas kernels: 10.9 us -> 17.2 us
    ppermute x15 -> x10, waiting for transfers between devices: 35.7 us -> 22.8 us  [swap(): return lax.ppermute(x, 'visit', [(i, i ^ bit) for i in range(axis_size)])]
    pallas_call x5, Pallas kernels: 10.5 us -> 17 us  [the longest x1 10.9 us: shards(): pl.pallas_call(functools.partial(match_kernel, peers, bases, most, steps)...]
    ppermute x15 -> x10, starting transfers between devices: 20.4 us -> 14 us  [swap(): return lax.ppermute(x, 'visit', [(i, i ^ bit) for i in range(axis_size)])]
    unnamed x22 -> x16, local copies, waits for them, and re-layouts: 4.51 us -> 3.66 us
  transfers between devices with their start and end apart: 15 -> 10, of which waited for: 13 -> 7; matrix products, arithmetic and copies ran while one was open for 0% -> 0% of each run, Pallas kernels for 1% -> 3%
where the time goes in v3:
time: 59.6 us; the launch traced here: 59.4 us
  waiting for transfers between devices  22.8 us (38%)
  Pallas kernels  17.2 us (29%)
  starting transfers between devices  14 us (23%)
  local copies, waits for them, and re-layouts  3.84 us (6%)
  between operations  1.41 us (2%)
    ppermute x10, waiting for transfers between devices, swap(): return lax.ppermute(x, 'visit', [(i, i ^ bit) for i in range(axis_size)])  22.8 us
    ppermute x10, starting transfers between devices, swap(): return lax.ppermute(x, 'visit', [(i, i ^ bit) for i in range(axis_size)])  14 us
    pallas_call x1, Pallas kernels, shards(): pl.pallas_call(functools.partial(match_kernel, peers, bases, most, steps)...  10.9 us
    unnamed x16, local copies, waits for them, and re-layouts  3.66 us
    pallas_call x1, Pallas kernels, shards(): pl.pallas_call(functools.partial(warp_kernel, peers, bases), out_shape=[h...  3.34 us
    pallas_call x1, Pallas kernels, shards(): pl.pallas_call(gauss_kernel, out_shape=[jax.ShapeDtypeStruct((table_size,...  1.25 us
  transfers between devices with their start and end apart: 10, of which 7 were waited for; matrix products, arithmetic and copies ran while one was open for 0% of the time, Pallas kernels for 3%

profile of v3, /device:TPU:0, one launch (start us, length us, event | category | flops | bytes accessed | tf_op | source)
XLA Modules:
  0.0 59.4 jit_solution(2531622255435653290)
XLA Ops:
  1.3 0.6 %copy-done.5 = s32[1,128,1]{1,2,0:T(1,128)S(1)} copy-done((s32[1,128,1]{1,2,0:T(1,128)S(1)}, s32[1,128,1]{1,2,0:T(1,128)}, u32[]{:S(2)}) %copy-start.5) | copy-done | bytes 536
  2.0 0.7 %copy-done.6 = s32[1,128]{1,0:T(1,128)S(1)} copy-done((s32[1,128]{1,0:T(1,128)S(1)}, s32[1,128]{1,0:T(1,128)}, u32[]{:S(2)}) %copy-start.6) | copy-done | bytes 536
  2.6 0.7 %copy-done.7 = s32[1,6]{1,0:T(1,128)S(1)} copy-done((s32[1,6]{1,0:T(1,128)S(1)}, s32[1,6]{1,0:T(1,128)}, u32[]{:S(2)}) %copy-start.7) | copy-done | bytes 48
  3.3 0.1 pad.8.clone
  3.4 0.7 %copy-done.2 = f32[1,2]{1,0:T(1,128)S(1)} copy-done((f32[1,2]{1,0:T(1,128)S(1)}, f32[1,2]{1,0:T(1,128)}, u32[]{:S(2)}) %copy-start.2) | copy-done | bytes 32
  4.0 0.1 concatenate.6
  4.1 0.1 fusion.packed.scalars
  4.2 1.0 %copy-done = bf16[1,256,1024]{2,1,0:T(8,128)(2,1)S(1)} copy-done((bf16[1,256,1024]{2,1,0:T(8,128)(2,1)S(1)}, bf16[1,256,1024]{2,1,0:T(8,128)(2,1)}, u32[]{:S(2)}) %copy-start) | copy-done | bytes 524312
  5.3 3.3 %warp.1 = (bf16[2304,128]{1,0:T(8,128)(2,1)S(1)}, bf16[2304,128]{1,0:T(8,128)(2,1)S(1)}) custom-call(bf16[256,1024]{1,0:T(8,128)(2,1)S(1)} %bitcast.9, f32[8,128]{1,0:T(8,128)S(1)} %fusion.packed.scalars, f32[8,128]{1,0:T(8,128)S(1)} %fusion.packed.scalars, s32[1]{0:T(128)} %bitcast.me_ref), custom_call_target="tpu_custom_call" | custom-call | tf_op jit(solution)/shard_map/warp/pallas_call | solution.py:428
  8.6 0.5 collective-permute-start
  9.1 1.6 %collective-permute-done.theirs = bf16[2304,128]{1,0:T(8,128)(2,1)S(1)} collective-permute-done((bf16[2304,128]{1,0:T(8,128)(2,1)S(1)}, bf16[2304,128]{1,0:T(8,128)(2,1)S(1)}, u32[]{:S(2)}, u32[]{:S(2)}) %collective-permute-start) | collective-permute-done | bytes 589856 | tf_op jit(solution)/shard_map/ppermute | solution.py:179
  10.7 0.1 add_parts.2
  10.9 3.0 %collective-permute-start.1 = (bf16[1152,128]{1,0:T(8,128)(2,1)S(1)}, bf16[1152,128]{1,0:T(8,128)(2,1)S(1)}, u32[]{:S(2)}, u32[]{:S(2)}) collective-permute-start(bf16[1152,128]{1,0:T(8,128)(2,1)S(1)} %get-tuple-element.21), channel_id=1, source_target_pairs={{0,2},{1,3},{2,0},{3,1},{4,6},{5,7},{6,4},{7,5},{8,10},{9,11},{10,... | collective-permute-start | bytes 884744 | tf_op jit(solution)/shard_map/ppermute | solution.py:179
  13.8 7.3 %collective-permute-done.1.theirs = bf16[1152,128]{1,0:T(8,128)(2,1)S(1)} collective-permute-done((bf16[1152,128]{1,0:T(8,128)(2,1)S(1)}, bf16[1152,128]{1,0:T(8,128)(2,1)S(1)}, u32[]{:S(2)}, u32[]{:S(2)}) %collective-permute-start.1) | collective-permute-done | bytes 294944 | tf_op jit(solution)/shard_map/ppermute | solution.py:179
  21.2 0.1 add_parts.3
  21.2 3.9 %collective-permute-start.2 = (bf16[288,128]{1,0:T(8,128)(2,1)S(1)}, bf16[288,128]{1,0:T(8,128)(2,1)S(1)}, u32[]{:S(2)}, u32[]{:S(2)}) collective-permute-start(bf16[288,128]{1,0:T(8,128)(2,1)S(1)} %get-tuple-element.23), channel_id=1, source_target_pairs={{0,12},{1,13},{2,14},{3,15},{4,8},{5,9},{6,10},{7,11},{8,4},{9,5},... | collective-permute-start | bytes 221192 | tf_op jit(solution)/shard_map/ppermute | solution.py:179
  25.1 0.6 %collective-permute-start.4 = (bf16[288,128]{1,0:T(8,128)(2,1)S(1)}, bf16[288,128]{1,0:T(8,128)(2,1)S(1)}, u32[]{:S(2)}, u32[]{:S(2)}) collective-permute-start(bf16[288,128]{1,0:T(8,128)(2,1)S(1)} %get-tuple-element.25), channel_id=1, source_target_pairs={{0,4},{1,5},{2,6},{3,7},{4,0},{5,1},{6,2},{7,3},{8,12},{9,13},{10,... | collective-permute-start | bytes 221192 | tf_op jit(solution)/shard_map/ppermute | solution.py:179
  25.7 2.6 %collective-permute-done.2.refs_1_ = bf16[288,128]{1,0:T(8,128)(2,1)S(1)} collective-permute-done((bf16[288,128]{1,0:T(8,128)(2,1)S(1)}, bf16[288,128]{1,0:T(8,128)(2,1)S(1)}, u32[]{:S(2)}, u32[]{:S(2)}) %collective-permute-start.2) | collective-permute-done | bytes 73760 | tf_op jit(solution)/shard_map/ppermute | solution.py:179
  28.3 2.6 %collective-permute-done.3.refs_2_ = bf16[288,128]{1,0:T(8,128)(2,1)S(1)} collective-permute-done((bf16[288,128]{1,0:T(8,128)(2,1)S(1)}, bf16[288,128]{1,0:T(8,128)(2,1)S(1)}, u32[]{:S(2)}, u32[]{:S(2)}) %collective-permute-start.3) | collective-permute-done | bytes 73760 | tf_op jit(solution)/shard_map/ppermute | solution.py:179
  30.9 0.0 collective-permute-done.4.refs_3_
  30.9 0.9 %template.1 = (bf16[256,128]{1,0:T(8,128)(2,1)}, bf16[256,128]{1,0:T(8,128)(2,1)S(1)}, f32[256,128]{1,0:T(8,128)S(1)}, f32[16,128]{1,0:T(8,128)S(1)}) custom-call(s32[1]{0:T(128)} %bitcast.me_ref, bf16[288,128]{1,0:T(8,128)(2,1)S(1)} %get-tuple-element.22.refs_0_, bf16[288,128]{1,0:T(8,128)(2,1)S(1)} %collective-permute-done.2.refs_1_, ...), custom_call_target="tpu_custom_call" | custom-call | tf_op jit(solution)/shard_map/template/pallas_call | solution.py:458
  31.8 2.6 %collective-permute-start.7 = (bf16[256,128]{1,0:T(8,128)(2,1)S(1)}, bf16[256,128]{1,0:T(8,128)(2,1)S(1)}, u32[]{:S(2)}, u32[]{:S(2)}) collective-permute-start(bf16[256,128]{1,0:T(8,128)(2,1)S(1)} %get-tuple-element.27.refs_0_), channel_id=1, source_target_pairs={{0,12},{1,13},{2,14},{3,15},{4,8},{5,9},{6,10},{7,11},{8,4},{9,5},... | collective-permute-start | bytes 196616 | tf_op jit(solution)/shard_map/ppermute | solution.py:179
  34.4 1.8 %collective-permute-start.5 = (bf16[256,128]{1,0:T(8,128)(2,1)S(1)}, bf16[256,128]{1,0:T(8,128)(2,1)S(1)}, u32[]{:S(2)}, u32[]{:S(2)}) collective-permute-start(bf16[256,128]{1,0:T(8,128)(2,1)S(1)} %get-tuple-element.27.refs_0_), channel_id=1, source_target_pairs={{0,4},{1,5},{2,6},{3,7},{4,0},{5,1},{6,2},{7,3},{8,12},{9,13},{10,... | collective-permute-start | bytes 196616 | tf_op jit(solution)/shard_map/ppermute | solution.py:179
  36.2 2.4 %collective-permute-done.7.refs_3_ = bf16[256,128]{1,0:T(8,128)(2,1)S(1)} collective-permute-done((bf16[256,128]{1,0:T(8,128)(2,1)S(1)}, bf16[256,128]{1,0:T(8,128)(2,1)S(1)}, u32[]{:S(2)}, u32[]{:S(2)}) %collective-permute-start.7) | collective-permute-done | bytes 65568 | tf_op jit(solution)/shard_map/ppermute | solution.py:179
  38.6 1.4 %collective-permute-done.6.refs_2_ = bf16[256,128]{1,0:T(8,128)(2,1)S(1)} collective-permute-done((bf16[256,128]{1,0:T(8,128)(2,1)S(1)}, bf16[256,128]{1,0:T(8,128)(2,1)S(1)}, u32[]{:S(2)}, u32[]{:S(2)}) %collective-permute-start.6) | collective-permute-done | bytes 65568 | tf_op jit(solution)/shard_map/ppermute | solution.py:179
  40.0 1.5 %collective-permute-start.8 = (bf16[1024,128]{1,0:T(8,128)(2,1)S(1)}, bf16[1024,128]{1,0:T(8,128)(2,1)S(1)}, u32[]{:S(2)}, u32[]{:S(2)}) collective-permute-start(bf16[1024,128]{1,0:T(8,128)(2,1)S(1)} %join.2.refs_0_), channel_id=1, source_target_pairs={{0,2},{1,3},{2,0},{3,1},{4,6},{5,7},{6,4},{7,5},{8,10},{9,11},{10,... | collective-permute-start | bytes 786440 | tf_op jit(solution)/shard_map/ppermute | solution.py:179
  41.5 4.9 %collective-permute-done.8.refs_1_ = bf16[1024,128]{1,0:T(8,128)(2,1)S(1)} collective-permute-done((bf16[1024,128]{1,0:T(8,128)(2,1)S(1)}, bf16[1024,128]{1,0:T(8,128)(2,1)S(1)}, u32[]{:S(2)}, u32[]{:S(2)}) %collective-permute-start.8) | collective-permute-done | bytes 262176 | tf_op jit(solution)/shard_map/ppermute | solution.py:179
  46.5 0.1 collective-permute-start.9
  46.6 1.3 %gauss_bands.1 = (bf16[12,256,128]{2,1,0:T(8,128)(2,1)S(1)}, bf16[12,128,256]{2,1,0:T(8,128)(2,1)S(1)}) custom-call(f32[12]{0:T(128)S(1)} %copy-done.1), custom_call_target="tpu_custom_call" | custom-call | tf_op jit(solution)/shard_map/gauss_bands/pallas_call | solution.py:444
  47.8 0.6 plan.1
  48.4 0.0 collective-permute-done.9.other
  48.4 10.9 %match.1 = f32[256,128]{1,0:T(8,128)} custom-call(bf16[2048,128]{1,0:T(8,128)(2,1)S(1)} %join.3.near, bf16[2048,128]{1,0:T(8,128)(2,1)S(1)} %collective-permute-done.9.other, bf16[12,256,128]{2,1,0:T(8,128)(2,1)S(1)} %get-tuple-element.28.across_bands, bf16[12,128,256]{2,1,0:T(8,128)(2,1)S(1)} %get-tuple-element.29.down_bands, ...), custom_call_target="tpu_custom_call" | custom-call | tf_op jit(solution)/shard_map/match/pallas_call | solution.py:486
  (21 shorter events, 0.1 us)
Async XLA Ops:
  0.6 0.7 %copy-start.4 = (s32[1,2]{1,0:T(1,128)S(1)}, s32[1,2]{1,0:T(1,128)}, u32[]{:S(2)}) copy-start(s32[1,2]{1,0:T(1,128)} %param.10) | copy-start | bytes 28
  1.3 0.7 %copy-start.5 = (s32[1,128,1]{1,2,0:T(1,128)S(1)}, s32[1,128,1]{1,2,0:T(1,128)}, u32[]{:S(2)}) copy-start(s32[1,128,1]{1,2,0:T(1,128)} %param.13) | copy-start | bytes 1540
  2.0 0.7 %copy-start.6 = (s32[1,128]{1,0:T(1,128)S(1)}, s32[1,128]{1,0:T(1,128)}, u32[]{:S(2)}) copy-start(s32[1,128]{1,0:T(1,128)} %param.14) | copy-start | bytes 1540
  2.6 0.7 %copy-start.7 = (s32[1,6]{1,0:T(1,128)S(1)}, s32[1,6]{1,0:T(1,128)}, u32[]{:S(2)}) copy-start(s32[1,6]{1,0:T(1,128)} %param.15) | copy-start | bytes 76
  3.4 0.7 %copy-start.2 = (f32[1,2]{1,0:T(1,128)S(1)}, f32[1,2]{1,0:T(1,128)}, u32[]{:S(2)}) copy-start(f32[1,2]{1,0:T(1,128)} %param.11) | copy-start | bytes 28
  3.4 0.7 %copy-start.3 = (f32[1,6]{1,0:T(1,128)S(1)}, f32[1,6]{1,0:T(1,128)}, u32[]{:S(2)}) copy-start(f32[1,6]{1,0:T(1,128)} %param.16) | copy-start | bytes 76
  4.2 1.0 %copy-start = (bf16[1,256,1024]{2,1,0:T(8,128)(2,1)S(1)}, bf16[1,256,1024]{2,1,0:T(8,128)(2,1)}, u32[]{:S(2)}) copy-start(bf16[1,256,1024]{2,1,0:T(8,128)(2,1)} %param.9) | copy-start | bytes 1572868
  8.6 2.1 %collective-permute-start = (bf16[2304,128]{1,0:T(8,128)(2,1)S(1)}, bf16[2304,128]{1,0:T(8,128)(2,1)S(1)}, u32[]{:S(2)}, u32[]{:S(2)}) collective-permute-start(bf16[2304,128]{1,0:T(8,128)(2,1)S(1)} %get-tuple-element.19), channel_id=1, source_target_pairs={{0,1},{1,0},{2,3},{3,2},{4,5},{5,4},{6,7},{7,6},{8,9},{9,8},{10,11... | collective-permute-start | bytes 1769480 | tf_op jit(solution)/shard_map/ppermute | solution.py:179
  10.9 10.3 %collective-permute-start.1 = (bf16[1152,128]{1,0:T(8,128)(2,1)S(1)}, bf16[1152,128]{1,0:T(8,128)(2,1)S(1)}, u32[]{:S(2)}, u32[]{:S(2)}) collective-permute-start(bf16[1152,128]{1,0:T(8,128)(2,1)S(1)} %get-tuple-element.21), channel_id=1, source_target_pairs={{0,2},{1,3},{2,0},{3,1},{4,6},{5,7},{6,4},{7,5},{8,10},{9,11},{10,... | collective-permute-start | bytes 884744 | tf_op jit(solution)/shard_map/ppermute | solution.py:179
  21.2 7.1 %collective-permute-start.2 = (bf16[288,128]{1,0:T(8,128)(2,1)S(1)}, bf16[288,128]{1,0:T(8,128)(2,1)S(1)}, u32[]{:S(2)}, u32[]{:S(2)}) collective-permute-start(bf16[288,128]{1,0:T(8,128)(2,1)S(1)} %get-tuple-element.23), channel_id=1, source_target_pairs={{0,12},{1,13},{2,14},{3,15},{4,8},{5,9},{6,10},{7,11},{8,4},{9,5},... | collective-permute-start | bytes 221192 | tf_op jit(solution)/shard_map/ppermute | solution.py:179
  25.1 5.8 %collective-permute-start.3 = (bf16[288,128]{1,0:T(8,128)(2,1)S(1)}, bf16[288,128]{1,0:T(8,128)(2,1)S(1)}, u32[]{:S(2)}, u32[]{:S(2)}) collective-permute-start(bf16[288,128]{1,0:T(8,128)(2,1)S(1)} %get-tuple-element.24), channel_id=1, source_target_pairs={{0,8},{1,9},{2,10},{3,11},{4,12},{5,13},{6,14},{7,15},{8,0},{9,1},... | collective-permute-start | bytes 221192 | tf_op jit(solution)/shard_map/ppermute | solution.py:179
  25.1 5.8 %collective-permute-start.4 = (bf16[288,128]{1,0:T(8,128)(2,1)S(1)}, bf16[288,128]{1,0:T(8,128)(2,1)S(1)}, u32[]{:S(2)}, u32[]{:S(2)}) collective-permute-start(bf16[288,128]{1,0:T(8,128)(2,1)S(1)} %get-tuple-element.25), channel_id=1, source_target_pairs={{0,4},{1,5},{2,6},{3,7},{4,0},{5,1},{6,2},{7,3},{8,12},{9,13},{10,... | collective-permute-start | bytes 221192 | tf_op jit(solution)/shard_map/ppermute | solution.py:179
  31.8 6.8 %collective-permute-start.7 = (bf16[256,128]{1,0:T(8,128)(2,1)S(1)}, bf16[256,128]{1,0:T(8,128)(2,1)S(1)}, u32[]{:S(2)}, u32[]{:S(2)}) collective-permute-start(bf16[256,128]{1,0:T(8,128)(2,1)S(1)} %get-tuple-element.27.refs_0_), channel_id=1, source_target_pairs={{0,12},{1,13},{2,14},{3,15},{4,8},{5,9},{6,10},{7,11},{8,4},{9,5},... | collective-permute-start | bytes 196616 | tf_op jit(solution)/shard_map/ppermute | solution.py:179
  34.4 5.6 %collective-permute-start.6 = (bf16[256,128]{1,0:T(8,128)(2,1)S(1)}, bf16[256,128]{1,0:T(8,128)(2,1)S(1)}, u32[]{:S(2)}, u32[]{:S(2)}) collective-permute-start(bf16[256,128]{1,0:T(8,128)(2,1)S(1)} %get-tuple-element.27.refs_0_), channel_id=1, source_target_pairs={{0,8},{1,9},{2,10},{3,11},{4,12},{5,13},{6,14},{7,15},{8,0},{9,1},... | collective-permute-start | bytes 196616 | tf_op jit(solution)/shard_map/ppermute | solution.py:179
  34.4 5.6 %collective-permute-start.5 = (bf16[256,128]{1,0:T(8,128)(2,1)S(1)}, bf16[256,128]{1,0:T(8,128)(2,1)S(1)}, u32[]{:S(2)}, u32[]{:S(2)}) collective-permute-start(bf16[256,128]{1,0:T(8,128)(2,1)S(1)} %get-tuple-element.27.refs_0_), channel_id=1, source_target_pairs={{0,4},{1,5},{2,6},{3,7},{4,0},{5,1},{6,2},{7,3},{8,12},{9,13},{10,... | collective-permute-start | bytes 196616 | tf_op jit(solution)/shard_map/ppermute | solution.py:179
  40.0 6.6 %copy-start.1 = (f32[12]{0:T(128)S(1)}, f32[12]{0:T(128)}, u32[]{:S(2)}) copy-start(f32[12]{0:T(128)} %basis_width.1) | copy-start | bytes 148
  40.0 6.4 %collective-permute-start.8 = (bf16[1024,128]{1,0:T(8,128)(2,1)S(1)}, bf16[1024,128]{1,0:T(8,128)(2,1)S(1)}, u32[]{:S(2)}, u32[]{:S(2)}) collective-permute-start(bf16[1024,128]{1,0:T(8,128)(2,1)S(1)} %join.2.refs_0_), channel_id=1, source_target_pairs={{0,2},{1,3},{2,0},{3,1},{4,6},{5,7},{6,4},{7,5},{8,10},{9,11},{10,... | collective-permute-start | bytes 786440 | tf_op jit(solution)/shard_map/ppermute | solution.py:179
  46.5 2.0 %collective-permute-start.9 = (bf16[2048,128]{1,0:T(8,128)(2,1)S(1)}, bf16[2048,128]{1,0:T(8,128)(2,1)S(1)}, u32[]{:S(2)}, u32[]{:S(2)}) collective-permute-start(bf16[2048,128]{1,0:T(8,128)(2,1)S(1)} %join.3.near), channel_id=1, source_target_pairs={{0,1},{1,0},{2,3},{3,2},{4,5},{5,4},{6,7},{7,6},{8,9},{9,8},{10,11... | collective-permute-start | bytes 1572872 | tf_op jit(solution)/shard_map/ppermute | solution.py:179

commit v4 on v3

--- a/solution.py
+++ b/solution.py
@@ -73,12 +73,20 @@
 
 
 def pack(owner, slot, band_offset, shift_frac, weight, basis_index, basis_coef):
-    def line(x):
-        return x.astype(jnp.float32).reshape(1, -1)
-
-    misc = jnp.concatenate([line(x) for x in (band_offset, shift_frac, weight, basis_index, basis_coef)], axis=1)
-    misc = jnp.pad(misc, ((0, 0), (0, BW - misc.shape[1])))
-    return jnp.concatenate([line(owner), line(slot), misc, jnp.zeros((5, BW), jnp.float32)], axis=0)
+    def put(x, row, lane):
+        x = x.astype(jnp.float32).reshape(1, -1)
+        return jnp.pad(x, ((row, 7 - row), (lane, BW - lane - x.shape[1])))
+
+    bases = basis_index.shape[1]
+    return (
+        put(owner, OWNER, 0)
+        + put(slot, SLOT, 0)
+        + put(band_offset, MISC, OFFSET)
+        + put(shift_frac, MISC, FRACTION)
+        + put(weight, MISC, WEIGHT)
+        + put(basis_index, MISC, BASES)
+        + put(basis_coef, MISC, BASES + bases)
+    )
 
 
 def warp_kernel(peers, bases, picture, packed, scalars, me_ref, keep, send, total, wide_band, spots, starts, sem):
@@ -386,18 +394,20 @@
                 ).astype(jnp.bfloat16)
         for step in range(steps):
             visit = turn * steps + step
-            for group in range(groups):
-                here = slice((step * groups + group) * high, (step * groups + group + 1) * high)
-                total = jnp.zeros((GROUP * BH, BW), jnp.float32)
-                for k in range(bases):
-                    total = total + scales[visit, k] * jnp.dot(
-                        down_bands[spots[peers + visit, 2 * most + k]],
-                        blurred[here, k * BW : (k + 1) * BW],
-                        preferred_element_type=jnp.float32,
-                    )
-                for i in range(min(GROUP, most - group * GROUP)):
-                    at = spots[peers + visit, most + group * GROUP + i]
-                    matched[pl.ds(pl.multiple_of(at, BH), BH), :] += total[i * BH : (i + 1) * BH]
+            parts = [slice((step * groups + i) * high, (step * groups + i + 1) * high) for i in range(groups)]
+            total = jnp.zeros((GROUP * BH, groups * BW), jnp.float32)
+            for k in range(bases):
+                side = [blurred[here, k * BW : (k + 1) * BW] for here in parts]
+                side = jnp.concatenate(side, axis=1) if groups > 1 else side[0]
+                total = total + scales[visit, k] * jnp.dot(
+                    down_bands[spots[peers + visit, 2 * most + k]], side, preferred_element_type=jnp.float32
+                )
+            for j in range(most):
+                group, i = divmod(j, GROUP)
+                at = spots[peers + visit, most + j]
+                matched[pl.ds(pl.multiple_of(at, BH), BH), :] += total[
+                    i * BH : (i + 1) * BH, group * BW : (group + 1) * BW
+                ]
 
     for i in range(PS):
         here = slice(i * BH, (i + 1) * BH)
@@ -481,7 +491,7 @@
         name="plan",
     )(me, *terms)
 
-    steps = 4
+    steps = min(peers, 16)
     tall = steps * pl.cdiv(most, GROUP) * GROUP * TALL
     difference_coadd = pl.pallas_call(
         functools.partial(match_kernel, peers, bases, most, steps),

time: 59.6 us -> 56.9 us (0.955)
  Pallas kernels: 17.2 us -> 14.8 us
    pallas_call x1, Pallas kernels: 10.9 us -> 8.44 us  [shards(): pl.pallas_call(functools.partial(match_kernel, peers, bases, most, steps)...]
  transfers between devices with their start and end apart: 10 -> 10, of which waited for: 7 -> 8; matrix products, arithmetic and copies ran while one was open for 0% -> 0% of each run, Pallas kernels for 3% -> 3%
where the time goes in v4:
time: 56.9 us; the launch traced here: 56.7 us
  waiting for transfers between devices  22.8 us (40%)
  Pallas kernels  14.8 us (26%)
  starting transfers between devices  14 us (25%)
  local copies, waits for them, and re-layouts  3.66 us (6%)
  between operations  1.41 us (2%)
    ppermute x10, waiting for transfers between devices, swap(): return lax.ppermute(x, 'visit', [(i, i ^ bit) for i in range(axis_size)])  22.8 us
    ppermute x10, starting transfers between devices, swap(): return lax.ppermute(x, 'visit', [(i, i ^ bit) for i in range(axis_size)])  14 us
    pallas_call x1, Pallas kernels, shards(): pl.pallas_call(functools.partial(match_kernel, peers, bases, most, steps)...  8.44 us
    unnamed x16, local copies, waits for them, and re-layouts  3.66 us
    pallas_call x1, Pallas kernels, shards(): pl.pallas_call(functools.partial(warp_kernel, peers, bases), out_shape=[h...  3.33 us
    pallas_call x1, Pallas kernels, shards(): pl.pallas_call(gauss_kernel, out_shape=[jax.ShapeDtypeStruct((table_size,...  1.25 us
  transfers between devices with their start and end apart: 10, of which 8 were waited for; matrix products, arithmetic and copies ran while one was open for 0% of the time, Pallas kernels for 3%

profile of v4, /device:TPU:0, one launch (start us, length us, event | category | flops | bytes accessed | tf_op | source)
XLA Modules:
  0.0 56.7 jit_solution(4430368841048561994)
XLA Ops:
  1.3 0.6 %copy-done.5 = s32[1,128,1]{1,2,0:T(1,128)S(1)} copy-done((s32[1,128,1]{1,2,0:T(1,128)S(1)}, s32[1,128,1]{1,2,0:T(1,128)}, u32[]{:S(2)}) %copy-start.5) | copy-done | bytes 536
  2.0 0.7 %copy-done.6 = s32[1,128]{1,0:T(1,128)S(1)} copy-done((s32[1,128]{1,0:T(1,128)S(1)}, s32[1,128]{1,0:T(1,128)}, u32[]{:S(2)}) %copy-start.6) | copy-done | bytes 536
  2.6 0.7 %copy-done.7 = s32[1,6]{1,0:T(1,128)S(1)} copy-done((s32[1,6]{1,0:T(1,128)S(1)}, s32[1,6]{1,0:T(1,128)}, u32[]{:S(2)}) %copy-start.7) | copy-done | bytes 48
  3.3 0.7 %copy-done.2 = f32[1,6]{1,0:T(1,128)S(1)} copy-done((f32[1,6]{1,0:T(1,128)S(1)}, f32[1,6]{1,0:T(1,128)}, u32[]{:S(2)}) %copy-start.2) | copy-done | bytes 48
  3.9 0.0 copy-done.3
  4.0 0.1 pad_add_fusion.packed.scalars
  4.0 1.0 %copy-done = bf16[1,256,1024]{2,1,0:T(8,128)(2,1)S(1)} copy-done((bf16[1,256,1024]{2,1,0:T(8,128)(2,1)S(1)}, bf16[1,256,1024]{2,1,0:T(8,128)(2,1)}, u32[]{:S(2)}) %copy-start) | copy-done | bytes 524312
  5.1 3.3 %warp.1 = (bf16[2304,128]{1,0:T(8,128)(2,1)S(1)}, bf16[2304,128]{1,0:T(8,128)(2,1)S(1)}) custom-call(bf16[256,1024]{1,0:T(8,128)(2,1)S(1)} %bitcast.8, f32[8,128]{1,0:T(8,128)S(1)} %pad_add_fusion.packed.scalars, f32[8,128]{1,0:T(8,128)S(1)} %pad_add_fusion.packed.scalars, s32[1]{0:T(128)} %bitcast.me_ref), custom_call_target="tpu_custom_call" | custom-call | tf_op jit(solution)/shard_map/warp/pallas_call | solution.py:438
  8.4 0.5 collective-permute-start
  9.0 1.6 %collective-permute-done.theirs = bf16[2304,128]{1,0:T(8,128)(2,1)S(1)} collective-permute-done((bf16[2304,128]{1,0:T(8,128)(2,1)S(1)}, bf16[2304,128]{1,0:T(8,128)(2,1)S(1)}, u32[]{:S(2)}, u32[]{:S(2)}) %collective-permute-start) | collective-permute-done | bytes 589856 | tf_op jit(solution)/shard_map/ppermute | solution.py:187
  10.6 0.1 add_parts.2
  10.7 2.9 %collective-permute-start.1 = (bf16[1152,128]{1,0:T(8,128)(2,1)S(1)}, bf16[1152,128]{1,0:T(8,128)(2,1)S(1)}, u32[]{:S(2)}, u32[]{:S(2)}) collective-permute-start(bf16[1152,128]{1,0:T(8,128)(2,1)S(1)} %get-tuple-element.21), channel_id=1, source_target_pairs={{0,2},{1,3},{2,0},{3,1},{4,6},{5,7},{6,4},{7,5},{8,10},{9,11},{10,... | collective-permute-start | bytes 884744 | tf_op jit(solution)/shard_map/ppermute | solution.py:187
  13.7 7.3 %collective-permute-done.1.theirs = bf16[1152,128]{1,0:T(8,128)(2,1)S(1)} collective-permute-done((bf16[1152,128]{1,0:T(8,128)(2,1)S(1)}, bf16[1152,128]{1,0:T(8,128)(2,1)S(1)}, u32[]{:S(2)}, u32[]{:S(2)}) %collective-permute-start.1) | collective-permute-done | bytes 294944 | tf_op jit(solution)/shard_map/ppermute | solution.py:187
  21.0 0.1 add_parts.3
  21.1 3.9 %collective-permute-start.2 = (bf16[288,128]{1,0:T(8,128)(2,1)S(1)}, bf16[288,128]{1,0:T(8,128)(2,1)S(1)}, u32[]{:S(2)}, u32[]{:S(2)}) collective-permute-start(bf16[288,128]{1,0:T(8,128)(2,1)S(1)} %get-tuple-element.23), channel_id=1, source_target_pairs={{0,12},{1,13},{2,14},{3,15},{4,8},{5,9},{6,10},{7,11},{8,4},{9,5},... | collective-permute-start | bytes 221192 | tf_op jit(solution)/shard_map/ppermute | solution.py:187
  24.9 0.6 %collective-permute-start.4 = (bf16[288,128]{1,0:T(8,128)(2,1)S(1)}, bf16[288,128]{1,0:T(8,128)(2,1)S(1)}, u32[]{:S(2)}, u32[]{:S(2)}) collective-permute-start(bf16[288,128]{1,0:T(8,128)(2,1)S(1)} %get-tuple-element.25), channel_id=1, source_target_pairs={{0,4},{1,5},{2,6},{3,7},{4,0},{5,1},{6,2},{7,3},{8,12},{9,13},{10,... | collective-permute-start | bytes 221192 | tf_op jit(solution)/shard_map/ppermute | solution.py:187
  25.6 2.6 %collective-permute-done.2.refs_1_ = bf16[288,128]{1,0:T(8,128)(2,1)S(1)} collective-permute-done((bf16[288,128]{1,0:T(8,128)(2,1)S(1)}, bf16[288,128]{1,0:T(8,128)(2,1)S(1)}, u32[]{:S(2)}, u32[]{:S(2)}) %collective-permute-start.2) | collective-permute-done | bytes 73760 | tf_op jit(solution)/shard_map/ppermute | solution.py:187
  28.1 2.6 %collective-permute-done.3.refs_2_ = bf16[288,128]{1,0:T(8,128)(2,1)S(1)} collective-permute-done((bf16[288,128]{1,0:T(8,128)(2,1)S(1)}, bf16[288,128]{1,0:T(8,128)(2,1)S(1)}, u32[]{:S(2)}, u32[]{:S(2)}) %collective-permute-start.3) | collective-permute-done | bytes 73760 | tf_op jit(solution)/shard_map/ppermute | solution.py:187
  30.7 0.1 collective-permute-done.4.refs_3_
  30.8 0.9 %template.1 = (bf16[256,128]{1,0:T(8,128)(2,1)}, bf16[256,128]{1,0:T(8,128)(2,1)S(1)}, f32[256,128]{1,0:T(8,128)S(1)}, f32[16,128]{1,0:T(8,128)S(1)}) custom-call(s32[1]{0:T(128)} %bitcast.me_ref, bf16[288,128]{1,0:T(8,128)(2,1)S(1)} %get-tuple-element.22.refs_0_, bf16[288,128]{1,0:T(8,128)(2,1)S(1)} %collective-permute-done.2.refs_1_, ...), custom_call_target="tpu_custom_call" | custom-call | tf_op jit(solution)/shard_map/template/pallas_call | solution.py:468
  31.7 2.6 %collective-permute-start.7 = (bf16[256,128]{1,0:T(8,128)(2,1)S(1)}, bf16[256,128]{1,0:T(8,128)(2,1)S(1)}, u32[]{:S(2)}, u32[]{:S(2)}) collective-permute-start(bf16[256,128]{1,0:T(8,128)(2,1)S(1)} %get-tuple-element.27.refs_0_), channel_id=1, source_target_pairs={{0,12},{1,13},{2,14},{3,15},{4,8},{5,9},{6,10},{7,11},{8,4},{9,5},... | collective-permute-start | bytes 196616 | tf_op jit(solution)/shard_map/ppermute | solution.py:187
  34.2 1.8 %collective-permute-start.5 = (bf16[256,128]{1,0:T(8,128)(2,1)S(1)}, bf16[256,128]{1,0:T(8,128)(2,1)S(1)}, u32[]{:S(2)}, u32[]{:S(2)}) collective-permute-start(bf16[256,128]{1,0:T(8,128)(2,1)S(1)} %get-tuple-element.27.refs_0_), channel_id=1, source_target_pairs={{0,4},{1,5},{2,6},{3,7},{4,0},{5,1},{6,2},{7,3},{8,12},{9,13},{10,... | collective-permute-start | bytes 196616 | tf_op jit(solution)/shard_map/ppermute | solution.py:187
  36.0 2.4 %collective-permute-done.7.refs_3_ = bf16[256,128]{1,0:T(8,128)(2,1)S(1)} collective-permute-done((bf16[256,128]{1,0:T(8,128)(2,1)S(1)}, bf16[256,128]{1,0:T(8,128)(2,1)S(1)}, u32[]{:S(2)}, u32[]{:S(2)}) %collective-permute-start.7) | collective-permute-done | bytes 65568 | tf_op jit(solution)/shard_map/ppermute | solution.py:187
  38.4 1.3 %collective-permute-done.6.refs_2_ = bf16[256,128]{1,0:T(8,128)(2,1)S(1)} collective-permute-done((bf16[256,128]{1,0:T(8,128)(2,1)S(1)}, bf16[256,128]{1,0:T(8,128)(2,1)S(1)}, u32[]{:S(2)}, u32[]{:S(2)}) %collective-permute-start.6) | collective-permute-done | bytes 65568 | tf_op jit(solution)/shard_map/ppermute | solution.py:187
  39.8 0.0 copy-start.1
  39.8 1.5 %collective-permute-start.8 = (bf16[1024,128]{1,0:T(8,128)(2,1)S(1)}, bf16[1024,128]{1,0:T(8,128)(2,1)S(1)}, u32[]{:S(2)}, u32[]{:S(2)}) collective-permute-start(bf16[1024,128]{1,0:T(8,128)(2,1)S(1)} %join.2.refs_0_), channel_id=1, source_target_pairs={{0,2},{1,3},{2,0},{3,1},{4,6},{5,7},{6,4},{7,5},{8,10},{9,11},{10,... | collective-permute-start | bytes 786440 | tf_op jit(solution)/shard_map/ppermute | solution.py:187
  41.3 4.9 %collective-permute-done.8.refs_1_ = bf16[1024,128]{1,0:T(8,128)(2,1)S(1)} collective-permute-done((bf16[1024,128]{1,0:T(8,128)(2,1)S(1)}, bf16[1024,128]{1,0:T(8,128)(2,1)S(1)}, u32[]{:S(2)}, u32[]{:S(2)}) %collective-permute-start.8) | collective-permute-done | bytes 262176 | tf_op jit(solution)/shard_map/ppermute | solution.py:187
  46.3 0.1 collective-permute-start.9
  46.4 1.3 %gauss_bands.1 = (bf16[12,256,128]{2,1,0:T(8,128)(2,1)S(1)}, bf16[12,128,256]{2,1,0:T(8,128)(2,1)S(1)}) custom-call(f32[12]{0:T(128)S(1)} %copy-done.1), custom_call_target="tpu_custom_call" | custom-call | tf_op jit(solution)/shard_map/gauss_bands/pallas_call | solution.py:454
  47.6 0.6 %plan.1 = (s32[32,128]{1,0:T(8,128)S(1)}, f32[16,128]{1,0:T(8,128)S(1)}) custom-call(s32[1]{0:T(128)} %bitcast.me_ref, bf16[288,128]{1,0:T(8,128)(2,1)S(1)} %get-tuple-element.22.refs_0_, bf16[288,128]{1,0:T(8,128)(2,1)S(1)} %collective-permute-done.2.refs_1_, bf16[288,128]{1,0:T(8,128)(2,1)S(1)} %collective-permute-done.3.refs_2_, ...), custom_call_target="tpu_custom_call" | custom-call | tf_op jit(solution)/shard_map/plan/pallas_call | solution.py:482
  48.2 0.0 collective-permute-done.9.other
  48.3 8.4 %match.1 = f32[256,128]{1,0:T(8,128)} custom-call(bf16[2048,128]{1,0:T(8,128)(2,1)S(1)} %join.3.near, bf16[2048,128]{1,0:T(8,128)(2,1)S(1)} %collective-permute-done.9.other, bf16[12,256,128]{2,1,0:T(8,128)(2,1)S(1)} %get-tuple-element.28.across_bands, bf16[12,128,256]{2,1,0:T(8,128)(2,1)S(1)} %get-tuple-element.29.down_bands, ...), custom_call_target="tpu_custom_call" | custom-call | tf_op jit(solution)/shard_map/match/pallas_call | solution.py:496
  (18 shorter events, 0.1 us)
Async XLA Ops:
  0.6 0.7 %copy-start.4 = (s32[1,2]{1,0:T(1,128)S(1)}, s32[1,2]{1,0:T(1,128)}, u32[]{:S(2)}) copy-start(s32[1,2]{1,0:T(1,128)} %param.10) | copy-start | bytes 28
  1.3 0.7 %copy-start.5 = (s32[1,128,1]{1,2,0:T(1,128)S(1)}, s32[1,128,1]{1,2,0:T(1,128)}, u32[]{:S(2)}) copy-start(s32[1,128,1]{1,2,0:T(1,128)} %param.13) | copy-start | bytes 1540
  2.0 0.7 %copy-start.6 = (s32[1,128]{1,0:T(1,128)S(1)}, s32[1,128]{1,0:T(1,128)}, u32[]{:S(2)}) copy-start(s32[1,128]{1,0:T(1,128)} %param.14) | copy-start | bytes 1540
  2.6 0.7 %copy-start.7 = (s32[1,6]{1,0:T(1,128)S(1)}, s32[1,6]{1,0:T(1,128)}, u32[]{:S(2)}) copy-start(s32[1,6]{1,0:T(1,128)} %param.15) | copy-start | bytes 76
  3.3 0.7 %copy-start.2 = (f32[1,6]{1,0:T(1,128)S(1)}, f32[1,6]{1,0:T(1,128)}, u32[]{:S(2)}) copy-start(f32[1,6]{1,0:T(1,128)} %param.16) | copy-start | bytes 76
  3.3 0.7 %copy-start.3 = (f32[1,2]{1,0:T(1,128)S(1)}, f32[1,2]{1,0:T(1,128)}, u32[]{:S(2)}) copy-start(f32[1,2]{1,0:T(1,128)} %param.11) | copy-start | bytes 28
  4.0 1.0 %copy-start = (bf16[1,256,1024]{2,1,0:T(8,128)(2,1)S(1)}, bf16[1,256,1024]{2,1,0:T(8,128)(2,1)}, u32[]{:S(2)}) copy-start(bf16[1,256,1024]{2,1,0:T(8,128)(2,1)} %param.9) | copy-start | bytes 1572868
  8.4 2.2 %collective-permute-start = (bf16[2304,128]{1,0:T(8,128)(2,1)S(1)}, bf16[2304,128]{1,0:T(8,128)(2,1)S(1)}, u32[]{:S(2)}, u32[]{:S(2)}) collective-permute-start(bf16[2304,128]{1,0:T(8,128)(2,1)S(1)} %get-tuple-element.19), channel_id=1, source_target_pairs={{0,1},{1,0},{2,3},{3,2},{4,5},{5,4},{6,7},{7,6},{8,9},{9,8},{10,11... | collective-permute-start | bytes 1769480 | tf_op jit(solution)/shard_map/ppermute | solution.py:187
  10.7 10.3 %collective-permute-start.1 = (bf16[1152,128]{1,0:T(8,128)(2,1)S(1)}, bf16[1152,128]{1,0:T(8,128)(2,1)S(1)}, u32[]{:S(2)}, u32[]{:S(2)}) collective-permute-start(bf16[1152,128]{1,0:T(8,128)(2,1)S(1)} %get-tuple-element.21), channel_id=1, source_target_pairs={{0,2},{1,3},{2,0},{3,1},{4,6},{5,7},{6,4},{7,5},{8,10},{9,11},{10,... | collective-permute-start | bytes 884744 | tf_op jit(solution)/shard_map/ppermute | solution.py:187
  21.1 7.1 %collective-permute-start.2 = (bf16[288,128]{1,0:T(8,128)(2,1)S(1)}, bf16[288,128]{1,0:T(8,128)(2,1)S(1)}, u32[]{:S(2)}, u32[]{:S(2)}) collective-permute-start(bf16[288,128]{1,0:T(8,128)(2,1)S(1)} %get-tuple-element.23), channel_id=1, source_target_pairs={{0,12},{1,13},{2,14},{3,15},{4,8},{5,9},{6,10},{7,11},{8,4},{9,5},... | collective-permute-start | bytes 221192 | tf_op jit(solution)/shard_map/ppermute | solution.py:187
  24.9 5.8 %collective-permute-start.3 = (bf16[288,128]{1,0:T(8,128)(2,1)S(1)}, bf16[288,128]{1,0:T(8,128)(2,1)S(1)}, u32[]{:S(2)}, u32[]{:S(2)}) collective-permute-start(bf16[288,128]{1,0:T(8,128)(2,1)S(1)} %get-tuple-element.24), channel_id=1, source_target_pairs={{0,8},{1,9},{2,10},{3,11},{4,12},{5,13},{6,14},{7,15},{8,0},{9,1},... | collective-permute-start | bytes 221192 | tf_op jit(solution)/shard_map/ppermute | solution.py:187
  24.9 5.8 %collective-permute-start.4 = (bf16[288,128]{1,0:T(8,128)(2,1)S(1)}, bf16[288,128]{1,0:T(8,128)(2,1)S(1)}, u32[]{:S(2)}, u32[]{:S(2)}) collective-permute-start(bf16[288,128]{1,0:T(8,128)(2,1)S(1)} %get-tuple-element.25), channel_id=1, source_target_pairs={{0,4},{1,5},{2,6},{3,7},{4,0},{5,1},{6,2},{7,3},{8,12},{9,13},{10,... | collective-permute-start | bytes 221192 | tf_op jit(solution)/shard_map/ppermute | solution.py:187
  31.7 6.8 %collective-permute-start.7 = (bf16[256,128]{1,0:T(8,128)(2,1)S(1)}, bf16[256,128]{1,0:T(8,128)(2,1)S(1)}, u32[]{:S(2)}, u32[]{:S(2)}) collective-permute-start(bf16[256,128]{1,0:T(8,128)(2,1)S(1)} %get-tuple-element.27.refs_0_), channel_id=1, source_target_pairs={{0,12},{1,13},{2,14},{3,15},{4,8},{5,9},{6,10},{7,11},{8,4},{9,5},... | collective-permute-start | bytes 196616 | tf_op jit(solution)/shard_map/ppermute | solution.py:187
  34.2 5.5 %collective-permute-start.6 = (bf16[256,128]{1,0:T(8,128)(2,1)S(1)}, bf16[256,128]{1,0:T(8,128)(2,1)S(1)}, u32[]{:S(2)}, u32[]{:S(2)}) collective-permute-start(bf16[256,128]{1,0:T(8,128)(2,1)S(1)} %get-tuple-element.27.refs_0_), channel_id=1, source_target_pairs={{0,8},{1,9},{2,10},{3,11},{4,12},{5,13},{6,14},{7,15},{8,0},{9,1},... | collective-permute-start | bytes 196616 | tf_op jit(solution)/shard_map/ppermute | solution.py:187
  34.2 5.5 %collective-permute-start.5 = (bf16[256,128]{1,0:T(8,128)(2,1)S(1)}, bf16[256,128]{1,0:T(8,128)(2,1)S(1)}, u32[]{:S(2)}, u32[]{:S(2)}) collective-permute-start(bf16[256,128]{1,0:T(8,128)(2,1)S(1)} %get-tuple-element.27.refs_0_), channel_id=1, source_target_pairs={{0,4},{1,5},{2,6},{3,7},{4,0},{5,1},{6,2},{7,3},{8,12},{9,13},{10,... | collective-permute-start | bytes 196616 | tf_op jit(solution)/shard_map/ppermute | solution.py:187
  39.8 6.6 %copy-start.1 = (f32[12]{0:T(128)S(1)}, f32[12]{0:T(128)}, u32[]{:S(2)}) copy-start(f32[12]{0:T(128)} %basis_width.1) | copy-start | bytes 148
  39.8 6.4 %collective-permute-start.8 = (bf16[1024,128]{1,0:T(8,128)(2,1)S(1)}, bf16[1024,128]{1,0:T(8,128)(2,1)S(1)}, u32[]{:S(2)}, u32[]{:S(2)}) collective-permute-start(bf16[1024,128]{1,0:T(8,128)(2,1)S(1)} %join.2.refs_0_), channel_id=1, source_target_pairs={{0,2},{1,3},{2,0},{3,1},{4,6},{5,7},{6,4},{7,5},{8,10},{9,11},{10,... | collective-permute-start | bytes 786440 | tf_op jit(solution)/shard_map/ppermute | solution.py:187
  46.3 2.0 %collective-permute-start.9 = (bf16[2048,128]{1,0:T(8,128)(2,1)S(1)}, bf16[2048,128]{1,0:T(8,128)(2,1)S(1)}, u32[]{:S(2)}, u32[]{:S(2)}) collective-permute-start(bf16[2048,128]{1,0:T(8,128)(2,1)S(1)} %join.3.near), channel_id=1, source_target_pairs={{0,1},{1,0},{2,3},{3,2},{4,5},{5,4},{6,7},{7,6},{8,9},{9,8},{10,11... | collective-permute-start | bytes 1572872 | tf_op jit(solution)/shard_map/ppermute | solution.py:187

commit v5 on v4

--- a/solution.py
+++ b/solution.py
@@ -21,6 +21,7 @@
 
 VMEM = pl.BlockSpec(memory_space=pltpu.VMEM)
 SMEM = pl.BlockSpec(memory_space=pltpu.SMEM)
+ANY = pl.BlockSpec(memory_space=pl.ANY)
 
 
 def params():
@@ -68,83 +69,89 @@
     return band.astype(jnp.bfloat16)
 
 
-OWNER, SLOT, MISC = 0, 1, 2
-OFFSET, FRACTION, WEIGHT, BASES = 0, 2, 4, 5
-
-
-def pack(owner, slot, band_offset, shift_frac, weight, basis_index, basis_coef):
-    def put(x, row, lane):
-        x = x.astype(jnp.float32).reshape(1, -1)
-        return jnp.pad(x, ((row, 7 - row), (lane, BW - lane - x.shape[1])))
-
-    bases = basis_index.shape[1]
-    return (
-        put(owner, OWNER, 0)
-        + put(slot, SLOT, 0)
-        + put(band_offset, MISC, OFFSET)
-        + put(shift_frac, MISC, FRACTION)
-        + put(weight, MISC, WEIGHT)
-        + put(basis_index, MISC, BASES)
-        + put(basis_coef, MISC, BASES + bases)
-    )
-
-
-def warp_kernel(peers, bases, picture, packed, scalars, me_ref, keep, send, total, wide_band, spots, starts, sem):
+def warp_kernel(
+    peers,
+    bases,
+    me_ref,
+    picture_in,
+    owner_in,
+    slot_in,
+    offset_in,
+    fraction_in,
+    weight_in,
+    index_in,
+    coef_in,
+    keep,
+    send,
+    picture,
+    owner,
+    slot,
+    offset,
+    fraction,
+    weight,
+    index,
+    coef,
+    total,
+    wide_band,
+    spots,
+    starts,
+    sems,
+):
     rows, width = picture.shape
     me = me_ref[0]
     chunk = chunk_rows(peers)
-    half = peers // 2 * chunk
-    named = packed[OWNER : OWNER + 1, :].astype(jnp.int32)
-    slots = packed[SLOT : SLOT + 1, :].astype(jnp.int32)
-    spots[...] = (place(named, me, peers) * PS + slots) * BH
-    copy = pltpu.make_async_copy(spots, starts, sem)
-    copy.start()
+    sources = (owner_in, slot_in, offset_in, fraction_in, weight_in, index_in, coef_in, picture_in)
+    targets = (owner, slot, offset, fraction, weight, index, coef, picture)
+    copies = [pltpu.make_async_copy(x, y, sems.at[i]) for i, (x, y) in enumerate(zip(sources, targets))]
+    for copy in copies:
+        copy.start()
     total[...] = jnp.zeros_like(total)
-
-    heavy = packed[MISC : MISC + 1, WEIGHT : WEIGHT + 1]
-    mean = jnp.sum(jnp.sum(picture[...].astype(jnp.float32), axis=0, keepdims=True), axis=1, keepdims=True)
-    mean = (mean * (1.0 / (rows * width))).astype(jnp.bfloat16).astype(jnp.float32)
-
-    if name_tiles(peers) == 1:
-        names = [packed[OWNER : OWNER + 1, :] * PS + packed[SLOT : SLOT + 1, :]]
-    else:
-        names = [packed[OWNER : OWNER + 1, :], packed[SLOT : SLOT + 1, :]]
-    misc = packed[MISC : MISC + 1, :]
-    lane = lax.broadcasted_iota(jnp.int32, (1, BW), 1)
-
-    def lanes(x, first, count, to):
-        moved = turned(jnp.broadcast_to(x, (8, BW)), to - first)[0:1]
-        return jnp.where((lane >= to) & (lane < to + count), moved, 0.0)
-
-    high = misc.astype(jnp.bfloat16).astype(jnp.float32)
-    middle = (misc - high).astype(jnp.bfloat16).astype(jnp.float32)
-    low = misc - high - middle
-    numbers = lanes(misc, BASES, bases, 0)
-    for i, piece in enumerate((high, middle, low)):
-        numbers = numbers + lanes(piece, BASES + bases, bases, (1 + i) * bases)
-    numbers = numbers + jnp.where(lane == 4 * bases, heavy, 0.0) + jnp.where(lane == 4 * bases + 1, mean, 0.0)
-    row = lax.broadcasted_iota(jnp.int32, (peers, BW), 0)
-    tags = jnp.concatenate(
-        [jnp.where(row == me, x, 0.0).astype(jnp.bfloat16) for x in (*names, numbers)], axis=0
-    )
+    for copy in copies[:-1]:
+        copy.wait()
+    spots[...] = (place(owner[...], me, peers) * PS + slot[...]) * BH
+    turn_in = pltpu.make_async_copy(spots, starts, sems.at[len(copies)])
+    turn_in.start()
 
     gap = (
         lax.broadcasted_iota(jnp.int32, (WIDE + 2 * SIDE, WIDE), 0)
         - lax.broadcasted_iota(jnp.int32, (WIDE + 2 * SIDE, WIDE), 1)
         - SIDE
     ).astype(jnp.float32)
-    wide_band[...] = lanczos_taps(gap, scalars[MISC, OFFSET + 1], scalars[MISC, FRACTION + 1])
+    wide_band[...] = lanczos_taps(gap, offset[0, 1].astype(jnp.float32), fraction[0, 1])
     gap = (
         lax.broadcasted_iota(jnp.int32, (rows, rows), 1) - lax.broadcasted_iota(jnp.int32, (rows, rows), 0)
     ).astype(jnp.float32)
-    row_warp = lanczos_taps(gap, scalars[MISC, OFFSET], scalars[MISC, FRACTION])
+    row_warp = lanczos_taps(gap, offset[0, 0].astype(jnp.float32), fraction[0, 0])
+    heavy = weight[...].astype(jnp.float32)
+    named, slotted = owner[...].astype(jnp.float32), slot[...].astype(jnp.float32)
+    names = [named * PS + slotted] if name_tiles(peers) == 1 else [named, slotted]
+    lane = lax.broadcasted_iota(jnp.int32, (8, BW), 1)
+    numbers = jnp.zeros((8, BW), jnp.float32)
+    share = jnp.zeros((8, BW), jnp.float32)
+    for k in range(bases):
+        numbers = jnp.where(lane == k, index[0, k].astype(jnp.float32), numbers)
+        share = jnp.where(lane == k, coef[0, k], share)
+    for i in range(1, 4):
+        piece = share.astype(jnp.bfloat16).astype(jnp.float32)
+        share = share - piece
+        numbers = numbers + turned(piece, i * bases)
+    numbers = jnp.where(lane == 4 * bases, heavy, numbers)
+
+    copies[-1].wait()
+    mean = jnp.sum(jnp.sum(picture[...].astype(jnp.float32), axis=0, keepdims=True), axis=1, keepdims=True)
+    mean = (mean * (1.0 / (rows * width))).astype(jnp.bfloat16).astype(jnp.float32)
+    numbers = jnp.where(lane == 4 * bases + 1, mean, numbers)[0:1]
+    row = lax.broadcasted_iota(jnp.int32, (peers, BW), 0)
+    tags = jnp.concatenate(
+        [jnp.where(row == me, x, 0.0).astype(jnp.bfloat16) for x in (*names, numbers)], axis=0
+    )
     passes = [
         jnp.dot(
             picture[:, low:high], wide_band[top:bottom, :], preferred_element_type=jnp.float32
         ).astype(jnp.bfloat16)
         for low, high, top, bottom in windows(width)
     ]
-    copy.wait()
+    turn_in.wait()
     across = WIDE // BW
     for block, col_pass in enumerate(passes):
         done = jnp.dot(row_warp, col_pass, preferred_element_type=jnp.float32).astype(jnp.bfloat16)
@@ -432,24 +439,42 @@
     most = max(2, 2 * box_slot.shape[1] // peers)
     me = lax.axis_index("visit").astype(jnp.int32).reshape(1)
     chunk = chunk_rows(peers)
-    packed = pack(box_owner, box_slot, band_offset, shift_frac, weights, basis_index, basis_coef)
+    owner = box_owner.reshape(1, -1)
 
     half = jax.ShapeDtypeStruct((peers // 2 * chunk, BW), jnp.bfloat16)
     keep, send = pl.pallas_call(
         functools.partial(warp_kernel, peers, bases),
         out_shape=[half, half],
-        in_specs=[VMEM, VMEM, SMEM, SMEM],
+        in_specs=[SMEM] + [ANY] * 8,
         out_specs=[VMEM] * 2,
         scratch_shapes=[
+            pltpu.VMEM((rows, width), jnp.bfloat16),
+            pltpu.VMEM(owner.shape, jnp.int32),
+            pltpu.VMEM(box_slot.shape, jnp.int32),
+            pltpu.SMEM(band_offset.shape, jnp.int32),
+            pltpu.SMEM(shift_frac.shape, jnp.float32),
+            pltpu.VMEM((1, 1), jnp.bfloat16),
+            pltpu.SMEM(basis_index.shape, jnp.int32),
+            pltpu.SMEM(basis_coef.shape, jnp.float32),
             pltpu.VMEM((peers * BOXES, BW), jnp.float32),
             pltpu.VMEM((WIDE + 2 * SIDE, WIDE), jnp.bfloat16),
             pltpu.VMEM((1, BW), jnp.int32),
             pltpu.SMEM((1, BW), jnp.int32),
-            pltpu.SemaphoreType.DMA,
+            pltpu.SemaphoreType.DMA((9,)),
         ],
-        compiler_params=params(),
+        compiler_params=pltpu.CompilerParams(vmem_limit_bytes=48 * 1024 * 1024),
         name="warp",
-    )(visit_image[0], packed, packed, me)
+    )(
+        me,
+        visit_image[0],
+        owner,
+        box_slot,
+        band_offset,
+        shift_frac,
+        weights.reshape(1, 1),
+        basis_index,
+        basis_coef,
+    )
 
     across_bands, down_bands = pl.pallas_call(
         gauss_kernel,

time: 56.9 us -> 54.6 us (0.960)
  local copies, waits for them, and re-layouts: 3.66 us -> 1.73 us
    unnamed x16, local copies, waits for them, and re-layouts: 3.66 us -> 1.73 us
where the time goes in v5:
time: 54.6 us; the launch traced here: 54.5 us
  waiting for transfers between devices  22.8 us (42%)
  Pallas kernels  14.6 us (27%)
  starting transfers between devices  14 us (26%)
  local copies, waits for them, and re-layouts  1.73 us (3%)
  between operations  1.41 us (3%)
    ppermute x10, waiting for transfers between devices, swap(): return lax.ppermute(x, 'visit', [(i, i ^ bit) for i in range(axis_size)])  22.8 us
    ppermute x10, starting transfers between devices, swap(): return lax.ppermute(x, 'visit', [(i, i ^ bit) for i in range(axis_size)])  14 us
    pallas_call x1, Pallas kernels, shards(): pl.pallas_call(functools.partial(match_kernel, peers, bases, most, steps)...  8.44 us
    pallas_call x1, Pallas kernels, shards(): pl.pallas_call(functools.partial(warp_kernel, peers, bases), out_shape=[h...  3.2 us
    unnamed x16, local copies, waits for them, and re-layouts  1.73 us
    pallas_call x1, Pallas kernels, shards(): pl.pallas_call(gauss_kernel, out_shape=[jax.ShapeDtypeStruct((table_size,...  1.25 us
  transfers between devices with their start and end apart: 10, of which 8 were waited for; matrix products, arithmetic and copies ran while one was open for 0% of the time, Pallas kernels for 3%

profile of v5, /device:TPU:0, one launch (start us, length us, event | category | flops | bytes accessed | tf_op | source)
XLA Modules:
  0.0 54.5 jit_solution(7597253095766362079)
XLA Ops:
  1.3 0.6 %copy-done.4 = f32[1,2]{1,0:T(1,128)S(1)} copy-done((f32[1,2]{1,0:T(1,128)S(1)}, f32[1,2]{1,0:T(1,128)}, u32[]{:S(2)}) %copy-start.4) | copy-done | bytes 32
  1.9 0.0 copy-done.5
  2.0 0.0 copy-done.6
  2.0 0.0 copy-done.1
  2.0 0.0 copy-done.2
  2.0 0.0 copy-done.3
  2.0 1.0 %copy-done = bf16[1,256,1024]{2,1,0:T(8,128)(2,1)S(1)} copy-done((bf16[1,256,1024]{2,1,0:T(8,128)(2,1)S(1)}, bf16[1,256,1024]{2,1,0:T(8,128)(2,1)}, u32[]{:S(2)}) %copy-start) | copy-done | bytes 524312
  3.1 3.2 %warp.1 = (bf16[2304,128]{1,0:T(8,128)(2,1)S(1)}, bf16[2304,128]{1,0:T(8,128)(2,1)S(1)}) custom-call(s32[1]{0:T(128)} %bitcast.me_ref, bf16[256,1024]{1,0:T(8,128)(2,1)S(1)} %bitcast.7, s32[1,128]{1,0:T(1,128)S(1)} %bitcast.8, s32[1,128]{1,0:T(1,128)S(1)} %copy-done.2, s32[1,2]{1,0:T(1,128)S(1)} %copy-done.3, f32[1,2]{1,0:T(1,128)S(1)} %copy-done.4, ...), custom_call_target="tpu_custom_call" | custom-call | tf_op jit(solution)/shard_map/warp/pallas_call | solution.py:445
  6.3 0.5 collective-permute-start
  6.8 1.6 %collective-permute-done.theirs = bf16[2304,128]{1,0:T(8,128)(2,1)S(1)} collective-permute-done((bf16[2304,128]{1,0:T(8,128)(2,1)S(1)}, bf16[2304,128]{1,0:T(8,128)(2,1)S(1)}, u32[]{:S(2)}, u32[]{:S(2)}) %collective-permute-start) | collective-permute-done | bytes 589856 | tf_op jit(solution)/shard_map/ppermute | solution.py:194
  8.4 0.1 add_parts.2
  8.6 3.0 %collective-permute-start.1 = (bf16[1152,128]{1,0:T(8,128)(2,1)S(1)}, bf16[1152,128]{1,0:T(8,128)(2,1)S(1)}, u32[]{:S(2)}, u32[]{:S(2)}) collective-permute-start(bf16[1152,128]{1,0:T(8,128)(2,1)S(1)} %get-tuple-element.21), channel_id=1, source_target_pairs={{0,2},{1,3},{2,0},{3,1},{4,6},{5,7},{6,4},{7,5},{8,10},{9,11},{10,... | collective-permute-start | bytes 884744 | tf_op jit(solution)/shard_map/ppermute | solution.py:194
  11.5 7.3 %collective-permute-done.1.theirs = bf16[1152,128]{1,0:T(8,128)(2,1)S(1)} collective-permute-done((bf16[1152,128]{1,0:T(8,128)(2,1)S(1)}, bf16[1152,128]{1,0:T(8,128)(2,1)S(1)}, u32[]{:S(2)}, u32[]{:S(2)}) %collective-permute-start.1) | collective-permute-done | bytes 294944 | tf_op jit(solution)/shard_map/ppermute | solution.py:194
  18.8 0.1 add_parts.3
  18.9 3.9 %collective-permute-start.2 = (bf16[288,128]{1,0:T(8,128)(2,1)S(1)}, bf16[288,128]{1,0:T(8,128)(2,1)S(1)}, u32[]{:S(2)}, u32[]{:S(2)}) collective-permute-start(bf16[288,128]{1,0:T(8,128)(2,1)S(1)} %get-tuple-element.23), channel_id=1, source_target_pairs={{0,12},{1,13},{2,14},{3,15},{4,8},{5,9},{6,10},{7,11},{8,4},{9,5},... | collective-permute-start | bytes 221192 | tf_op jit(solution)/shard_map/ppermute | solution.py:194
  22.8 0.6 %collective-permute-start.4 = (bf16[288,128]{1,0:T(8,128)(2,1)S(1)}, bf16[288,128]{1,0:T(8,128)(2,1)S(1)}, u32[]{:S(2)}, u32[]{:S(2)}) collective-permute-start(bf16[288,128]{1,0:T(8,128)(2,1)S(1)} %get-tuple-element.25), channel_id=1, source_target_pairs={{0,4},{1,5},{2,6},{3,7},{4,0},{5,1},{6,2},{7,3},{8,12},{9,13},{10,... | collective-permute-start | bytes 221192 | tf_op jit(solution)/shard_map/ppermute | solution.py:194
  23.4 2.6 %collective-permute-done.2.refs_1_ = bf16[288,128]{1,0:T(8,128)(2,1)S(1)} collective-permute-done((bf16[288,128]{1,0:T(8,128)(2,1)S(1)}, bf16[288,128]{1,0:T(8,128)(2,1)S(1)}, u32[]{:S(2)}, u32[]{:S(2)}) %collective-permute-start.2) | collective-permute-done | bytes 73760 | tf_op jit(solution)/shard_map/ppermute | solution.py:194
  26.0 2.6 %collective-permute-done.3.refs_2_ = bf16[288,128]{1,0:T(8,128)(2,1)S(1)} collective-permute-done((bf16[288,128]{1,0:T(8,128)(2,1)S(1)}, bf16[288,128]{1,0:T(8,128)(2,1)S(1)}, u32[]{:S(2)}, u32[]{:S(2)}) %collective-permute-start.3) | collective-permute-done | bytes 73760 | tf_op jit(solution)/shard_map/ppermute | solution.py:194
  28.6 0.1 collective-permute-done.4.refs_3_
  28.6 0.9 %template.1 = (bf16[256,128]{1,0:T(8,128)(2,1)}, bf16[256,128]{1,0:T(8,128)(2,1)S(1)}, f32[256,128]{1,0:T(8,128)S(1)}, f32[16,128]{1,0:T(8,128)S(1)}) custom-call(s32[1]{0:T(128)} %bitcast.me_ref, bf16[288,128]{1,0:T(8,128)(2,1)S(1)} %get-tuple-element.22.refs_0_, bf16[288,128]{1,0:T(8,128)(2,1)S(1)} %collective-permute-done.2.refs_1_, ...), custom_call_target="tpu_custom_call" | custom-call | tf_op jit(solution)/shard_map/template/pallas_call | solution.py:493
  29.5 2.6 %collective-permute-start.7 = (bf16[256,128]{1,0:T(8,128)(2,1)S(1)}, bf16[256,128]{1,0:T(8,128)(2,1)S(1)}, u32[]{:S(2)}, u32[]{:S(2)}) collective-permute-start(bf16[256,128]{1,0:T(8,128)(2,1)S(1)} %get-tuple-element.27.refs_0_), channel_id=1, source_target_pairs={{0,12},{1,13},{2,14},{3,15},{4,8},{5,9},{6,10},{7,11},{8,4},{9,5},... | collective-permute-start | bytes 196616 | tf_op jit(solution)/shard_map/ppermute | solution.py:194
  32.1 1.8 %collective-permute-start.5 = (bf16[256,128]{1,0:T(8,128)(2,1)S(1)}, bf16[256,128]{1,0:T(8,128)(2,1)S(1)}, u32[]{:S(2)}, u32[]{:S(2)}) collective-permute-start(bf16[256,128]{1,0:T(8,128)(2,1)S(1)} %get-tuple-element.27.refs_0_), channel_id=1, source_target_pairs={{0,4},{1,5},{2,6},{3,7},{4,0},{5,1},{6,2},{7,3},{8,12},{9,13},{10,... | collective-permute-start | bytes 196616 | tf_op jit(solution)/shard_map/ppermute | solution.py:194
  33.9 2.4 %collective-permute-done.7.refs_3_ = bf16[256,128]{1,0:T(8,128)(2,1)S(1)} collective-permute-done((bf16[256,128]{1,0:T(8,128)(2,1)S(1)}, bf16[256,128]{1,0:T(8,128)(2,1)S(1)}, u32[]{:S(2)}, u32[]{:S(2)}) %collective-permute-start.7) | collective-permute-done | bytes 65568 | tf_op jit(solution)/shard_map/ppermute | solution.py:194
  36.3 1.3 %collective-permute-done.6.refs_2_ = bf16[256,128]{1,0:T(8,128)(2,1)S(1)} collective-permute-done((bf16[256,128]{1,0:T(8,128)(2,1)S(1)}, bf16[256,128]{1,0:T(8,128)(2,1)S(1)}, u32[]{:S(2)}, u32[]{:S(2)}) %collective-permute-start.6) | collective-permute-done | bytes 65568 | tf_op jit(solution)/shard_map/ppermute | solution.py:194
  37.6 0.0 copy-start.7
  37.7 1.6 %collective-permute-start.8 = (bf16[1024,128]{1,0:T(8,128)(2,1)S(1)}, bf16[1024,128]{1,0:T(8,128)(2,1)S(1)}, u32[]{:S(2)}, u32[]{:S(2)}) collective-permute-start(bf16[1024,128]{1,0:T(8,128)(2,1)S(1)} %join.2.refs_0_), channel_id=1, source_target_pairs={{0,2},{1,3},{2,0},{3,1},{4,6},{5,7},{6,4},{7,5},{8,10},{9,11},{10,... | collective-permute-start | bytes 786440 | tf_op jit(solution)/shard_map/ppermute | solution.py:194
  39.2 4.9 %collective-permute-done.8.refs_1_ = bf16[1024,128]{1,0:T(8,128)(2,1)S(1)} collective-permute-done((bf16[1024,128]{1,0:T(8,128)(2,1)S(1)}, bf16[1024,128]{1,0:T(8,128)(2,1)S(1)}, u32[]{:S(2)}, u32[]{:S(2)}) %collective-permute-start.8) | collective-permute-done | bytes 262176 | tf_op jit(solution)/shard_map/ppermute | solution.py:194
  44.1 0.1 collective-permute-start.9
  44.2 1.3 %gauss_bands.1 = (bf16[12,256,128]{2,1,0:T(8,128)(2,1)S(1)}, bf16[12,128,256]{2,1,0:T(8,128)(2,1)S(1)}) custom-call(f32[12]{0:T(128)S(1)} %copy-done.7), custom_call_target="tpu_custom_call" | custom-call | tf_op jit(solution)/shard_map/gauss_bands/pallas_call | solution.py:479
  45.5 0.6 %plan.1 = (s32[32,128]{1,0:T(8,128)S(1)}, f32[16,128]{1,0:T(8,128)S(1)}) custom-call(s32[1]{0:T(128)} %bitcast.me_ref, bf16[288,128]{1,0:T(8,128)(2,1)S(1)} %get-tuple-element.22.refs_0_, bf16[288,128]{1,0:T(8,128)(2,1)S(1)} %collective-permute-done.2.refs_1_, bf16[288,128]{1,0:T(8,128)(2,1)S(1)} %collective-permute-done.3.refs_2_, ...), custom_call_target="tpu_custom_call" | custom-call | tf_op jit(solution)/shard_map/plan/pallas_call | solution.py:507
  46.1 0.0 collective-permute-done.9.other
  46.1 8.4 %match.1 = f32[256,128]{1,0:T(8,128)} custom-call(bf16[2048,128]{1,0:T(8,128)(2,1)S(1)} %join.3.near, bf16[2048,128]{1,0:T(8,128)(2,1)S(1)} %collective-permute-done.9.other, bf16[12,256,128]{2,1,0:T(8,128)(2,1)S(1)} %get-tuple-element.28.across_bands, bf16[12,128,256]{2,1,0:T(8,128)(2,1)S(1)} %get-tuple-element.29.down_bands, ...), custom_call_target="tpu_custom_call" | custom-call | tf_op jit(solution)/shard_map/match/pallas_call | solution.py:521
  (13 shorter events, 0.1 us)
Async XLA Ops:
  1.3 0.7 %copy-start.4 = (f32[1,2]{1,0:T(1,128)S(1)}, f32[1,2]{1,0:T(1,128)}, u32[]{:S(2)}) copy-start(f32[1,2]{1,0:T(1,128)} %fraction_in.1) | copy-start | bytes 28
  1.3 0.7 %copy-start.5 = (s32[1,6]{1,0:T(1,128)S(1)}, s32[1,6]{1,0:T(1,128)}, u32[]{:S(2)}) copy-start(s32[1,6]{1,0:T(1,128)} %index_in.1) | copy-start | bytes 76
  1.3 0.7 %copy-start.6 = (f32[1,6]{1,0:T(1,128)S(1)}, f32[1,6]{1,0:T(1,128)}, u32[]{:S(2)}) copy-start(f32[1,6]{1,0:T(1,128)} %coef_in.1) | copy-start | bytes 76
  1.3 0.7 %copy-start.1 = (s32[1,128,1]{1,2,0:T(1,128)S(1)}, s32[1,128,1]{1,2,0:T(1,128)}, u32[]{:S(2)}) copy-start(s32[1,128,1]{1,2,0:T(1,128)} %param.13) | copy-start | bytes 1540
  1.3 0.7 %copy-start.2 = (s32[1,128]{1,0:T(1,128)S(1)}, s32[1,128]{1,0:T(1,128)}, u32[]{:S(2)}) copy-start(s32[1,128]{1,0:T(1,128)} %slot_in.1) | copy-start | bytes 1540
  1.3 0.7 %copy-start.3 = (s32[1,2]{1,0:T(1,128)S(1)}, s32[1,2]{1,0:T(1,128)}, u32[]{:S(2)}) copy-start(s32[1,2]{1,0:T(1,128)} %offset_in.1) | copy-start | bytes 28
  2.0 1.0 %copy-start = (bf16[1,256,1024]{2,1,0:T(8,128)(2,1)S(1)}, bf16[1,256,1024]{2,1,0:T(8,128)(2,1)}, u32[]{:S(2)}) copy-start(bf16[1,256,1024]{2,1,0:T(8,128)(2,1)} %param.9) | copy-start | bytes 1572868
  6.3 2.1 %collective-permute-start = (bf16[2304,128]{1,0:T(8,128)(2,1)S(1)}, bf16[2304,128]{1,0:T(8,128)(2,1)S(1)}, u32[]{:S(2)}, u32[]{:S(2)}) collective-permute-start(bf16[2304,128]{1,0:T(8,128)(2,1)S(1)} %get-tuple-element.19), channel_id=1, source_target_pairs={{0,1},{1,0},{2,3},{3,2},{4,5},{5,4},{6,7},{7,6},{8,9},{9,8},{10,11... | collective-permute-start | bytes 1769480 | tf_op jit(solution)/shard_map/ppermute | solution.py:194
  8.6 10.3 %collective-permute-start.1 = (bf16[1152,128]{1,0:T(8,128)(2,1)S(1)}, bf16[1152,128]{1,0:T(8,128)(2,1)S(1)}, u32[]{:S(2)}, u32[]{:S(2)}) collective-permute-start(bf16[1152,128]{1,0:T(8,128)(2,1)S(1)} %get-tuple-element.21), channel_id=1, source_target_pairs={{0,2},{1,3},{2,0},{3,1},{4,6},{5,7},{6,4},{7,5},{8,10},{9,11},{10,... | collective-permute-start | bytes 884744 | tf_op jit(solution)/shard_map/ppermute | solution.py:194
  18.9 7.1 %collective-permute-start.2 = (bf16[288,128]{1,0:T(8,128)(2,1)S(1)}, bf16[288,128]{1,0:T(8,128)(2,1)S(1)}, u32[]{:S(2)}, u32[]{:S(2)}) collective-permute-start(bf16[288,128]{1,0:T(8,128)(2,1)S(1)} %get-tuple-element.23), channel_id=1, source_target_pairs={{0,12},{1,13},{2,14},{3,15},{4,8},{5,9},{6,10},{7,11},{8,4},{9,5},... | collective-permute-start | bytes 221192 | tf_op jit(solution)/shard_map/ppermute | solution.py:194
  22.8 5.8 %collective-permute-start.3 = (bf16[288,128]{1,0:T(8,128)(2,1)S(1)}, bf16[288,128]{1,0:T(8,128)(2,1)S(1)}, u32[]{:S(2)}, u32[]{:S(2)}) collective-permute-start(bf16[288,128]{1,0:T(8,128)(2,1)S(1)} %get-tuple-element.24), channel_id=1, source_target_pairs={{0,8},{1,9},{2,10},{3,11},{4,12},{5,13},{6,14},{7,15},{8,0},{9,1},... | collective-permute-start | bytes 221192 | tf_op jit(solution)/shard_map/ppermute | solution.py:194
  22.8 5.8 %collective-permute-start.4 = (bf16[288,128]{1,0:T(8,128)(2,1)S(1)}, bf16[288,128]{1,0:T(8,128)(2,1)S(1)}, u32[]{:S(2)}, u32[]{:S(2)}) collective-permute-start(bf16[288,128]{1,0:T(8,128)(2,1)S(1)} %get-tuple-element.25), channel_id=1, source_target_pairs={{0,4},{1,5},{2,6},{3,7},{4,0},{5,1},{6,2},{7,3},{8,12},{9,13},{10,... | collective-permute-start | bytes 221192 | tf_op jit(solution)/shard_map/ppermute | solution.py:194
  29.5 6.8 %collective-permute-start.7 = (bf16[256,128]{1,0:T(8,128)(2,1)S(1)}, bf16[256,128]{1,0:T(8,128)(2,1)S(1)}, u32[]{:S(2)}, u32[]{:S(2)}) collective-permute-start(bf16[256,128]{1,0:T(8,128)(2,1)S(1)} %get-tuple-element.27.refs_0_), channel_id=1, source_target_pairs={{0,12},{1,13},{2,14},{3,15},{4,8},{5,9},{6,10},{7,11},{8,4},{9,5},... | collective-permute-start | bytes 196616 | tf_op jit(solution)/shard_map/ppermute | solution.py:194
  32.1 5.5 %collective-permute-start.6 = (bf16[256,128]{1,0:T(8,128)(2,1)S(1)}, bf16[256,128]{1,0:T(8,128)(2,1)S(1)}, u32[]{:S(2)}, u32[]{:S(2)}) collective-permute-start(bf16[256,128]{1,0:T(8,128)(2,1)S(1)} %get-tuple-element.27.refs_0_), channel_id=1, source_target_pairs={{0,8},{1,9},{2,10},{3,11},{4,12},{5,13},{6,14},{7,15},{8,0},{9,1},... | collective-permute-start | bytes 196616 | tf_op jit(solution)/shard_map/ppermute | solution.py:194
  32.1 5.5 %collective-permute-start.5 = (bf16[256,128]{1,0:T(8,128)(2,1)S(1)}, bf16[256,128]{1,0:T(8,128)(2,1)S(1)}, u32[]{:S(2)}, u32[]{:S(2)}) collective-permute-start(bf16[256,128]{1,0:T(8,128)(2,1)S(1)} %get-tuple-element.27.refs_0_), channel_id=1, source_target_pairs={{0,4},{1,5},{2,6},{3,7},{4,0},{5,1},{6,2},{7,3},{8,12},{9,13},{10,... | collective-permute-start | bytes 196616 | tf_op jit(solution)/shard_map/ppermute | solution.py:194
  37.6 6.6 %copy-start.7 = (f32[12]{0:T(128)S(1)}, f32[12]{0:T(128)}, u32[]{:S(2)}) copy-start(f32[12]{0:T(128)} %basis_width.1) | copy-start | bytes 148
  37.7 6.4 %collective-permute-start.8 = (bf16[1024,128]{1,0:T(8,128)(2,1)S(1)}, bf16[1024,128]{1,0:T(8,128)(2,1)S(1)}, u32[]{:S(2)}, u32[]{:S(2)}) collective-permute-start(bf16[1024,128]{1,0:T(8,128)(2,1)S(1)} %join.2.refs_0_), channel_id=1, source_target_pairs={{0,2},{1,3},{2,0},{3,1},{4,6},{5,7},{6,4},{7,5},{8,10},{9,11},{10,... | collective-permute-start | bytes 786440 | tf_op jit(solution)/shard_map/ppermute | solution.py:194
  44.1 2.0 %collective-permute-start.9 = (bf16[2048,128]{1,0:T(8,128)(2,1)S(1)}, bf16[2048,128]{1,0:T(8,128)(2,1)S(1)}, u32[]{:S(2)}, u32[]{:S(2)}) collective-permute-start(bf16[2048,128]{1,0:T(8,128)(2,1)S(1)} %join.3.near), channel_id=1, source_target_pairs={{0,1},{1,0},{2,3},{3,2},{4,5},{5,4},{6,7},{7,6},{8,9},{9,8},{10,11... | collective-permute-start | bytes 1572872 | tf_op jit(solution)/shard_map/ppermute | solution.py:194

commit v6 on v5

--- a/solution.py
+++ b/solution.py
@@ -53,19 +53,21 @@
     return pltpu.roll(x, by % BW, 1)
 
 
-def lanczos_taps(gap, whole, part):
-    shift = whole + part
+def lanczos_taps(whole, part):
+    lane = lax.broadcasted_iota(jnp.int32, (8, BW), 1).astype(jnp.float32)
+    x = (whole + lane - 2.0) - (whole + part)
+
+    def sinc(v):
+        angle = jnp.pi * v
+        return jnp.where(v == 0.0, 1.0, jnp.sin(angle) / jnp.where(v == 0.0, 1.0, angle))
+
+    return jnp.where(jnp.abs(x) < 3.0, sinc(x) * sinc(x / 3.0), 0.0)
+
+
+def lanczos_band(gap, whole, taps):
     band = jnp.zeros(gap.shape, jnp.float32)
-    for tap in range(-2, 5):
-        spot = whole + tap
-        x = jnp.full((8, 128), spot - shift, jnp.float32)
-
-        def sinc(v):
-            angle = jnp.pi * v
-            return jnp.where(v == 0.0, 1.0, jnp.sin(angle) / jnp.where(v == 0.0, 1.0, angle))
-
-        value = jnp.where(jnp.abs(x) < 3.0, sinc(x) * sinc(x / 3.0), 0.0)
-        band = jnp.where(gap == spot, value[0:1, 0:1], band)
+    for tap in range(7):
+        band = jnp.where(gap == whole + (tap - 2), taps[0:1, tap : tap + 1], band)
     return band.astype(jnp.bfloat16)
 
 
@@ -112,16 +114,22 @@
     turn_in = pltpu.make_async_copy(spots, starts, sems.at[len(copies)])
     turn_in.start()
 
-    gap = (
-        lax.broadcasted_iota(jnp.int32, (WIDE + 2 * SIDE, WIDE), 0)
-        - lax.broadcasted_iota(jnp.int32, (WIDE + 2 * SIDE, WIDE), 1)
-        - SIDE
-    ).astype(jnp.float32)
-    wide_band[...] = lanczos_taps(gap, offset[0, 1].astype(jnp.float32), fraction[0, 1])
+    whole = offset[0, 1].astype(jnp.float32)
+    taps = lanczos_taps(whole, fraction[0, 1])
+    place_of = lax.broadcasted_iota(jnp.int32, (SIDE, SIDE), 0) - lax.broadcasted_iota(jnp.int32, (SIDE, SIDE), 1)
+    above, middle, below = [
+        lanczos_band((place_of - shift).astype(jnp.float32), whole, taps) for shift in (SIDE, 0, -SIDE)
+    ]
+    nothing = jnp.zeros_like(middle)
+    for down, pieces in enumerate(((above, nothing), (middle, above), (below, middle), (nothing, below))):
+        for col, piece in enumerate(pieces):
+            wide_band[down * SIDE : (down + 1) * SIDE, col * SIDE : (col + 1) * SIDE] = piece
     gap = (
         lax.broadcasted_iota(jnp.int32, (rows, rows), 1) - lax.broadcasted_iota(jnp.int32, (rows, rows), 0)
     ).astype(jnp.float32)
-    row_warp = lanczos_taps(gap, offset[0, 0].astype(jnp.float32), fraction[0, 0])
+    whole = offset[0, 0].astype(jnp.float32)
+    row_warp = lanczos_band(gap, whole, lanczos_taps(whole, fraction[0, 0]))
+
     heavy = weight[...].astype(jnp.float32)
     named, slotted = owner[...].astype(jnp.float32), slot[...].astype(jnp.float32)
     names = [named * PS + slotted] if name_tiles(peers) == 1 else [named, slotted]
@@ -247,27 +255,26 @@
 
 
 def template_kernel(peers, bases, me_ref, *refs):
-    *terms, template, leaning, coadd, weight_sum = refs
+    *terms, leaning, coadd, weight_sum = refs
     me = me_ref[0]
     owner, slot, numbers = read_tags(peers, terms)
     heavy = numbers[:, 4 * bases : 4 * bases + 1]
     level = heavy * numbers[:, 4 * bases + 1 : 4 * bases + 2]
     mine = owner == me
+    weighed, levelled = [], []
     for i in range(PS):
         hit = mine & (slot == i)
-
-        def over(x):
-            found = jnp.sum(jnp.where(hit, x, 0.0), axis=0, keepdims=True)
-            return jnp.sum(found, axis=1, keepdims=True)
-
-        total = 1.0 + over(heavy)
+        weighed.append(jnp.sum(jnp.where(hit, heavy, 0.0), axis=0, keepdims=True))
+        levelled.append(jnp.sum(jnp.where(hit, level, 0.0), axis=0, keepdims=True))
+    total = 1.0 + jnp.sum(jnp.concatenate(weighed, axis=0), axis=1, keepdims=True)
+    over = jnp.sum(jnp.concatenate(levelled, axis=0), axis=1, keepdims=True)
+    weight_sum[...] = jnp.broadcast_to(total, weight_sum.shape)
+    for i in range(PS):
         here = slice(i * BH, (i + 1) * BH)
-        mean = (summed_terms(terms, here) + over(level)) / total
-        rounded = mean.astype(jnp.bfloat16)
-        template[here, :] = rounded
-        leaning[here, :] = turned(rounded.astype(jnp.float32), LEAN).astype(jnp.bfloat16)
+        mean = (summed_terms(terms, here) + over[i : i + 1, :]) / total[i : i + 1, :]
+        rounded = mean.astype(jnp.bfloat16).astype(jnp.float32)
+        leaning[here, :] = turned(rounded, LEAN).astype(jnp.bfloat16)
         coadd[here, :] = mean
-        weight_sum[i : i + 1, :] = jnp.broadcast_to(total, (1, BW))
 
 
 AROUND = [(down, across) for down in (-1, 0, 1) for across in (-1, 0, 1)]
@@ -353,6 +360,7 @@
     weight_sum,
     spots,
     scales,
+    template,
     out,
     table,
     window,
@@ -366,6 +374,7 @@
     table[half : 2 * half, :] = other[...]
     table[2 * half :, :] = jnp.zeros((BH, BW), jnp.bfloat16)
     matched[...] = jnp.zeros_like(matched)
+    template[...] = coadd[...].astype(jnp.bfloat16)
     if most % GROUP:
         window[...] = jnp.zeros_like(window)
     lane = lax.broadcasted_iota(jnp.int32, (BH, BW), 1)
@@ -489,17 +498,15 @@
     )(basis_width)
 
     terms = scatter_sum(keep, send, peers)
-    square = jax.ShapeDtypeStruct((BOXES, BW), jnp.bfloat16)
-    template, leaning, coadd, weight_sum = pl.pallas_call(
+    leaning, coadd, weight_sum = pl.pallas_call(
         functools.partial(template_kernel, peers, bases),
         out_shape=[
-            square,
-            square,
+            jax.ShapeDtypeStruct((BOXES, BW), jnp.bfloat16),
             jax.ShapeDtypeStruct((BOXES, BW), jnp.float32),
             jax.ShapeDtypeStruct((PS, BW), jnp.float32),
         ],
         in_specs=[SMEM] + [VMEM] * len(terms),
-        out_specs=[VMEM] * 4,
+        out_specs=[VMEM] * 3,
         compiler_params=params(),
         name="template",
     )(me, *terms)
@@ -518,11 +525,14 @@
 
     steps = min(peers, 16)
     tall = steps * pl.cdiv(most, GROUP) * GROUP * TALL
-    difference_coadd = pl.pallas_call(
+    template, difference_coadd = pl.pallas_call(
         functools.partial(match_kernel, peers, bases, most, steps),
-        out_shape=jax.ShapeDtypeStruct((BOXES, BW), jnp.float32),
+        out_shape=[
+            jax.ShapeDtypeStruct((BOXES, BW), jnp.bfloat16),
+            jax.ShapeDtypeStruct((BOXES, BW), jnp.float32),
+        ],
         in_specs=[VMEM] * 6 + [SMEM] * 2,
-        out_specs=VMEM,
+        out_specs=[VMEM] * 2,
         scratch_shapes=[
             pltpu.VMEM(((peers * PS + 1) * BH, BW), jnp.bfloat16),
             pltpu.VMEM((tall, BW + 2 * LEAN), jnp.bfloat16),

time: 54.6 us -> 53.6 us (0.982)
  Pallas kernels: 14.6 us -> 13.2 us
    pallas_call x1, Pallas kernels: 3.2 us -> 2.52 us  [shards(): pl.pallas_call(functools.partial(warp_kernel, peers, bases), out_shape=[h...]
    pallas_call x1, Pallas kernels: 0.88 us -> 0.32 us  [shards(): pl.pallas_call(functools.partial(template_kernel, peers, bases), out_shap...]
  transfers between devices with their start and end apart: 10 -> 10, of which waited for: 8 -> 7; matrix products, arithmetic and copies ran while one was open for 0% -> 0% of each run, Pallas kernels for 3% -> 3%
where the time goes in v6:
time: 53.6 us; the launch traced here: 53.2 us
  waiting for transfers between devices  22.8 us (43%)
  starting transfers between devices  14 us (26%)
  Pallas kernels  13.2 us (25%)
  local copies, waits for them, and re-layouts  1.73 us (3%)
  between operations  1.41 us (3%)
    ppermute x10, waiting for transfers between devices, swap(): return lax.ppermute(x, 'visit', [(i, i ^ bit) for i in range(axis_size)])  22.8 us
    ppermute x10, starting transfers between devices, swap(): return lax.ppermute(x, 'visit', [(i, i ^ bit) for i in range(axis_size)])  14 us
    pallas_call x1, Pallas kernels, shards(): pl.pallas_call(functools.partial(match_kernel, peers, bases, most, steps)...  8.3 us
    pallas_call x1, Pallas kernels, shards(): pl.pallas_call(functools.partial(warp_kernel, peers, bases), out_shape=[h...  2.52 us
    unnamed x16, local copies, waits for them, and re-layouts  1.73 us
    pallas_call x1, Pallas kernels, shards(): pl.pallas_call(gauss_kernel, out_shape=[jax.ShapeDtypeStruct((table_size,...  1.25 us
  transfers between devices with their start and end apart: 10, of which 7 were waited for; matrix products, arithmetic and copies ran while one was open for 0% of the time, Pallas kernels for 3%

profile of v6, /device:TPU:0, one launch (start us, length us, event | category | flops | bytes accessed | tf_op | source)
XLA Modules:
  0.0 53.2 jit_solution(16971018781497873610)
XLA Ops:
  1.3 0.6 %copy-done.4 = f32[1,2]{1,0:T(1,128)S(1)} copy-done((f32[1,2]{1,0:T(1,128)S(1)}, f32[1,2]{1,0:T(1,128)}, u32[]{:S(2)}) %copy-start.4) | copy-done | bytes 32
  1.9 0.0 copy-done.5
  2.0 0.0 copy-done.6
  2.0 0.0 copy-done.1
  2.0 0.0 copy-done.2
  2.0 0.0 copy-done.3
  2.0 1.0 %copy-done = bf16[1,256,1024]{2,1,0:T(8,128)(2,1)S(1)} copy-done((bf16[1,256,1024]{2,1,0:T(8,128)(2,1)S(1)}, bf16[1,256,1024]{2,1,0:T(8,128)(2,1)}, u32[]{:S(2)}) %copy-start) | copy-done | bytes 524312
  3.1 2.5 %warp.1 = (bf16[2304,128]{1,0:T(8,128)(2,1)S(1)}, bf16[2304,128]{1,0:T(8,128)(2,1)S(1)}) custom-call(s32[1]{0:T(128)} %bitcast.me_ref, bf16[256,1024]{1,0:T(8,128)(2,1)S(1)} %bitcast.7, s32[1,128]{1,0:T(1,128)S(1)} %bitcast.8, s32[1,128]{1,0:T(1,128)S(1)} %copy-done.2, s32[1,2]{1,0:T(1,128)S(1)} %copy-done.3, f32[1,2]{1,0:T(1,128)S(1)} %copy-done.4, ...), custom_call_target="tpu_custom_call" | custom-call | tf_op jit(solution)/shard_map/warp/pallas_call | solution.py:454
  5.6 0.5 collective-permute-start
  6.1 1.6 %collective-permute-done.theirs = bf16[2304,128]{1,0:T(8,128)(2,1)S(1)} collective-permute-done((bf16[2304,128]{1,0:T(8,128)(2,1)S(1)}, bf16[2304,128]{1,0:T(8,128)(2,1)S(1)}, u32[]{:S(2)}, u32[]{:S(2)}) %collective-permute-start) | collective-permute-done | bytes 589856 | tf_op jit(solution)/shard_map/ppermute | solution.py:202
  7.7 0.1 add_parts.2
  7.9 3.0 %collective-permute-start.1 = (bf16[1152,128]{1,0:T(8,128)(2,1)S(1)}, bf16[1152,128]{1,0:T(8,128)(2,1)S(1)}, u32[]{:S(2)}, u32[]{:S(2)}) collective-permute-start(bf16[1152,128]{1,0:T(8,128)(2,1)S(1)} %get-tuple-element.22), channel_id=1, source_target_pairs={{0,2},{1,3},{2,0},{3,1},{4,6},{5,7},{6,4},{7,5},{8,10},{9,11},{10,... | collective-permute-start | bytes 884744 | tf_op jit(solution)/shard_map/ppermute | solution.py:202
  10.8 7.3 %collective-permute-done.1.theirs = bf16[1152,128]{1,0:T(8,128)(2,1)S(1)} collective-permute-done((bf16[1152,128]{1,0:T(8,128)(2,1)S(1)}, bf16[1152,128]{1,0:T(8,128)(2,1)S(1)}, u32[]{:S(2)}, u32[]{:S(2)}) %collective-permute-start.1) | collective-permute-done | bytes 294944 | tf_op jit(solution)/shard_map/ppermute | solution.py:202
  18.1 0.1 add_parts.3
  18.2 3.9 %collective-permute-start.2 = (bf16[288,128]{1,0:T(8,128)(2,1)S(1)}, bf16[288,128]{1,0:T(8,128)(2,1)S(1)}, u32[]{:S(2)}, u32[]{:S(2)}) collective-permute-start(bf16[288,128]{1,0:T(8,128)(2,1)S(1)} %get-tuple-element.24), channel_id=1, source_target_pairs={{0,12},{1,13},{2,14},{3,15},{4,8},{5,9},{6,10},{7,11},{8,4},{9,5},... | collective-permute-start | bytes 221192 | tf_op jit(solution)/shard_map/ppermute | solution.py:202
  22.1 0.6 %collective-permute-start.4 = (bf16[288,128]{1,0:T(8,128)(2,1)S(1)}, bf16[288,128]{1,0:T(8,128)(2,1)S(1)}, u32[]{:S(2)}, u32[]{:S(2)}) collective-permute-start(bf16[288,128]{1,0:T(8,128)(2,1)S(1)} %get-tuple-element.26), channel_id=1, source_target_pairs={{0,4},{1,5},{2,6},{3,7},{4,0},{5,1},{6,2},{7,3},{8,12},{9,13},{10,... | collective-permute-start | bytes 221192 | tf_op jit(solution)/shard_map/ppermute | solution.py:202
  22.7 2.6 %collective-permute-done.2.refs_1_ = bf16[288,128]{1,0:T(8,128)(2,1)S(1)} collective-permute-done((bf16[288,128]{1,0:T(8,128)(2,1)S(1)}, bf16[288,128]{1,0:T(8,128)(2,1)S(1)}, u32[]{:S(2)}, u32[]{:S(2)}) %collective-permute-start.2) | collective-permute-done | bytes 73760 | tf_op jit(solution)/shard_map/ppermute | solution.py:202
  25.3 2.6 %collective-permute-done.3.refs_2_ = bf16[288,128]{1,0:T(8,128)(2,1)S(1)} collective-permute-done((bf16[288,128]{1,0:T(8,128)(2,1)S(1)}, bf16[288,128]{1,0:T(8,128)(2,1)S(1)}, u32[]{:S(2)}, u32[]{:S(2)}) %collective-permute-start.3) | collective-permute-done | bytes 73760 | tf_op jit(solution)/shard_map/ppermute | solution.py:202
  27.9 0.0 collective-permute-done.4.refs_3_
  27.9 0.3 template.1
  28.3 2.6 %collective-permute-start.7 = (bf16[256,128]{1,0:T(8,128)(2,1)S(1)}, bf16[256,128]{1,0:T(8,128)(2,1)S(1)}, u32[]{:S(2)}, u32[]{:S(2)}) collective-permute-start(bf16[256,128]{1,0:T(8,128)(2,1)S(1)} %get-tuple-element.27.refs_0_), channel_id=1, source_target_pairs={{0,12},{1,13},{2,14},{3,15},{4,8},{5,9},{6,10},{7,11},{8,4},{9,5},... | collective-permute-start | bytes 196616 | tf_op jit(solution)/shard_map/ppermute | solution.py:202
  30.9 1.8 %collective-permute-start.5 = (bf16[256,128]{1,0:T(8,128)(2,1)S(1)}, bf16[256,128]{1,0:T(8,128)(2,1)S(1)}, u32[]{:S(2)}, u32[]{:S(2)}) collective-permute-start(bf16[256,128]{1,0:T(8,128)(2,1)S(1)} %get-tuple-element.27.refs_0_), channel_id=1, source_target_pairs={{0,4},{1,5},{2,6},{3,7},{4,0},{5,1},{6,2},{7,3},{8,12},{9,13},{10,... | collective-permute-start | bytes 196616 | tf_op jit(solution)/shard_map/ppermute | solution.py:202
  32.7 2.4 %collective-permute-done.7.refs_3_ = bf16[256,128]{1,0:T(8,128)(2,1)S(1)} collective-permute-done((bf16[256,128]{1,0:T(8,128)(2,1)S(1)}, bf16[256,128]{1,0:T(8,128)(2,1)S(1)}, u32[]{:S(2)}, u32[]{:S(2)}) %collective-permute-start.7) | collective-permute-done | bytes 65568 | tf_op jit(solution)/shard_map/ppermute | solution.py:202
  35.1 1.3 %collective-permute-done.6.refs_2_ = bf16[256,128]{1,0:T(8,128)(2,1)S(1)} collective-permute-done((bf16[256,128]{1,0:T(8,128)(2,1)S(1)}, bf16[256,128]{1,0:T(8,128)(2,1)S(1)}, u32[]{:S(2)}, u32[]{:S(2)}) %collective-permute-start.6) | collective-permute-done | bytes 65568 | tf_op jit(solution)/shard_map/ppermute | solution.py:202
  36.5 0.0 copy-start.7
  36.5 1.5 %collective-permute-start.8 = (bf16[1024,128]{1,0:T(8,128)(2,1)S(1)}, bf16[1024,128]{1,0:T(8,128)(2,1)S(1)}, u32[]{:S(2)}, u32[]{:S(2)}) collective-permute-start(bf16[1024,128]{1,0:T(8,128)(2,1)S(1)} %join.2.refs_0_), channel_id=1, source_target_pairs={{0,2},{1,3},{2,0},{3,1},{4,6},{5,7},{6,4},{7,5},{8,10},{9,11},{10,... | collective-permute-start | bytes 786440 | tf_op jit(solution)/shard_map/ppermute | solution.py:202
  38.0 4.9 %collective-permute-done.8.refs_1_ = bf16[1024,128]{1,0:T(8,128)(2,1)S(1)} collective-permute-done((bf16[1024,128]{1,0:T(8,128)(2,1)S(1)}, bf16[1024,128]{1,0:T(8,128)(2,1)S(1)}, u32[]{:S(2)}, u32[]{:S(2)}) %collective-permute-start.8) | collective-permute-done | bytes 262176 | tf_op jit(solution)/shard_map/ppermute | solution.py:202
  43.0 0.1 collective-permute-start.9
  43.1 1.3 %gauss_bands.1 = (bf16[12,256,128]{2,1,0:T(8,128)(2,1)S(1)}, bf16[12,128,256]{2,1,0:T(8,128)(2,1)S(1)}) custom-call(f32[12]{0:T(128)S(1)} %copy-done.7), custom_call_target="tpu_custom_call" | custom-call | tf_op jit(solution)/shard_map/gauss_bands/pallas_call | solution.py:488
  44.3 0.6 %plan.1 = (s32[32,128]{1,0:T(8,128)S(1)}, f32[16,128]{1,0:T(8,128)S(1)}) custom-call(s32[1]{0:T(128)} %bitcast.me_ref, bf16[288,128]{1,0:T(8,128)(2,1)S(1)} %get-tuple-element.23.refs_0_, bf16[288,128]{1,0:T(8,128)(2,1)S(1)} %collective-permute-done.2.refs_1_, bf16[288,128]{1,0:T(8,128)(2,1)S(1)} %collective-permute-done.3.refs_2_, ...), custom_call_target="tpu_custom_call" | custom-call | tf_op jit(solution)/shard_map/plan/pallas_call | solution.py:514
  44.9 0.0 collective-permute-done.9.other
  44.9 8.3 %match.1 = (bf16[256,128]{1,0:T(8,128)(2,1)}, f32[256,128]{1,0:T(8,128)}) custom-call(bf16[2048,128]{1,0:T(8,128)(2,1)S(1)} %join.3.near, bf16[2048,128]{1,0:T(8,128)(2,1)S(1)} %collective-permute-done.9.other, bf16[12,256,128]{2,1,0:T(8,128)(2,1)S(1)} %get-tuple-element.28.across_bands, bf16[12,128,256]{2,1,0:T(8,128)(2,1)S(1)} %get-tuple-element.29.down_bands, ...), custom_call_target="tpu_custom_call" | custom-call | tf_op jit(solution)/shard_map/match/pallas_call | solution.py:528
  (13 shorter events, 0.1 us)
Async XLA Ops:
  1.3 0.7 %copy-start.4 = (f32[1,2]{1,0:T(1,128)S(1)}, f32[1,2]{1,0:T(1,128)}, u32[]{:S(2)}) copy-start(f32[1,2]{1,0:T(1,128)} %fraction_in.1) | copy-start | bytes 28
  1.3 0.7 %copy-start.5 = (s32[1,6]{1,0:T(1,128)S(1)}, s32[1,6]{1,0:T(1,128)}, u32[]{:S(2)}) copy-start(s32[1,6]{1,0:T(1,128)} %index_in.1) | copy-start | bytes 76
  1.3 0.7 %copy-start.6 = (f32[1,6]{1,0:T(1,128)S(1)}, f32[1,6]{1,0:T(1,128)}, u32[]{:S(2)}) copy-start(f32[1,6]{1,0:T(1,128)} %coef_in.1) | copy-start | bytes 76
  1.3 0.7 %copy-start.1 = (s32[1,128,1]{1,2,0:T(1,128)S(1)}, s32[1,128,1]{1,2,0:T(1,128)}, u32[]{:S(2)}) copy-start(s32[1,128,1]{1,2,0:T(1,128)} %param.13) | copy-start | bytes 1540
  1.3 0.7 %copy-start.2 = (s32[1,128]{1,0:T(1,128)S(1)}, s32[1,128]{1,0:T(1,128)}, u32[]{:S(2)}) copy-start(s32[1,128]{1,0:T(1,128)} %slot_in.1) | copy-start | bytes 1540
  1.3 0.7 %copy-start.3 = (s32[1,2]{1,0:T(1,128)S(1)}, s32[1,2]{1,0:T(1,128)}, u32[]{:S(2)}) copy-start(s32[1,2]{1,0:T(1,128)} %offset_in.1) | copy-start | bytes 28
  2.0 1.0 %copy-start = (bf16[1,256,1024]{2,1,0:T(8,128)(2,1)S(1)}, bf16[1,256,1024]{2,1,0:T(8,128)(2,1)}, u32[]{:S(2)}) copy-start(bf16[1,256,1024]{2,1,0:T(8,128)(2,1)} %param.9) | copy-start | bytes 1572868
  5.6 2.1 %collective-permute-start = (bf16[2304,128]{1,0:T(8,128)(2,1)S(1)}, bf16[2304,128]{1,0:T(8,128)(2,1)S(1)}, u32[]{:S(2)}, u32[]{:S(2)}) collective-permute-start(bf16[2304,128]{1,0:T(8,128)(2,1)S(1)} %get-tuple-element.20), channel_id=1, source_target_pairs={{0,1},{1,0},{2,3},{3,2},{4,5},{5,4},{6,7},{7,6},{8,9},{9,8},{10,11... | collective-permute-start | bytes 1769480 | tf_op jit(solution)/shard_map/ppermute | solution.py:202
  7.9 10.3 %collective-permute-start.1 = (bf16[1152,128]{1,0:T(8,128)(2,1)S(1)}, bf16[1152,128]{1,0:T(8,128)(2,1)S(1)}, u32[]{:S(2)}, u32[]{:S(2)}) collective-permute-start(bf16[1152,128]{1,0:T(8,128)(2,1)S(1)} %get-tuple-element.22), channel_id=1, source_target_pairs={{0,2},{1,3},{2,0},{3,1},{4,6},{5,7},{6,4},{7,5},{8,10},{9,11},{10,... | collective-permute-start | bytes 884744 | tf_op jit(solution)/shard_map/ppermute | solution.py:202
  18.2 7.1 %collective-permute-start.2 = (bf16[288,128]{1,0:T(8,128)(2,1)S(1)}, bf16[288,128]{1,0:T(8,128)(2,1)S(1)}, u32[]{:S(2)}, u32[]{:S(2)}) collective-permute-start(bf16[288,128]{1,0:T(8,128)(2,1)S(1)} %get-tuple-element.24), channel_id=1, source_target_pairs={{0,12},{1,13},{2,14},{3,15},{4,8},{5,9},{6,10},{7,11},{8,4},{9,5},... | collective-permute-start | bytes 221192 | tf_op jit(solution)/shard_map/ppermute | solution.py:202
  22.1 5.8 %collective-permute-start.3 = (bf16[288,128]{1,0:T(8,128)(2,1)S(1)}, bf16[288,128]{1,0:T(8,128)(2,1)S(1)}, u32[]{:S(2)}, u32[]{:S(2)}) collective-permute-start(bf16[288,128]{1,0:T(8,128)(2,1)S(1)} %get-tuple-element.25), channel_id=1, source_target_pairs={{0,8},{1,9},{2,10},{3,11},{4,12},{5,13},{6,14},{7,15},{8,0},{9,1},... | collective-permute-start | bytes 221192 | tf_op jit(solution)/shard_map/ppermute | solution.py:202
  22.1 5.8 %collective-permute-start.4 = (bf16[288,128]{1,0:T(8,128)(2,1)S(1)}, bf16[288,128]{1,0:T(8,128)(2,1)S(1)}, u32[]{:S(2)}, u32[]{:S(2)}) collective-permute-start(bf16[288,128]{1,0:T(8,128)(2,1)S(1)} %get-tuple-element.26), channel_id=1, source_target_pairs={{0,4},{1,5},{2,6},{3,7},{4,0},{5,1},{6,2},{7,3},{8,12},{9,13},{10,... | collective-permute-start | bytes 221192 | tf_op jit(solution)/shard_map/ppermute | solution.py:202
  28.3 6.8 %collective-permute-start.7 = (bf16[256,128]{1,0:T(8,128)(2,1)S(1)}, bf16[256,128]{1,0:T(8,128)(2,1)S(1)}, u32[]{:S(2)}, u32[]{:S(2)}) collective-permute-start(bf16[256,128]{1,0:T(8,128)(2,1)S(1)} %get-tuple-element.27.refs_0_), channel_id=1, source_target_pairs={{0,12},{1,13},{2,14},{3,15},{4,8},{5,9},{6,10},{7,11},{8,4},{9,5},... | collective-permute-start | bytes 196616 | tf_op jit(solution)/shard_map/ppermute | solution.py:202
  30.9 5.5 %collective-permute-start.6 = (bf16[256,128]{1,0:T(8,128)(2,1)S(1)}, bf16[256,128]{1,0:T(8,128)(2,1)S(1)}, u32[]{:S(2)}, u32[]{:S(2)}) collective-permute-start(bf16[256,128]{1,0:T(8,128)(2,1)S(1)} %get-tuple-element.27.refs_0_), channel_id=1, source_target_pairs={{0,8},{1,9},{2,10},{3,11},{4,12},{5,13},{6,14},{7,15},{8,0},{9,1},... | collective-permute-start | bytes 196616 | tf_op jit(solution)/shard_map/ppermute | solution.py:202
  30.9 5.5 %collective-permute-start.5 = (bf16[256,128]{1,0:T(8,128)(2,1)S(1)}, bf16[256,128]{1,0:T(8,128)(2,1)S(1)}, u32[]{:S(2)}, u32[]{:S(2)}) collective-permute-start(bf16[256,128]{1,0:T(8,128)(2,1)S(1)} %get-tuple-element.27.refs_0_), channel_id=1, source_target_pairs={{0,4},{1,5},{2,6},{3,7},{4,0},{5,1},{6,2},{7,3},{8,12},{9,13},{10,... | collective-permute-start | bytes 196616 | tf_op jit(solution)/shard_map/ppermute | solution.py:202
  36.5 6.6 %copy-start.7 = (f32[12]{0:T(128)S(1)}, f32[12]{0:T(128)}, u32[]{:S(2)}) copy-start(f32[12]{0:T(128)} %basis_width.1) | copy-start | bytes 148
  36.5 6.4 %collective-permute-start.8 = (bf16[1024,128]{1,0:T(8,128)(2,1)S(1)}, bf16[1024,128]{1,0:T(8,128)(2,1)S(1)}, u32[]{:S(2)}, u32[]{:S(2)}) collective-permute-start(bf16[1024,128]{1,0:T(8,128)(2,1)S(1)} %join.2.refs_0_), channel_id=1, source_target_pairs={{0,2},{1,3},{2,0},{3,1},{4,6},{5,7},{6,4},{7,5},{8,10},{9,11},{10,... | collective-permute-start | bytes 786440 | tf_op jit(solution)/shard_map/ppermute | solution.py:202
  43.0 2.0 %collective-permute-start.9 = (bf16[2048,128]{1,0:T(8,128)(2,1)S(1)}, bf16[2048,128]{1,0:T(8,128)(2,1)S(1)}, u32[]{:S(2)}, u32[]{:S(2)}) collective-permute-start(bf16[2048,128]{1,0:T(8,128)(2,1)S(1)} %join.3.near), channel_id=1, source_target_pairs={{0,1},{1,0},{2,3},{3,2},{4,5},{5,4},{6,7},{7,6},{8,9},{9,8},{10,11... | collective-permute-start | bytes 1572872 | tf_op jit(solution)/shard_map/ppermute | solution.py:202

commit v7 on v6

--- a/solution.py
+++ b/solution.py
@@ -33,12 +33,8 @@
     return (away & 1) * (peers // 2) + ((away >> 1) & 1) * (peers // 4) + (away >> 2)
 
 
-def name_tiles(peers):
-    return 1 if peers * PS <= 256 else 2
-
-
-def chunk_rows(peers):
-    return BOXES + (name_tiles(peers) + 1) * peers
+QUAD = 4
+CHUNK = BOXES + BH
 
 
 def windows(width):
@@ -101,7 +97,7 @@
 ):
     rows, width = picture.shape
     me = me_ref[0]
-    chunk = chunk_rows(peers)
+    chunk = CHUNK
     sources = (owner_in, slot_in, offset_in, fraction_in, weight_in, index_in, coef_in, picture_in)
     targets = (owner, slot, offset, fraction, weight, index, coef, picture)
     copies = [pltpu.make_async_copy(x, y, sems.at[i]) for i, (x, y) in enumerate(zip(sources, targets))]
@@ -131,8 +127,6 @@
     row_warp = lanczos_band(gap, whole, lanczos_taps(whole, fraction[0, 0]))
 
     heavy = weight[...].astype(jnp.float32)
-    named, slotted = owner[...].astype(jnp.float32), slot[...].astype(jnp.float32)
-    names = [named * PS + slotted] if name_tiles(peers) == 1 else [named, slotted]
     lane = lax.broadcasted_iota(jnp.int32, (8, BW), 1)
     numbers = jnp.zeros((8, BW), jnp.float32)
     share = jnp.zeros((8, BW), jnp.float32)
@@ -149,10 +143,11 @@
     mean = jnp.sum(jnp.sum(picture[...].astype(jnp.float32), axis=0, keepdims=True), axis=1, keepdims=True)
     mean = (mean * (1.0 / (rows * width))).astype(jnp.bfloat16).astype(jnp.float32)
     numbers = jnp.where(lane == 4 * bases + 1, mean, numbers)[0:1]
-    row = lax.broadcasted_iota(jnp.int32, (peers, BW), 0)
-    tags = jnp.concatenate(
-        [jnp.where(row == me, x, 0.0).astype(jnp.bfloat16) for x in (*names, numbers)], axis=0
-    )
+    row = lax.broadcasted_iota(jnp.int32, (BH, BW), 0) - me % QUAD
+    tags = jnp.zeros((BH, BW), jnp.float32)
+    for i, line in enumerate((owner[...].astype(jnp.float32), slot[...].astype(jnp.float32), numbers)):
+        tags = jnp.where(row == i * QUAD, line, tags)
+    tags = tags.astype(jnp.bfloat16)
     passes = [
         jnp.dot(
             picture[:, low:high], wide_band[top:bottom, :], preferred_element_type=jnp.float32
@@ -242,22 +237,18 @@
     return total
 
 
-def read_tags(peers, terms):
-    tiles = [
-        summed_terms(terms, slice(BOXES + i * peers, BOXES + (i + 1) * peers)) for i in range(name_tiles(peers) + 1)
+def read_tags(terms):
+    tiles = [term[BOXES:, :].astype(jnp.float32) for term in terms]
+    owner, slot, numbers = [
+        jnp.concatenate([tile[i * QUAD : (i + 1) * QUAD, :] for tile in tiles], axis=0) for i in range(3)
     ]
-    if name_tiles(peers) == 1:
-        name = tiles[0].astype(jnp.int32)
-        owner, slot = name >> 4, name & (PS - 1)
-    else:
-        owner, slot = tiles[0].astype(jnp.int32), tiles[1].astype(jnp.int32)
-    return owner, slot, tiles[-1]
+    return owner.astype(jnp.int32), slot.astype(jnp.int32), numbers
 
 
 def template_kernel(peers, bases, me_ref, *refs):
     *terms, leaning, coadd, weight_sum = refs
     me = me_ref[0]
-    owner, slot, numbers = read_tags(peers, terms)
+    owner, slot, numbers = read_tags(terms)
     heavy = numbers[:, 4 * bases : 4 * bases + 1]
     level = heavy * numbers[:, 4 * bases + 1 : 4 * bases + 2]
     mine = owner == me
@@ -283,7 +274,7 @@
 def plan_kernel(peers, bases, most, rows_of_boxes, me_ref, *refs):
     *terms, spots, scales = refs
     me = me_ref[0]
-    owner, slot, numbers = read_tags(peers, terms)
+    owner, slot, numbers = read_tags(terms)
     nothing = peers * PS
     tile = place(owner, me, peers) * PS + slot
     boxes = owner.shape[1]
@@ -447,7 +438,7 @@
     table_size = basis_width.shape[0]
     most = max(2, 2 * box_slot.shape[1] // peers)
     me = lax.axis_index("visit").astype(jnp.int32).reshape(1)
-    chunk = chunk_rows(peers)
+    chunk = CHUNK
     owner = box_owner.reshape(1, -1)
 
     half = jax.ShapeDtypeStruct((peers // 2 * chunk, BW), jnp.bfloat16)

time: 53.6 us -> 52.7 us (0.983)
  waiting for transfers between devices: 22.8 us -> 21.9 us
    ppermute x10, waiting for transfers between devices: 22.8 us -> 21.9 us  [swap(): return lax.ppermute(x, 'visit', [(i, i ^ bit) for i in range(axis_size)])]
  transfers between devices with their start and end apart: 10 -> 10, of which waited for: 7 -> 8; matrix products, arithmetic and copies ran while one was open for 0% -> 0% of each run, Pallas kernels for 3% -> 3%
where the time goes in v7:
time: 52.7 us; the launch traced here: 52.5 us
  waiting for transfers between devices  21.9 us (42%)
  starting transfers between devices  14.1 us (27%)
  Pallas kernels  13.3 us (25%)
  local copies, waits for them, and re-layouts  1.73 us (3%)
  between operations  1.41 us (3%)
    ppermute x10, waiting for transfers between devices, swap(): return lax.ppermute(x, 'visit', [(i, i ^ bit) for i in range(axis_size)])  21.9 us
    ppermute x10, starting transfers between devices, swap(): return lax.ppermute(x, 'visit', [(i, i ^ bit) for i in range(axis_size)])  14.1 us
    pallas_call x1, Pallas kernels, shards(): pl.pallas_call(functools.partial(match_kernel, peers, bases, most, steps)...  8.39 us
    pallas_call x1, Pallas kernels, shards(): pl.pallas_call(functools.partial(warp_kernel, peers, bases), out_shape=[h...  2.52 us
    unnamed x16, local copies, waits for them, and re-layouts  1.73 us
    pallas_call x1, Pallas kernels, shards(): pl.pallas_call(gauss_kernel, out_shape=[jax.ShapeDtypeStruct((table_size,...  1.25 us
  transfers between devices with their start and end apart: 10, of which 8 were waited for; matrix products, arithmetic and copies ran while one was open for 0% of the time, Pallas kernels for 3%

profile of v7, /device:TPU:0, one launch (start us, length us, event | category | flops | bytes accessed | tf_op | source)
XLA Modules:
  0.0 52.5 jit_solution(5718912673371184222)
XLA Ops:
  1.3 0.6 %copy-done.4 = f32[1,2]{1,0:T(1,128)S(1)} copy-done((f32[1,2]{1,0:T(1,128)S(1)}, f32[1,2]{1,0:T(1,128)}, u32[]{:S(2)}) %copy-start.4) | copy-done | bytes 32
  1.9 0.0 copy-done.5
  2.0 0.0 copy-done.6
  2.0 0.0 copy-done.1
  2.0 0.0 copy-done.2
  2.0 0.0 copy-done.3
  2.0 1.0 %copy-done = bf16[1,256,1024]{2,1,0:T(8,128)(2,1)S(1)} copy-done((bf16[1,256,1024]{2,1,0:T(8,128)(2,1)S(1)}, bf16[1,256,1024]{2,1,0:T(8,128)(2,1)}, u32[]{:S(2)}) %copy-start) | copy-done | bytes 524312
  3.1 2.5 %warp.1 = (bf16[2176,128]{1,0:T(8,128)(2,1)S(1)}, bf16[2176,128]{1,0:T(8,128)(2,1)S(1)}) custom-call(s32[1]{0:T(128)} %bitcast.me_ref, bf16[256,1024]{1,0:T(8,128)(2,1)S(1)} %bitcast.7, s32[1,128]{1,0:T(1,128)S(1)} %bitcast.8, s32[1,128]{1,0:T(1,128)S(1)} %copy-done.2, s32[1,2]{1,0:T(1,128)S(1)} %copy-done.3, f32[1,2]{1,0:T(1,128)S(1)} %copy-done.4, ...), custom_call_target="tpu_custom_call" | custom-call | tf_op jit(solution)/shard_map/warp/pallas_call | solution.py:445
  5.6 0.5 collective-permute-start
  6.1 1.6 %collective-permute-done.theirs = bf16[2176,128]{1,0:T(8,128)(2,1)S(1)} collective-permute-done((bf16[2176,128]{1,0:T(8,128)(2,1)S(1)}, bf16[2176,128]{1,0:T(8,128)(2,1)S(1)}, u32[]{:S(2)}, u32[]{:S(2)}) %collective-permute-start) | collective-permute-done | bytes 557088 | tf_op jit(solution)/shard_map/ppermute | solution.py:197
  7.7 0.1 add_parts.2
  7.8 3.0 %collective-permute-start.1 = (bf16[1088,128]{1,0:T(8,128)(2,1)S(1)}, bf16[1088,128]{1,0:T(8,128)(2,1)S(1)}, u32[]{:S(2)}, u32[]{:S(2)}) collective-permute-start(bf16[1088,128]{1,0:T(8,128)(2,1)S(1)} %get-tuple-element.22), channel_id=1, source_target_pairs={{0,2},{1,3},{2,0},{3,1},{4,6},{5,7},{6,4},{7,5},{8,10},{9,11},{10,... | collective-permute-start | bytes 835592 | tf_op jit(solution)/shard_map/ppermute | solution.py:197
  10.8 7.0 %collective-permute-done.1.theirs = bf16[1088,128]{1,0:T(8,128)(2,1)S(1)} collective-permute-done((bf16[1088,128]{1,0:T(8,128)(2,1)S(1)}, bf16[1088,128]{1,0:T(8,128)(2,1)S(1)}, u32[]{:S(2)}, u32[]{:S(2)}) %collective-permute-start.1) | collective-permute-done | bytes 278560 | tf_op jit(solution)/shard_map/ppermute | solution.py:197
  17.7 0.1 add_parts.3
  17.8 3.9 %collective-permute-start.2 = (bf16[272,128]{1,0:T(8,128)(2,1)S(1)}, bf16[272,128]{1,0:T(8,128)(2,1)S(1)}, u32[]{:S(2)}, u32[]{:S(2)}) collective-permute-start(bf16[272,128]{1,0:T(8,128)(2,1)S(1)} %get-tuple-element.24), channel_id=1, source_target_pairs={{0,12},{1,13},{2,14},{3,15},{4,8},{5,9},{6,10},{7,11},{8,4},{9,5},... | collective-permute-start | bytes 208904 | tf_op jit(solution)/shard_map/ppermute | solution.py:197
  21.7 0.6 %collective-permute-start.4 = (bf16[272,128]{1,0:T(8,128)(2,1)S(1)}, bf16[272,128]{1,0:T(8,128)(2,1)S(1)}, u32[]{:S(2)}, u32[]{:S(2)}) collective-permute-start(bf16[272,128]{1,0:T(8,128)(2,1)S(1)} %get-tuple-element.26), channel_id=1, source_target_pairs={{0,4},{1,5},{2,6},{3,7},{4,0},{5,1},{6,2},{7,3},{8,12},{9,13},{10,... | collective-permute-start | bytes 208904 | tf_op jit(solution)/shard_map/ppermute | solution.py:197
  22.3 2.5 %collective-permute-done.2.refs_1_ = bf16[272,128]{1,0:T(8,128)(2,1)S(1)} collective-permute-done((bf16[272,128]{1,0:T(8,128)(2,1)S(1)}, bf16[272,128]{1,0:T(8,128)(2,1)S(1)}, u32[]{:S(2)}, u32[]{:S(2)}) %collective-permute-start.2) | collective-permute-done | bytes 69664 | tf_op jit(solution)/shard_map/ppermute | solution.py:197
  24.8 2.4 %collective-permute-done.3.refs_2_ = bf16[272,128]{1,0:T(8,128)(2,1)S(1)} collective-permute-done((bf16[272,128]{1,0:T(8,128)(2,1)S(1)}, bf16[272,128]{1,0:T(8,128)(2,1)S(1)}, u32[]{:S(2)}, u32[]{:S(2)}) %collective-permute-start.3) | collective-permute-done | bytes 69664 | tf_op jit(solution)/shard_map/ppermute | solution.py:197
  27.2 0.1 collective-permute-done.4.refs_3_
  27.3 0.3 template.1
  27.6 2.6 %collective-permute-start.7 = (bf16[256,128]{1,0:T(8,128)(2,1)S(1)}, bf16[256,128]{1,0:T(8,128)(2,1)S(1)}, u32[]{:S(2)}, u32[]{:S(2)}) collective-permute-start(bf16[256,128]{1,0:T(8,128)(2,1)S(1)} %get-tuple-element.27.refs_0_), channel_id=1, source_target_pairs={{0,12},{1,13},{2,14},{3,15},{4,8},{5,9},{6,10},{7,11},{8,4},{9,5},... | collective-permute-start | bytes 196616 | tf_op jit(solution)/shard_map/ppermute | solution.py:197
  30.2 1.8 %collective-permute-start.5 = (bf16[256,128]{1,0:T(8,128)(2,1)S(1)}, bf16[256,128]{1,0:T(8,128)(2,1)S(1)}, u32[]{:S(2)}, u32[]{:S(2)}) collective-permute-start(bf16[256,128]{1,0:T(8,128)(2,1)S(1)} %get-tuple-element.27.refs_0_), channel_id=1, source_target_pairs={{0,4},{1,5},{2,6},{3,7},{4,0},{5,1},{6,2},{7,3},{8,12},{9,13},{10,... | collective-permute-start | bytes 196616 | tf_op jit(solution)/shard_map/ppermute | solution.py:197
  32.0 2.2 %collective-permute-done.7.refs_3_ = bf16[256,128]{1,0:T(8,128)(2,1)S(1)} collective-permute-done((bf16[256,128]{1,0:T(8,128)(2,1)S(1)}, bf16[256,128]{1,0:T(8,128)(2,1)S(1)}, u32[]{:S(2)}, u32[]{:S(2)}) %collective-permute-start.7) | collective-permute-done | bytes 65568 | tf_op jit(solution)/shard_map/ppermute | solution.py:197
  34.3 1.3 %collective-permute-done.6.refs_2_ = bf16[256,128]{1,0:T(8,128)(2,1)S(1)} collective-permute-done((bf16[256,128]{1,0:T(8,128)(2,1)S(1)}, bf16[256,128]{1,0:T(8,128)(2,1)S(1)}, u32[]{:S(2)}, u32[]{:S(2)}) %collective-permute-start.6) | collective-permute-done | bytes 65568 | tf_op jit(solution)/shard_map/ppermute | solution.py:197
  35.6 0.0 copy-start.7
  35.6 1.6 %collective-permute-start.8 = (bf16[1024,128]{1,0:T(8,128)(2,1)S(1)}, bf16[1024,128]{1,0:T(8,128)(2,1)S(1)}, u32[]{:S(2)}, u32[]{:S(2)}) collective-permute-start(bf16[1024,128]{1,0:T(8,128)(2,1)S(1)} %join.2.refs_0_), channel_id=1, source_target_pairs={{0,2},{1,3},{2,0},{3,1},{4,6},{5,7},{6,4},{7,5},{8,10},{9,11},{10,... | collective-permute-start | bytes 786440 | tf_op jit(solution)/shard_map/ppermute | solution.py:197
  37.2 4.8 %collective-permute-done.8.refs_1_ = bf16[1024,128]{1,0:T(8,128)(2,1)S(1)} collective-permute-done((bf16[1024,128]{1,0:T(8,128)(2,1)S(1)}, bf16[1024,128]{1,0:T(8,128)(2,1)S(1)}, u32[]{:S(2)}, u32[]{:S(2)}) %collective-permute-start.8) | collective-permute-done | bytes 262176 | tf_op jit(solution)/shard_map/ppermute | solution.py:197
  42.1 0.1 collective-permute-start.9
  42.2 1.3 %gauss_bands.1 = (bf16[12,256,128]{2,1,0:T(8,128)(2,1)S(1)}, bf16[12,128,256]{2,1,0:T(8,128)(2,1)S(1)}) custom-call(f32[12]{0:T(128)S(1)} %copy-done.7), custom_call_target="tpu_custom_call" | custom-call | tf_op jit(solution)/shard_map/gauss_bands/pallas_call | solution.py:479
  43.4 0.6 %plan.1 = (s32[32,128]{1,0:T(8,128)S(1)}, f32[16,128]{1,0:T(8,128)S(1)}) custom-call(s32[1]{0:T(128)} %bitcast.me_ref, bf16[272,128]{1,0:T(8,128)(2,1)S(1)} %get-tuple-element.23.refs_0_, bf16[272,128]{1,0:T(8,128)(2,1)S(1)} %collective-permute-done.2.refs_1_, bf16[272,128]{1,0:T(8,128)(2,1)S(1)} %collective-permute-done.3.refs_2_, ...), custom_call_target="tpu_custom_call" | custom-call | tf_op jit(solution)/shard_map/plan/pallas_call | solution.py:505
  44.0 0.0 collective-permute-done.9.other
  44.1 8.4 %match.1 = (bf16[256,128]{1,0:T(8,128)(2,1)}, f32[256,128]{1,0:T(8,128)}) custom-call(bf16[2048,128]{1,0:T(8,128)(2,1)S(1)} %join.3.near, bf16[2048,128]{1,0:T(8,128)(2,1)S(1)} %collective-permute-done.9.other, bf16[12,256,128]{2,1,0:T(8,128)(2,1)S(1)} %get-tuple-element.28.across_bands, bf16[12,128,256]{2,1,0:T(8,128)(2,1)S(1)} %get-tuple-element.29.down_bands, ...), custom_call_target="tpu_custom_call" | custom-call | tf_op jit(solution)/shard_map/match/pallas_call | solution.py:519
  (13 shorter events, 0.1 us)
Async XLA Ops:
  1.3 0.7 %copy-start.4 = (f32[1,2]{1,0:T(1,128)S(1)}, f32[1,2]{1,0:T(1,128)}, u32[]{:S(2)}) copy-start(f32[1,2]{1,0:T(1,128)} %fraction_in.1) | copy-start | bytes 28
  1.3 0.7 %copy-start.5 = (s32[1,6]{1,0:T(1,128)S(1)}, s32[1,6]{1,0:T(1,128)}, u32[]{:S(2)}) copy-start(s32[1,6]{1,0:T(1,128)} %index_in.1) | copy-start | bytes 76
  1.3 0.7 %copy-start.6 = (f32[1,6]{1,0:T(1,128)S(1)}, f32[1,6]{1,0:T(1,128)}, u32[]{:S(2)}) copy-start(f32[1,6]{1,0:T(1,128)} %coef_in.1) | copy-start | bytes 76
  1.3 0.7 %copy-start.1 = (s32[1,128,1]{1,2,0:T(1,128)S(1)}, s32[1,128,1]{1,2,0:T(1,128)}, u32[]{:S(2)}) copy-start(s32[1,128,1]{1,2,0:T(1,128)} %param.13) | copy-start | bytes 1540
  1.3 0.7 %copy-start.2 = (s32[1,128]{1,0:T(1,128)S(1)}, s32[1,128]{1,0:T(1,128)}, u32[]{:S(2)}) copy-start(s32[1,128]{1,0:T(1,128)} %slot_in.1) | copy-start | bytes 1540
  1.3 0.7 %copy-start.3 = (s32[1,2]{1,0:T(1,128)S(1)}, s32[1,2]{1,0:T(1,128)}, u32[]{:S(2)}) copy-start(s32[1,2]{1,0:T(1,128)} %offset_in.1) | copy-start | bytes 28
  2.0 1.0 %copy-start = (bf16[1,256,1024]{2,1,0:T(8,128)(2,1)S(1)}, bf16[1,256,1024]{2,1,0:T(8,128)(2,1)}, u32[]{:S(2)}) copy-start(bf16[1,256,1024]{2,1,0:T(8,128)(2,1)} %param.9) | copy-start | bytes 1572868
  5.6 2.1 %collective-permute-start = (bf16[2176,128]{1,0:T(8,128)(2,1)S(1)}, bf16[2176,128]{1,0:T(8,128)(2,1)S(1)}, u32[]{:S(2)}, u32[]{:S(2)}) collective-permute-start(bf16[2176,128]{1,0:T(8,128)(2,1)S(1)} %get-tuple-element.20), channel_id=1, source_target_pairs={{0,1},{1,0},{2,3},{3,2},{4,5},{5,4},{6,7},{7,6},{8,9},{9,8},{10,11... | collective-permute-start | bytes 1671176 | tf_op jit(solution)/shard_map/ppermute | solution.py:197
  7.8 9.9 %collective-permute-start.1 = (bf16[1088,128]{1,0:T(8,128)(2,1)S(1)}, bf16[1088,128]{1,0:T(8,128)(2,1)S(1)}, u32[]{:S(2)}, u32[]{:S(2)}) collective-permute-start(bf16[1088,128]{1,0:T(8,128)(2,1)S(1)} %get-tuple-element.22), channel_id=1, source_target_pairs={{0,2},{1,3},{2,0},{3,1},{4,6},{5,7},{6,4},{7,5},{8,10},{9,11},{10,... | collective-permute-start | bytes 835592 | tf_op jit(solution)/shard_map/ppermute | solution.py:197
  17.8 7.0 %collective-permute-start.2 = (bf16[272,128]{1,0:T(8,128)(2,1)S(1)}, bf16[272,128]{1,0:T(8,128)(2,1)S(1)}, u32[]{:S(2)}, u32[]{:S(2)}) collective-permute-start(bf16[272,128]{1,0:T(8,128)(2,1)S(1)} %get-tuple-element.24), channel_id=1, source_target_pairs={{0,12},{1,13},{2,14},{3,15},{4,8},{5,9},{6,10},{7,11},{8,4},{9,5},... | collective-permute-start | bytes 208904 | tf_op jit(solution)/shard_map/ppermute | solution.py:197
  21.7 5.5 %collective-permute-start.3 = (bf16[272,128]{1,0:T(8,128)(2,1)S(1)}, bf16[272,128]{1,0:T(8,128)(2,1)S(1)}, u32[]{:S(2)}, u32[]{:S(2)}) collective-permute-start(bf16[272,128]{1,0:T(8,128)(2,1)S(1)} %get-tuple-element.25), channel_id=1, source_target_pairs={{0,8},{1,9},{2,10},{3,11},{4,12},{5,13},{6,14},{7,15},{8,0},{9,1},... | collective-permute-start | bytes 208904 | tf_op jit(solution)/shard_map/ppermute | solution.py:197
  21.7 5.6 %collective-permute-start.4 = (bf16[272,128]{1,0:T(8,128)(2,1)S(1)}, bf16[272,128]{1,0:T(8,128)(2,1)S(1)}, u32[]{:S(2)}, u32[]{:S(2)}) collective-permute-start(bf16[272,128]{1,0:T(8,128)(2,1)S(1)} %get-tuple-element.26), channel_id=1, source_target_pairs={{0,4},{1,5},{2,6},{3,7},{4,0},{5,1},{6,2},{7,3},{8,12},{9,13},{10,... | collective-permute-start | bytes 208904 | tf_op jit(solution)/shard_map/ppermute | solution.py:197
  27.6 6.7 %collective-permute-start.7 = (bf16[256,128]{1,0:T(8,128)(2,1)S(1)}, bf16[256,128]{1,0:T(8,128)(2,1)S(1)}, u32[]{:S(2)}, u32[]{:S(2)}) collective-permute-start(bf16[256,128]{1,0:T(8,128)(2,1)S(1)} %get-tuple-element.27.refs_0_), channel_id=1, source_target_pairs={{0,12},{1,13},{2,14},{3,15},{4,8},{5,9},{6,10},{7,11},{8,4},{9,5},... | collective-permute-start | bytes 196616 | tf_op jit(solution)/shard_map/ppermute | solution.py:197
  30.2 5.4 %collective-permute-start.6 = (bf16[256,128]{1,0:T(8,128)(2,1)S(1)}, bf16[256,128]{1,0:T(8,128)(2,1)S(1)}, u32[]{:S(2)}, u32[]{:S(2)}) collective-permute-start(bf16[256,128]{1,0:T(8,128)(2,1)S(1)} %get-tuple-element.27.refs_0_), channel_id=1, source_target_pairs={{0,8},{1,9},{2,10},{3,11},{4,12},{5,13},{6,14},{7,15},{8,0},{9,1},... | collective-permute-start | bytes 196616 | tf_op jit(solution)/shard_map/ppermute | solution.py:197
  30.2 5.4 %collective-permute-start.5 = (bf16[256,128]{1,0:T(8,128)(2,1)S(1)}, bf16[256,128]{1,0:T(8,128)(2,1)S(1)}, u32[]{:S(2)}, u32[]{:S(2)}) collective-permute-start(bf16[256,128]{1,0:T(8,128)(2,1)S(1)} %get-tuple-element.27.refs_0_), channel_id=1, source_target_pairs={{0,4},{1,5},{2,6},{3,7},{4,0},{5,1},{6,2},{7,3},{8,12},{9,13},{10,... | collective-permute-start | bytes 196616 | tf_op jit(solution)/shard_map/ppermute | solution.py:197
  35.6 6.6 %copy-start.7 = (f32[12]{0:T(128)S(1)}, f32[12]{0:T(128)}, u32[]{:S(2)}) copy-start(f32[12]{0:T(128)} %basis_width.1) | copy-start | bytes 148
  35.6 6.4 %collective-permute-start.8 = (bf16[1024,128]{1,0:T(8,128)(2,1)S(1)}, bf16[1024,128]{1,0:T(8,128)(2,1)S(1)}, u32[]{:S(2)}, u32[]{:S(2)}) collective-permute-start(bf16[1024,128]{1,0:T(8,128)(2,1)S(1)} %join.2.refs_0_), channel_id=1, source_target_pairs={{0,2},{1,3},{2,0},{3,1},{4,6},{5,7},{6,4},{7,5},{8,10},{9,11},{10,... | collective-permute-start | bytes 786440 | tf_op jit(solution)/shard_map/ppermute | solution.py:197
  42.1 2.0 %collective-permute-start.9 = (bf16[2048,128]{1,0:T(8,128)(2,1)S(1)}, bf16[2048,128]{1,0:T(8,128)(2,1)S(1)}, u32[]{:S(2)}, u32[]{:S(2)}) collective-permute-start(bf16[2048,128]{1,0:T(8,128)(2,1)S(1)} %join.3.near), channel_id=1, source_target_pairs={{0,1},{1,0},{2,3},{3,2},{4,5},{5,4},{6,7},{7,6},{8,9},{9,8},{10,11... | collective-permute-start | bytes 1572872 | tf_op jit(solution)/shard_map/ppermute | solution.py:197

commit v8 on v7

--- a/solution.py
+++ b/solution.py
@@ -79,8 +79,10 @@
     weight_in,
     index_in,
     coef_in,
-    keep,
-    send,
+    keep_near,
+    keep_far,
+    send_near,
+    send_far,
     picture,
     owner,
     slot,
@@ -165,69 +167,67 @@
                 piece = pl.ds(pl.multiple_of(starts[0, box], BH), BH)
                 total[piece, :] += scaled[down * BH : (down + 1) * BH, col * BW : (col + 1) * BW]
 
-    @pl.loop(0, peers // 2)
+    @pl.loop(0, peers // 4)
     def _(i):
         start = pl.multiple_of(i * chunk, PS)
-        for out, base in ((keep, 0), (send, peers // 2 * BOXES)):
-            source = pl.multiple_of(base + i * BOXES, BOXES)
+        for quarter, out in enumerate((keep_near, keep_far, send_near, send_far)):
+            source = pl.multiple_of((quarter * (peers // 4) + i) * BOXES, BOXES)
             out[pl.ds(start, BOXES), :] = total[pl.ds(source, BOXES), :].astype(jnp.bfloat16)
             out[pl.ds(start + BOXES, chunk - BOXES), :] = tags
 
 
-def add_kernel(parts, ours, theirs, *outs):
-    length = ours.shape[0] // parts
+def add_kernel(count, *refs):
+    parts, outs = refs[:count], refs[count:]
+    length = outs[0].shape[0]
     for i, out in enumerate(outs):
-        here = pl.ds(i * length, length)
-        out[...] = (ours[here, :].astype(jnp.float32) + theirs[here, :].astype(jnp.float32)).astype(jnp.bfloat16)
-
-
-def add_parts(ours, theirs, parts):
-    length = ours.shape[0] // parts
+        out[...] = summed_terms(parts, slice(i * length, (i + 1) * length)).astype(jnp.bfloat16)
+
+
+def add_parts(pieces, *parts):
+    length = parts[0].shape[0] // pieces
     return pl.pallas_call(
-        functools.partial(add_kernel, parts),
-        out_shape=[jax.ShapeDtypeStruct((length, BW), jnp.bfloat16)] * parts,
-        in_specs=[VMEM, VMEM],
-        out_specs=[VMEM] * parts,
+        functools.partial(add_kernel, len(parts)),
+        out_shape=[jax.ShapeDtypeStruct((length, BW), jnp.bfloat16)] * pieces,
+        in_specs=[VMEM] * len(parts),
+        out_specs=[VMEM] * pieces,
         compiler_params=params(),
         name="add_parts",
-    )(ours, theirs)
+    )(*parts)
 
 
 def swap(x, axis_size, bit):
     return lax.ppermute(x, "visit", [(i, i ^ bit) for i in range(axis_size)])
 
 
-def scatter_sum(keep, send, peers):
-    near = swap(send, peers, 1)
-    ours, theirs = add_parts(keep, near, 2)
-    near = swap(theirs, peers, 2)
-    terms = add_parts(ours, near, peers // 4)
+def scatter_sum(keep_near, keep_far, send_near, send_far, peers):
+    (beyond,) = add_parts(1, keep_far, swap(send_far, peers, 1))
+    terms = add_parts(peers // 4, keep_near, swap(send_near, peers, 1), swap(beyond, peers, 2))
     return [terms[0]] + [swap(terms[far], peers, 4 * far) for far in reversed(range(1, peers // 4))]
 
 
-def join_kernel(*refs):
-    *parts, out = refs
+def join_kernel(count, *refs):
+    parts, out = refs[:count], refs[-1]
     length = parts[0].shape[0]
     for i, part in enumerate(parts):
         out[i * length : (i + 1) * length, :] = part[...]
 
 
-def join(*parts):
+def join(*parts, before=()):
     rows, lanes = parts[0].shape
     return pl.pallas_call(
-        join_kernel,
+        functools.partial(join_kernel, len(parts)),
         out_shape=jax.ShapeDtypeStruct((rows * len(parts), lanes), parts[0].dtype),
-        in_specs=[VMEM] * len(parts),
+        in_specs=[VMEM] * len(parts) + [ANY] * len(before),
         out_specs=VMEM,
         compiler_params=params(),
         name="join",
-    )(*parts)
-
-
-def gather_slots(own, peers):
-    line = join(own, *[swap(own, peers, 4 * away) for away in range(1, peers // 4)])
-    pair = join(line, swap(line, peers, 2))
-    return pair, swap(pair, peers, 1)
+    )(*parts, *before)
+
+
+def gather_slots(own, peers, before):
+    line = join(*[own] + [swap(own, peers, 4 * away) for away in range(1, peers // 4)], before=before)
+    side = swap(line, peers, 2)
+    return line, side, swap(line, peers, 1), swap(side, peers, 1)
 
 
 def summed_terms(terms, here):
@@ -343,27 +343,21 @@
     bases,
     most,
     steps,
-    near,
-    other,
     across_bands,
     down_bands,
     coadd,
     weight_sum,
     spots,
     scales,
-    template,
-    out,
-    table,
-    window,
-    blurred,
-    matched,
+    *refs,
 ):
+    pieces, (template, out, table, window, blurred, matched) = refs[:4], refs[4:]
     groups = pl.cdiv(most, GROUP)
     high = GROUP * TALL
-    half = near.shape[0]
-    table[0:half, :] = near[...]
-    table[half : 2 * half, :] = other[...]
-    table[2 * half :, :] = jnp.zeros((BH, BW), jnp.bfloat16)
+    length = pieces[0].shape[0]
+    for i, piece in enumerate(pieces):
+        table[i * length : (i + 1) * length, :] = piece[...]
+    table[4 * length :, :] = jnp.zeros((BH, BW), jnp.bfloat16)
     matched[...] = jnp.zeros_like(matched)
     template[...] = coadd[...].astype(jnp.bfloat16)
     if most % GROUP:
@@ -441,12 +435,12 @@
     chunk = CHUNK
     owner = box_owner.reshape(1, -1)
 
-    half = jax.ShapeDtypeStruct((peers // 2 * chunk, BW), jnp.bfloat16)
-    keep, send = pl.pallas_call(
+    quarter = jax.ShapeDtypeStruct((peers // 4 * chunk, BW), jnp.bfloat16)
+    sums = pl.pallas_call(
         functools.partial(warp_kernel, peers, bases),
-        out_shape=[half, half],
+        out_shape=[quarter] * 4,
         in_specs=[SMEM] + [ANY] * 8,
-        out_specs=[VMEM] * 2,
+        out_specs=[VMEM] * 4,
         scratch_shapes=[
             pltpu.VMEM((rows, width), jnp.bfloat16),
             pltpu.VMEM(owner.shape, jnp.int32),
@@ -488,7 +482,7 @@
         name="gauss_bands",
     )(basis_width)
 
-    terms = scatter_sum(keep, send, peers)
+    terms = scatter_sum(*sums, peers)
     leaning, coadd, weight_sum = pl.pallas_call(
         functools.partial(template_kernel, peers, bases),
         out_shape=[
@@ -501,7 +495,6 @@
         compiler_params=params(),
         name="template",
     )(me, *terms)
-    near, other = gather_slots(leaning, peers)
     spots, scales = pl.pallas_call(
         functools.partial(plan_kernel, peers, bases, most, rows // BH),
         out_shape=[
@@ -514,6 +507,7 @@
         name="plan",
     )(me, *terms)
 
+    pieces = gather_slots(leaning, peers, (across_bands, spots))
     steps = min(peers, 16)
     tall = steps * pl.cdiv(most, GROUP) * GROUP * TALL
     template, difference_coadd = pl.pallas_call(
@@ -522,7 +516,7 @@
             jax.ShapeDtypeStruct((BOXES, BW), jnp.bfloat16),
             jax.ShapeDtypeStruct((BOXES, BW), jnp.float32),
         ],
-        in_specs=[VMEM] * 6 + [SMEM] * 2,
+        in_specs=[VMEM] * 4 + [SMEM] * 2 + [VMEM] * 4,
         out_specs=[VMEM] * 2,
         scratch_shapes=[
             pltpu.VMEM(((peers * PS + 1) * BH, BW), jnp.bfloat16),
@@ -532,7 +526,7 @@
         ],
         compiler_params=params(),
         name="match",
-    )(near, other, across_bands, down_bands, coadd, weight_sum, spots, scales)
+    )(across_bands, down_bands, coadd, weight_sum, spots, scales, *pieces)
     return (template.reshape(PS, BH, BW), difference_coadd.reshape(PS, BH, BW))
 
 

time: 52.7 us -> 51.7 us (0.981)
  waiting for transfers between devices: 21.9 us -> 21 us
    ppermute x10 -> x12, waiting for transfers between devices: 21.9 us -> 21 us  [swap(): return lax.ppermute(x, 'visit', [(i, i ^ bit) for i in range(axis_size)])]
    pallas_call x5 -> x4, Pallas kernels: 2.77 us -> 2.7 us  [the longest x1 2.5 us: shards(): pl.pallas_call(functools.partial(warp_kernel, peers, bases), out_shape=[q...]
    ppermute x10 -> x12, starting transfers between devices: 14.1 us -> 14.1 us  [swap(): return lax.ppermute(x, 'visit', [(i, i ^ bit) for i in range(axis_size)])]
  transfers between devices with their start and end apart: 10 -> 12, of which waited for: 8 -> 9; matrix products, arithmetic and copies ran while one was open for 0% -> 0% of each run, Pallas kernels for 3% -> 4%
where the time goes in v8:
time: 51.7 us; the launch traced here: 51.5 us
  waiting for transfers between devices  21 us (41%)
  starting transfers between devices  14.1 us (27%)
  Pallas kernels  13.2 us (26%)
  local copies, waits for them, and re-layouts  1.73 us (3%)
  between operations  1.4 us (3%)
    ppermute x12, waiting for transfers between devices, swap(): return lax.ppermute(x, 'visit', [(i, i ^ bit) for i in range(axis_size)])  21 us
    ppermute x12, starting transfers between devices, swap(): return lax.ppermute(x, 'visit', [(i, i ^ bit) for i in range(axis_size)])  14.1 us
    pallas_call x1, Pallas kernels, shards(): pl.pallas_call(functools.partial(match_kernel, peers, bases, most, steps)...  8.38 us
    pallas_call x1, Pallas kernels, shards(): pl.pallas_call(functools.partial(warp_kernel, peers, bases), out_shape=[q...  2.5 us
    unnamed x16, local copies, waits for them, and re-layouts  1.73 us
    pallas_call x1, Pallas kernels, shards(): pl.pallas_call(gauss_kernel, out_shape=[jax.ShapeDtypeStruct((table_size,...  1.25 us
  transfers between devices with their start and end apart: 12, of which 9 were waited for; matrix products, arithmetic and copies ran while one was open for 0% of the time, Pallas kernels for 4%

profile of v8, /device:TPU:0, one launch (start us, length us, event | category | flops | bytes accessed | tf_op | source)
XLA Modules:
  0.0 51.5 jit_solution(8940615602248353932)
XLA Ops:
  1.3 0.6 %copy-done.4 = f32[1,2]{1,0:T(1,128)S(1)} copy-done((f32[1,2]{1,0:T(1,128)S(1)}, f32[1,2]{1,0:T(1,128)}, u32[]{:S(2)}) %copy-start.4) | copy-done | bytes 32
  1.9 0.0 copy-done.5
  2.0 0.0 copy-done.6
  2.0 0.0 copy-done.1
  2.0 0.0 copy-done.2
  2.0 0.0 copy-done.3
  2.0 1.0 %copy-done = bf16[1,256,1024]{2,1,0:T(8,128)(2,1)S(1)} copy-done((bf16[1,256,1024]{2,1,0:T(8,128)(2,1)S(1)}, bf16[1,256,1024]{2,1,0:T(8,128)(2,1)}, u32[]{:S(2)}) %copy-start) | copy-done | bytes 524312
  3.1 2.5 %warp.1 = (bf16[1088,128]{1,0:T(8,128)(2,1)S(1)}, bf16[1088,128]{1,0:T(8,128)(2,1)S(1)}, bf16[1088,128]{1,0:T(8,128)(2,1)S(1)}, bf16[1088,128]{1,0:T(8,128)(2,1)S(1)}) custom-call(s32[1]{0:T(128)} %bitcast.me_ref, bf16[256,1024]{1,0:T(8,128)(2,1)S(1)} %bitcast.7, s32[1,128]{1,0:T(1,128)S(1)} %bitcast.8, s32[1,128]{1,0:T(1,128)S(1)} %copy-done.2, ...), custom_call_target="tpu_custom_call" | custom-call | tf_op jit(solution)/shard_map/warp/pallas_call | solution.py:439
  5.6 0.5 %collective-permute-start.1 = (bf16[1088,128]{1,0:T(8,128)(2,1)S(1)}, bf16[1088,128]{1,0:T(8,128)(2,1)S(1)}, u32[]{:S(2)}, u32[]{:S(2)}) collective-permute-start(bf16[1088,128]{1,0:T(8,128)(2,1)S(1)} %get-tuple-element.24), channel_id=1, source_target_pairs={{0,1},{1,0},{2,3},{3,2},{4,5},{5,4},{6,7},{7,6},{8,9},{9,8},{10,11... | collective-permute-start | bytes 835592 | tf_op jit(solution)/shard_map/ppermute | solution.py:199
  6.1 0.1 collective-permute-start
  6.2 1.1 %collective-permute-done.1.refs_1_ = bf16[1088,128]{1,0:T(8,128)(2,1)S(1)} collective-permute-done((bf16[1088,128]{1,0:T(8,128)(2,1)S(1)}, bf16[1088,128]{1,0:T(8,128)(2,1)S(1)}, u32[]{:S(2)}, u32[]{:S(2)}) %collective-permute-start.1) | collective-permute-done | bytes 278560 | tf_op jit(solution)/shard_map/ppermute | solution.py:199
  7.3 0.1 add_parts.2
  7.4 3.0 %collective-permute-start.2 = (bf16[1088,128]{1,0:T(8,128)(2,1)S(1)}, bf16[1088,128]{1,0:T(8,128)(2,1)S(1)}, u32[]{:S(2)}, u32[]{:S(2)}) collective-permute-start(bf16[1088,128]{1,0:T(8,128)(2,1)S(1)} %add_parts.2), channel_id=1, source_target_pairs={{0,2},{1,3},{2,0},{3,1},{4,6},{5,7},{6,4},{7,5},{8,10},{9,11},{10,... | collective-permute-start | bytes 835592 | tf_op jit(solution)/shard_map/ppermute | solution.py:199
  10.3 7.0 %collective-permute-done.2.refs_2_ = bf16[1088,128]{1,0:T(8,128)(2,1)S(1)} collective-permute-done((bf16[1088,128]{1,0:T(8,128)(2,1)S(1)}, bf16[1088,128]{1,0:T(8,128)(2,1)S(1)}, u32[]{:S(2)}, u32[]{:S(2)}) %collective-permute-start.2) | collective-permute-done | bytes 278560 | tf_op jit(solution)/shard_map/ppermute | solution.py:199
  17.3 0.1 add_parts.3
  17.4 3.9 %collective-permute-start.3 = (bf16[272,128]{1,0:T(8,128)(2,1)S(1)}, bf16[272,128]{1,0:T(8,128)(2,1)S(1)}, u32[]{:S(2)}, u32[]{:S(2)}) collective-permute-start(bf16[272,128]{1,0:T(8,128)(2,1)S(1)} %get-tuple-element.26), channel_id=1, source_target_pairs={{0,12},{1,13},{2,14},{3,15},{4,8},{5,9},{6,10},{7,11},{8,4},{9,5},... | collective-permute-start | bytes 208904 | tf_op jit(solution)/shard_map/ppermute | solution.py:199
  21.3 0.6 %collective-permute-start.5 = (bf16[272,128]{1,0:T(8,128)(2,1)S(1)}, bf16[272,128]{1,0:T(8,128)(2,1)S(1)}, u32[]{:S(2)}, u32[]{:S(2)}) collective-permute-start(bf16[272,128]{1,0:T(8,128)(2,1)S(1)} %get-tuple-element.28), channel_id=1, source_target_pairs={{0,4},{1,5},{2,6},{3,7},{4,0},{5,1},{6,2},{7,3},{8,12},{9,13},{10,... | collective-permute-start | bytes 208904 | tf_op jit(solution)/shard_map/ppermute | solution.py:199
  21.9 2.5 %collective-permute-done.3.refs_1_ = bf16[272,128]{1,0:T(8,128)(2,1)S(1)} collective-permute-done((bf16[272,128]{1,0:T(8,128)(2,1)S(1)}, bf16[272,128]{1,0:T(8,128)(2,1)S(1)}, u32[]{:S(2)}, u32[]{:S(2)}) %collective-permute-start.3) | collective-permute-done | bytes 69664 | tf_op jit(solution)/shard_map/ppermute | solution.py:199
  24.4 2.4 %collective-permute-done.4.refs_2_ = bf16[272,128]{1,0:T(8,128)(2,1)S(1)} collective-permute-done((bf16[272,128]{1,0:T(8,128)(2,1)S(1)}, bf16[272,128]{1,0:T(8,128)(2,1)S(1)}, u32[]{:S(2)}, u32[]{:S(2)}) %collective-permute-start.4) | collective-permute-done | bytes 69664 | tf_op jit(solution)/shard_map/ppermute | solution.py:199
  26.8 0.1 collective-permute-done.5.refs_3_
  26.8 0.3 template.1
  27.2 0.0 copy-start.7
  27.2 2.6 %collective-permute-start.8 = (bf16[256,128]{1,0:T(8,128)(2,1)S(1)}, bf16[256,128]{1,0:T(8,128)(2,1)S(1)}, u32[]{:S(2)}, u32[]{:S(2)}) collective-permute-start(bf16[256,128]{1,0:T(8,128)(2,1)S(1)} %get-tuple-element.33.refs_0_), channel_id=1, source_target_pairs={{0,12},{1,13},{2,14},{3,15},{4,8},{5,9},{6,10},{7,11},{8,4},{9,5},... | collective-permute-start | bytes 196616 | tf_op jit(solution)/shard_map/ppermute | solution.py:199
  29.8 1.8 %collective-permute-start.6 = (bf16[256,128]{1,0:T(8,128)(2,1)S(1)}, bf16[256,128]{1,0:T(8,128)(2,1)S(1)}, u32[]{:S(2)}, u32[]{:S(2)}) collective-permute-start(bf16[256,128]{1,0:T(8,128)(2,1)S(1)} %get-tuple-element.33.refs_0_), channel_id=1, source_target_pairs={{0,4},{1,5},{2,6},{3,7},{4,0},{5,1},{6,2},{7,3},{8,12},{9,13},{10,... | collective-permute-start | bytes 196616 | tf_op jit(solution)/shard_map/ppermute | solution.py:199
  31.6 1.3 %gauss_bands.1 = (bf16[12,256,128]{2,1,0:T(8,128)(2,1)S(1)}, bf16[12,128,256]{2,1,0:T(8,128)(2,1)S(1)}) custom-call(f32[12]{0:T(128)S(1)} %copy-done.7), custom_call_target="tpu_custom_call" | custom-call | tf_op jit(solution)/shard_map/gauss_bands/pallas_call | solution.py:473
  32.9 0.6 %plan.1 = (s32[32,128]{1,0:T(8,128)S(1)}, f32[16,128]{1,0:T(8,128)S(1)}) custom-call(s32[1]{0:T(128)} %bitcast.me_ref, bf16[272,128]{1,0:T(8,128)(2,1)S(1)} %get-tuple-element.25.refs_0_, bf16[272,128]{1,0:T(8,128)(2,1)S(1)} %collective-permute-done.3.refs_1_, bf16[272,128]{1,0:T(8,128)(2,1)S(1)} %collective-permute-done.4.refs_2_, ...), custom_call_target="tpu_custom_call" | custom-call | tf_op jit(solution)/shard_map/plan/pallas_call | solution.py:498
  33.5 0.4 collective-permute-done.8.refs_3_
  33.9 1.3 %collective-permute-done.7.refs_2_ = bf16[256,128]{1,0:T(8,128)(2,1)S(1)} collective-permute-done((bf16[256,128]{1,0:T(8,128)(2,1)S(1)}, bf16[256,128]{1,0:T(8,128)(2,1)S(1)}, u32[]{:S(2)}, u32[]{:S(2)}) %collective-permute-start.7) | collective-permute-done | bytes 65568 | tf_op jit(solution)/shard_map/ppermute | solution.py:199
  35.2 1.6 %collective-permute-start.9 = (bf16[1024,128]{1,0:T(8,128)(2,1)S(1)}, bf16[1024,128]{1,0:T(8,128)(2,1)S(1)}, u32[]{:S(2)}, u32[]{:S(2)}) collective-permute-start(bf16[1024,128]{1,0:T(8,128)(2,1)S(1)} %join.1.refs_0_), channel_id=1, source_target_pairs={{0,2},{1,3},{2,0},{3,1},{4,6},{5,7},{6,4},{7,5},{8,10},{9,11},{10,... | collective-permute-start | bytes 786440 | tf_op jit(solution)/shard_map/ppermute | solution.py:199
  36.8 4.8 %collective-permute-done.9.refs_1_ = bf16[1024,128]{1,0:T(8,128)(2,1)S(1)} collective-permute-done((bf16[1024,128]{1,0:T(8,128)(2,1)S(1)}, bf16[1024,128]{1,0:T(8,128)(2,1)S(1)}, u32[]{:S(2)}, u32[]{:S(2)}) %collective-permute-start.9) | collective-permute-done | bytes 262176 | tf_op jit(solution)/shard_map/ppermute | solution.py:199
  41.6 1.5 %collective-permute-done.11.refs_3_ = bf16[1024,128]{1,0:T(8,128)(2,1)S(1)} collective-permute-done((bf16[1024,128]{1,0:T(8,128)(2,1)S(1)}, bf16[1024,128]{1,0:T(8,128)(2,1)S(1)}, u32[]{:S(2)}, u32[]{:S(2)}) %collective-permute-start.11) | collective-permute-done | bytes 262176 | tf_op jit(solution)/shard_map/ppermute | solution.py:199
  43.2 8.4 %match.1 = (bf16[256,128]{1,0:T(8,128)(2,1)}, f32[256,128]{1,0:T(8,128)}) custom-call(bf16[12,256,128]{2,1,0:T(8,128)(2,1)S(1)} %get-tuple-element.19.refs_4_.across_bands, bf16[12,128,256]{2,1,0:T(8,128)(2,1)S(1)} %get-tuple-element.20.down_bands, f32[256,128]{1,0:T(8,128)S(1)} %get-tuple-element.29.coadd, f32[16,128]{1,0:T(8,128)S(1)} %get-tuple-element.30.weight_sum, ...), custom_call_target="tpu_custom_call" | custom-call | tf_op jit(solution)/shard_map/match/pallas_call | solution.py:513
  (16 shorter events, 0.1 us)
Async XLA Ops:
  1.3 0.7 %copy-start.4 = (f32[1,2]{1,0:T(1,128)S(1)}, f32[1,2]{1,0:T(1,128)}, u32[]{:S(2)}) copy-start(f32[1,2]{1,0:T(1,128)} %fraction_in.1) | copy-start | bytes 28
  1.3 0.7 %copy-start.5 = (s32[1,6]{1,0:T(1,128)S(1)}, s32[1,6]{1,0:T(1,128)}, u32[]{:S(2)}) copy-start(s32[1,6]{1,0:T(1,128)} %index_in.1) | copy-start | bytes 76
  1.3 0.7 %copy-start.6 = (f32[1,6]{1,0:T(1,128)S(1)}, f32[1,6]{1,0:T(1,128)}, u32[]{:S(2)}) copy-start(f32[1,6]{1,0:T(1,128)} %coef_in.1) | copy-start | bytes 76
  1.3 0.7 %copy-start.1 = (s32[1,128,1]{1,2,0:T(1,128)S(1)}, s32[1,128,1]{1,2,0:T(1,128)}, u32[]{:S(2)}) copy-start(s32[1,128,1]{1,2,0:T(1,128)} %param.13) | copy-start | bytes 1540
  1.3 0.7 %copy-start.2 = (s32[1,128]{1,0:T(1,128)S(1)}, s32[1,128]{1,0:T(1,128)}, u32[]{:S(2)}) copy-start(s32[1,128]{1,0:T(1,128)} %slot_in.1) | copy-start | bytes 1540
  1.3 0.7 %copy-start.3 = (s32[1,2]{1,0:T(1,128)S(1)}, s32[1,2]{1,0:T(1,128)}, u32[]{:S(2)}) copy-start(s32[1,2]{1,0:T(1,128)} %offset_in.1) | copy-start | bytes 28
  2.0 1.0 %copy-start = (bf16[1,256,1024]{2,1,0:T(8,128)(2,1)S(1)}, bf16[1,256,1024]{2,1,0:T(8,128)(2,1)}, u32[]{:S(2)}) copy-start(bf16[1,256,1024]{2,1,0:T(8,128)(2,1)} %param.9) | copy-start | bytes 1572868
  5.6 1.7 %collective-permute-start.1 = (bf16[1088,128]{1,0:T(8,128)(2,1)S(1)}, bf16[1088,128]{1,0:T(8,128)(2,1)S(1)}, u32[]{:S(2)}, u32[]{:S(2)}) collective-permute-start(bf16[1088,128]{1,0:T(8,128)(2,1)S(1)} %get-tuple-element.24), channel_id=1, source_target_pairs={{0,1},{1,0},{2,3},{3,2},{4,5},{5,4},{6,7},{7,6},{8,9},{9,8},{10,11... | collective-permute-start | bytes 835592 | tf_op jit(solution)/shard_map/ppermute | solution.py:199
  6.1 4.2 %collective-permute-start = (bf16[1088,128]{1,0:T(8,128)(2,1)S(1)}, bf16[1088,128]{1,0:T(8,128)(2,1)S(1)}, u32[]{:S(2)}, u32[]{:S(2)}) collective-permute-start(bf16[1088,128]{1,0:T(8,128)(2,1)S(1)} %get-tuple-element.22), channel_id=1, source_target_pairs={{0,1},{1,0},{2,3},{3,2},{4,5},{5,4},{6,7},{7,6},{8,9},{9,8},{10,11... | collective-permute-start | bytes 835592 | tf_op jit(solution)/shard_map/ppermute | solution.py:199
  7.4 9.9 %collective-permute-start.2 = (bf16[1088,128]{1,0:T(8,128)(2,1)S(1)}, bf16[1088,128]{1,0:T(8,128)(2,1)S(1)}, u32[]{:S(2)}, u32[]{:S(2)}) collective-permute-start(bf16[1088,128]{1,0:T(8,128)(2,1)S(1)} %add_parts.2), channel_id=1, source_target_pairs={{0,2},{1,3},{2,0},{3,1},{4,6},{5,7},{6,4},{7,5},{8,10},{9,11},{10,... | collective-permute-start | bytes 835592 | tf_op jit(solution)/shard_map/ppermute | solution.py:199
  17.4 7.0 %collective-permute-start.3 = (bf16[272,128]{1,0:T(8,128)(2,1)S(1)}, bf16[272,128]{1,0:T(8,128)(2,1)S(1)}, u32[]{:S(2)}, u32[]{:S(2)}) collective-permute-start(bf16[272,128]{1,0:T(8,128)(2,1)S(1)} %get-tuple-element.26), channel_id=1, source_target_pairs={{0,12},{1,13},{2,14},{3,15},{4,8},{5,9},{6,10},{7,11},{8,4},{9,5},... | collective-permute-start | bytes 208904 | tf_op jit(solution)/shard_map/ppermute | solution.py:199
  21.3 5.5 %collective-permute-start.4 = (bf16[272,128]{1,0:T(8,128)(2,1)S(1)}, bf16[272,128]{1,0:T(8,128)(2,1)S(1)}, u32[]{:S(2)}, u32[]{:S(2)}) collective-permute-start(bf16[272,128]{1,0:T(8,128)(2,1)S(1)} %get-tuple-element.27), channel_id=1, source_target_pairs={{0,8},{1,9},{2,10},{3,11},{4,12},{5,13},{6,14},{7,15},{8,0},{9,1},... | collective-permute-start | bytes 208904 | tf_op jit(solution)/shard_map/ppermute | solution.py:199
  21.3 5.6 %collective-permute-start.5 = (bf16[272,128]{1,0:T(8,128)(2,1)S(1)}, bf16[272,128]{1,0:T(8,128)(2,1)S(1)}, u32[]{:S(2)}, u32[]{:S(2)}) collective-permute-start(bf16[272,128]{1,0:T(8,128)(2,1)S(1)} %get-tuple-element.28), channel_id=1, source_target_pairs={{0,4},{1,5},{2,6},{3,7},{4,0},{5,1},{6,2},{7,3},{8,12},{9,13},{10,... | collective-permute-start | bytes 208904 | tf_op jit(solution)/shard_map/ppermute | solution.py:199
  27.2 4.5 %copy-start.7 = (f32[12]{0:T(128)S(1)}, f32[12]{0:T(128)}, u32[]{:S(2)}) copy-start(f32[12]{0:T(128)} %basis_width.1) | copy-start | bytes 148
  27.2 6.7 %collective-permute-start.8 = (bf16[256,128]{1,0:T(8,128)(2,1)S(1)}, bf16[256,128]{1,0:T(8,128)(2,1)S(1)}, u32[]{:S(2)}, u32[]{:S(2)}) collective-permute-start(bf16[256,128]{1,0:T(8,128)(2,1)S(1)} %get-tuple-element.33.refs_0_), channel_id=1, source_target_pairs={{0,12},{1,13},{2,14},{3,15},{4,8},{5,9},{6,10},{7,11},{8,4},{9,5},... | collective-permute-start | bytes 196616 | tf_op jit(solution)/shard_map/ppermute | solution.py:199
  29.8 5.4 %collective-permute-start.7 = (bf16[256,128]{1,0:T(8,128)(2,1)S(1)}, bf16[256,128]{1,0:T(8,128)(2,1)S(1)}, u32[]{:S(2)}, u32[]{:S(2)}) collective-permute-start(bf16[256,128]{1,0:T(8,128)(2,1)S(1)} %get-tuple-element.33.refs_0_), channel_id=1, source_target_pairs={{0,8},{1,9},{2,10},{3,11},{4,12},{5,13},{6,14},{7,15},{8,0},{9,1},... | collective-permute-start | bytes 196616 | tf_op jit(solution)/shard_map/ppermute | solution.py:199
  29.8 5.4 %collective-permute-start.6 = (bf16[256,128]{1,0:T(8,128)(2,1)S(1)}, bf16[256,128]{1,0:T(8,128)(2,1)S(1)}, u32[]{:S(2)}, u32[]{:S(2)}) collective-permute-start(bf16[256,128]{1,0:T(8,128)(2,1)S(1)} %get-tuple-element.33.refs_0_), channel_id=1, source_target_pairs={{0,4},{1,5},{2,6},{3,7},{4,0},{5,1},{6,2},{7,3},{8,12},{9,13},{10,... | collective-permute-start | bytes 196616 | tf_op jit(solution)/shard_map/ppermute | solution.py:199
  35.2 6.4 %collective-permute-start.9 = (bf16[1024,128]{1,0:T(8,128)(2,1)S(1)}, bf16[1024,128]{1,0:T(8,128)(2,1)S(1)}, u32[]{:S(2)}, u32[]{:S(2)}) collective-permute-start(bf16[1024,128]{1,0:T(8,128)(2,1)S(1)} %join.1.refs_0_), channel_id=1, source_target_pairs={{0,2},{1,3},{2,0},{3,1},{4,6},{5,7},{6,4},{7,5},{8,10},{9,11},{10,... | collective-permute-start | bytes 786440 | tf_op jit(solution)/shard_map/ppermute | solution.py:199
  36.8 4.8 %collective-permute-start.10 = (bf16[1024,128]{1,0:T(8,128)(2,1)S(1)}, bf16[1024,128]{1,0:T(8,128)(2,1)S(1)}, u32[]{:S(2)}, u32[]{:S(2)}) collective-permute-start(bf16[1024,128]{1,0:T(8,128)(2,1)S(1)} %join.1.refs_0_), channel_id=1, source_target_pairs={{0,1},{1,0},{2,3},{3,2},{4,5},{5,4},{6,7},{7,6},{8,9},{9,8},{10,11... | collective-permute-start | bytes 786440 | tf_op jit(solution)/shard_map/ppermute | solution.py:199
  41.6 1.5 %collective-permute-start.11 = (bf16[1024,128]{1,0:T(8,128)(2,1)S(1)}, bf16[1024,128]{1,0:T(8,128)(2,1)S(1)}, u32[]{:S(2)}, u32[]{:S(2)}) collective-permute-start(bf16[1024,128]{1,0:T(8,128)(2,1)S(1)} %collective-permute-done.9.refs_1_), channel_id=1, source_target_pairs={{0,1},{1,0},{2,3},{3,2},{4,5},{5,4},{6,7},{7,6},{8,9},{9,8},{10,11... | collective-permute-start | bytes 786440 | tf_op jit(solution)/shard_map/ppermute | solution.py:199

commit v9 on v8

--- a/solution.py
+++ b/solution.py
@@ -225,8 +225,14 @@
 
 
 def gather_slots(own, peers, before):
-    line = join(*[own] + [swap(own, peers, 4 * away) for away in range(1, peers // 4)], before=before)
-    side = swap(line, peers, 2)
+    count = peers // 8
+    far = {away: swap(own, peers, 4 * away) for away in reversed(range(1, peers // 4))}
+    high = join(*[far[away] for away in range(count, 2 * count)], before=before)
+    high_side = swap(high, peers, 2)
+    low = join(own, *[far[away] for away in range(1, count)])
+    low_side = swap(low, peers, 2)
+    line = join(low, high)
+    side = join(low_side, high_side)
     return line, side, swap(line, peers, 1), swap(side, peers, 1)
 
 

time: 51.7 us -> 51.4 us (level)
  waiting for transfers between devices: 21 us -> 19.9 us
  starting transfers between devices: 14.1 us -> 15 us
    ppermute x12 -> x13, waiting for transfers between devices: 21 us -> 19.9 us  [swap(): return lax.ppermute(x, 'visit', [(i, i ^ bit) for i in range(axis_size)])]
    ppermute x12 -> x13, starting transfers between devices: 14.1 us -> 15 us  [swap(): return lax.ppermute(x, 'visit', [(i, i ^ bit) for i in range(axis_size)])]
  transfers between devices with their start and end apart: 12 -> 13, of which waited for: 9 -> 10; matrix products, arithmetic and copies ran while one was open for 0% -> 0% of each run, Pallas kernels for 4% -> 4%
where the time goes in v9:
time: 51.4 us; the launch traced here: 51.2 us
  waiting for transfers between devices  19.9 us (39%)
  starting transfers between devices  15 us (29%)
  Pallas kernels  13.2 us (26%)
  local copies, waits for them, and re-layouts  1.73 us (3%)
  between operations  1.44 us (3%)
    ppermute x13, waiting for transfers between devices, swap(): return lax.ppermute(x, 'visit', [(i, i ^ bit) for i in range(axis_size)])  19.9 us
    ppermute x13, starting transfers between devices, swap(): return lax.ppermute(x, 'visit', [(i, i ^ bit) for i in range(axis_size)])  15 us
    pallas_call x1, Pallas kernels, shards(): pl.pallas_call(functools.partial(match_kernel, peers, bases, most, steps)...  8.31 us
    pallas_call x1, Pallas kernels, shards(): pl.pallas_call(functools.partial(warp_kernel, peers, bases), out_shape=[q...  2.5 us
    unnamed x16, local copies, waits for them, and re-layouts  1.73 us
    pallas_call x1, Pallas kernels, shards(): pl.pallas_call(gauss_kernel, out_shape=[jax.ShapeDtypeStruct((table_size,...  1.25 us
  transfers between devices with their start and end apart: 13, of which 10 were waited for; matrix products, arithmetic and copies ran while one was open for 0% of the time, Pallas kernels for 4%

profile of v9, /device:TPU:0, one launch (start us, length us, event | category | flops | bytes accessed | tf_op | source)
XLA Modules:
  0.0 51.2 jit_solution(17674273133168805464)
XLA Ops:
  1.3 0.6 %copy-done.4 = f32[1,2]{1,0:T(1,128)S(1)} copy-done((f32[1,2]{1,0:T(1,128)S(1)}, f32[1,2]{1,0:T(1,128)}, u32[]{:S(2)}) %copy-start.4) | copy-done | bytes 32
  1.9 0.0 copy-done.5
  2.0 1.0 %copy-done = bf16[1,256,1024]{2,1,0:T(8,128)(2,1)S(1)} copy-done((bf16[1,256,1024]{2,1,0:T(8,128)(2,1)S(1)}, bf16[1,256,1024]{2,1,0:T(8,128)(2,1)}, u32[]{:S(2)}) %copy-start) | copy-done | bytes 524312
  3.1 2.5 %warp.1 = (bf16[1088,128]{1,0:T(8,128)(2,1)S(1)}, bf16[1088,128]{1,0:T(8,128)(2,1)S(1)}, bf16[1088,128]{1,0:T(8,128)(2,1)S(1)}, bf16[1088,128]{1,0:T(8,128)(2,1)S(1)}) custom-call(s32[1]{0:T(128)} %bitcast.me_ref, bf16[256,1024]{1,0:T(8,128)(2,1)S(1)} %bitcast.7, s32[1,128]{1,0:T(1,128)S(1)} %bitcast.8, s32[1,128]{1,0:T(1,128)S(1)} %copy-done.2, ...), custom_call_target="tpu_custom_call" | custom-call | tf_op jit(solution)/shard_map/warp/pallas_call | solution.py:445
  5.6 0.5 %collective-permute-start.1 = (bf16[1088,128]{1,0:T(8,128)(2,1)S(1)}, bf16[1088,128]{1,0:T(8,128)(2,1)S(1)}, u32[]{:S(2)}, u32[]{:S(2)}) collective-permute-start(bf16[1088,128]{1,0:T(8,128)(2,1)S(1)} %get-tuple-element.24), channel_id=1, source_target_pairs={{0,1},{1,0},{2,3},{3,2},{4,5},{5,4},{6,7},{7,6},{8,9},{9,8},{10,11... | collective-permute-start | bytes 835592 | tf_op jit(solution)/shard_map/ppermute | solution.py:199
  6.1 0.1 collective-permute-start
  6.2 1.1 %collective-permute-done.1.refs_1_ = bf16[1088,128]{1,0:T(8,128)(2,1)S(1)} collective-permute-done((bf16[1088,128]{1,0:T(8,128)(2,1)S(1)}, bf16[1088,128]{1,0:T(8,128)(2,1)S(1)}, u32[]{:S(2)}, u32[]{:S(2)}) %collective-permute-start.1) | collective-permute-done | bytes 278560 | tf_op jit(solution)/shard_map/ppermute | solution.py:199
  7.3 0.1 add_parts.2
  7.4 3.0 %collective-permute-start.2 = (bf16[1088,128]{1,0:T(8,128)(2,1)S(1)}, bf16[1088,128]{1,0:T(8,128)(2,1)S(1)}, u32[]{:S(2)}, u32[]{:S(2)}) collective-permute-start(bf16[1088,128]{1,0:T(8,128)(2,1)S(1)} %add_parts.2), channel_id=1, source_target_pairs={{0,2},{1,3},{2,0},{3,1},{4,6},{5,7},{6,4},{7,5},{8,10},{9,11},{10,... | collective-permute-start | bytes 835592 | tf_op jit(solution)/shard_map/ppermute | solution.py:199
  10.3 7.0 %collective-permute-done.2.refs_2_ = bf16[1088,128]{1,0:T(8,128)(2,1)S(1)} collective-permute-done((bf16[1088,128]{1,0:T(8,128)(2,1)S(1)}, bf16[1088,128]{1,0:T(8,128)(2,1)S(1)}, u32[]{:S(2)}, u32[]{:S(2)}) %collective-permute-start.2) | collective-permute-done | bytes 278560 | tf_op jit(solution)/shard_map/ppermute | solution.py:199
  17.3 0.1 add_parts.3
  17.4 3.9 %collective-permute-start.3 = (bf16[272,128]{1,0:T(8,128)(2,1)S(1)}, bf16[272,128]{1,0:T(8,128)(2,1)S(1)}, u32[]{:S(2)}, u32[]{:S(2)}) collective-permute-start(bf16[272,128]{1,0:T(8,128)(2,1)S(1)} %get-tuple-element.26), channel_id=1, source_target_pairs={{0,12},{1,13},{2,14},{3,15},{4,8},{5,9},{6,10},{7,11},{8,4},{9,5},... | collective-permute-start | bytes 208904 | tf_op jit(solution)/shard_map/ppermute | solution.py:199
  21.3 0.6 %collective-permute-start.5 = (bf16[272,128]{1,0:T(8,128)(2,1)S(1)}, bf16[272,128]{1,0:T(8,128)(2,1)S(1)}, u32[]{:S(2)}, u32[]{:S(2)}) collective-permute-start(bf16[272,128]{1,0:T(8,128)(2,1)S(1)} %get-tuple-element.28), channel_id=1, source_target_pairs={{0,4},{1,5},{2,6},{3,7},{4,0},{5,1},{6,2},{7,3},{8,12},{9,13},{10,... | collective-permute-start | bytes 208904 | tf_op jit(solution)/shard_map/ppermute | solution.py:199
  21.9 2.5 %collective-permute-done.3.refs_1_ = bf16[272,128]{1,0:T(8,128)(2,1)S(1)} collective-permute-done((bf16[272,128]{1,0:T(8,128)(2,1)S(1)}, bf16[272,128]{1,0:T(8,128)(2,1)S(1)}, u32[]{:S(2)}, u32[]{:S(2)}) %collective-permute-start.3) | collective-permute-done | bytes 69664 | tf_op jit(solution)/shard_map/ppermute | solution.py:199
  24.4 2.4 %collective-permute-done.4.refs_2_ = bf16[272,128]{1,0:T(8,128)(2,1)S(1)} collective-permute-done((bf16[272,128]{1,0:T(8,128)(2,1)S(1)}, bf16[272,128]{1,0:T(8,128)(2,1)S(1)}, u32[]{:S(2)}, u32[]{:S(2)}) %collective-permute-start.4) | collective-permute-done | bytes 69664 | tf_op jit(solution)/shard_map/ppermute | solution.py:199
  26.8 0.1 collective-permute-done.5.refs_3_
  26.8 0.3 template.1
  27.2 0.9 %collective-permute-start.6 = (bf16[256,128]{1,0:T(8,128)(2,1)S(1)}, bf16[256,128]{1,0:T(8,128)(2,1)S(1)}, u32[]{:S(2)}, u32[]{:S(2)}) collective-permute-start(bf16[256,128]{1,0:T(8,128)(2,1)S(1)} %get-tuple-element.33.refs_0_), channel_id=1, source_target_pairs={{0,4},{1,5},{2,6},{3,7},{4,0},{5,1},{6,2},{7,3},{8,12},{9,13},{10,... | collective-permute-start | bytes 196616 | tf_op jit(solution)/shard_map/ppermute | solution.py:199
  28.1 2.3 %collective-permute-start.8 = (bf16[256,128]{1,0:T(8,128)(2,1)S(1)}, bf16[256,128]{1,0:T(8,128)(2,1)S(1)}, u32[]{:S(2)}, u32[]{:S(2)}) collective-permute-start(bf16[256,128]{1,0:T(8,128)(2,1)S(1)} %get-tuple-element.33.refs_0_), channel_id=1, source_target_pairs={{0,12},{1,13},{2,14},{3,15},{4,8},{5,9},{6,10},{7,11},{8,4},{9,5},... | collective-permute-start | bytes 196616 | tf_op jit(solution)/shard_map/ppermute | solution.py:199
  30.4 0.4 collective-permute-start.7
  30.7 1.3 %gauss_bands.1 = (bf16[12,256,128]{2,1,0:T(8,128)(2,1)S(1)}, bf16[12,128,256]{2,1,0:T(8,128)(2,1)S(1)}) custom-call(f32[12]{0:T(128)S(1)} %copy-done.7), custom_call_target="tpu_custom_call" | custom-call | tf_op jit(solution)/shard_map/gauss_bands/pallas_call | solution.py:479
  32.0 0.6 %plan.1 = (s32[32,128]{1,0:T(8,128)S(1)}, f32[16,128]{1,0:T(8,128)S(1)}) custom-call(s32[1]{0:T(128)} %bitcast.me_ref, bf16[272,128]{1,0:T(8,128)(2,1)S(1)} %get-tuple-element.25.refs_0_, bf16[272,128]{1,0:T(8,128)(2,1)S(1)} %collective-permute-done.3.refs_1_, bf16[272,128]{1,0:T(8,128)(2,1)S(1)} %collective-permute-done.4.refs_2_, ...), custom_call_target="tpu_custom_call" | custom-call | tf_op jit(solution)/shard_map/plan/pallas_call | solution.py:504
  32.6 1.6 %collective-permute-start.9 = (bf16[512,128]{1,0:T(8,128)(2,1)S(1)}, bf16[512,128]{1,0:T(8,128)(2,1)S(1)}, u32[]{:S(2)}, u32[]{:S(2)}) collective-permute-start(bf16[512,128]{1,0:T(8,128)(2,1)S(1)} %join.4.refs_0_), channel_id=1, source_target_pairs={{0,2},{1,3},{2,0},{3,1},{4,6},{5,7},{6,4},{7,5},{8,10},{9,11},{10,... | collective-permute-start | bytes 393224 | tf_op jit(solution)/shard_map/ppermute | solution.py:199
  34.2 0.1 collective-permute-done.8.refs_1_
  34.3 1.9 %collective-permute-done.7.refs_0_ = bf16[256,128]{1,0:T(8,128)(2,1)S(1)} collective-permute-done((bf16[256,128]{1,0:T(8,128)(2,1)S(1)}, bf16[256,128]{1,0:T(8,128)(2,1)S(1)}, u32[]{:S(2)}, u32[]{:S(2)}) %collective-permute-start.7) | collective-permute-done | bytes 65568 | tf_op jit(solution)/shard_map/ppermute | solution.py:199
  36.2 1.6 %collective-permute-start.10 = (bf16[512,128]{1,0:T(8,128)(2,1)S(1)}, bf16[512,128]{1,0:T(8,128)(2,1)S(1)}, u32[]{:S(2)}, u32[]{:S(2)}) collective-permute-start(bf16[512,128]{1,0:T(8,128)(2,1)S(1)} %join.5.refs_1_), channel_id=1, source_target_pairs={{0,2},{1,3},{2,0},{3,1},{4,6},{5,7},{6,4},{7,5},{8,10},{9,11},{10,... | collective-permute-start | bytes 393224 | tf_op jit(solution)/shard_map/ppermute | solution.py:199
  37.8 0.1 collective-permute-start.11
  37.9 0.5 collective-permute-done.9.refs_0_
  38.4 2.9 %collective-permute-done.10.refs_1_ = bf16[512,128]{1,0:T(8,128)(2,1)S(1)} collective-permute-done((bf16[512,128]{1,0:T(8,128)(2,1)S(1)}, bf16[512,128]{1,0:T(8,128)(2,1)S(1)}, u32[]{:S(2)}, u32[]{:S(2)}) %collective-permute-start.10) | collective-permute-done | bytes 131104 | tf_op jit(solution)/shard_map/ppermute | solution.py:199
  41.3 0.1 collective-permute-start.12
  41.4 1.5 %collective-permute-done.12.refs_3_ = bf16[1024,128]{1,0:T(8,128)(2,1)S(1)} collective-permute-done((bf16[1024,128]{1,0:T(8,128)(2,1)S(1)}, bf16[1024,128]{1,0:T(8,128)(2,1)S(1)}, u32[]{:S(2)}, u32[]{:S(2)}) %collective-permute-start.12) | collective-permute-done | bytes 262176 | tf_op jit(solution)/shard_map/ppermute | solution.py:199
  42.9 8.3 %match.1 = (bf16[256,128]{1,0:T(8,128)(2,1)}, f32[256,128]{1,0:T(8,128)}) custom-call(bf16[12,256,128]{2,1,0:T(8,128)(2,1)S(1)} %get-tuple-element.19.refs_2_.across_bands, bf16[12,128,256]{2,1,0:T(8,128)(2,1)S(1)} %get-tuple-element.20.down_bands, f32[256,128]{1,0:T(8,128)S(1)} %get-tuple-element.29.coadd, f32[16,128]{1,0:T(8,128)S(1)} %get-tuple-element.30.weight_sum, ...), custom_call_target="tpu_custom_call" | custom-call | tf_op jit(solution)/shard_map/match/pallas_call | solution.py:519
  (21 shorter events, 0.1 us)
Async XLA Ops:
  1.3 0.7 %copy-start.4 = (f32[1,2]{1,0:T(1,128)S(1)}, f32[1,2]{1,0:T(1,128)}, u32[]{:S(2)}) copy-start(f32[1,2]{1,0:T(1,128)} %fraction_in.1) | copy-start | bytes 28
  1.3 0.7 %copy-start.5 = (s32[1,6]{1,0:T(1,128)S(1)}, s32[1,6]{1,0:T(1,128)}, u32[]{:S(2)}) copy-start(s32[1,6]{1,0:T(1,128)} %index_in.1) | copy-start | bytes 76
  1.3 0.7 %copy-start.6 = (f32[1,6]{1,0:T(1,128)S(1)}, f32[1,6]{1,0:T(1,128)}, u32[]{:S(2)}) copy-start(f32[1,6]{1,0:T(1,128)} %coef_in.1) | copy-start | bytes 76
  1.3 0.7 %copy-start.1 = (s32[1,128,1]{1,2,0:T(1,128)S(1)}, s32[1,128,1]{1,2,0:T(1,128)}, u32[]{:S(2)}) copy-start(s32[1,128,1]{1,2,0:T(1,128)} %param.13) | copy-start | bytes 1540
  1.3 0.7 %copy-start.2 = (s32[1,128]{1,0:T(1,128)S(1)}, s32[1,128]{1,0:T(1,128)}, u32[]{:S(2)}) copy-start(s32[1,128]{1,0:T(1,128)} %slot_in.1) | copy-start | bytes 1540
  1.3 0.7 %copy-start.3 = (s32[1,2]{1,0:T(1,128)S(1)}, s32[1,2]{1,0:T(1,128)}, u32[]{:S(2)}) copy-start(s32[1,2]{1,0:T(1,128)} %offset_in.1) | copy-start | bytes 28
  2.0 1.0 %copy-start = (bf16[1,256,1024]{2,1,0:T(8,128)(2,1)S(1)}, bf16[1,256,1024]{2,1,0:T(8,128)(2,1)}, u32[]{:S(2)}) copy-start(bf16[1,256,1024]{2,1,0:T(8,128)(2,1)} %param.9) | copy-start | bytes 1572868
  5.6 1.7 %collective-permute-start.1 = (bf16[1088,128]{1,0:T(8,128)(2,1)S(1)}, bf16[1088,128]{1,0:T(8,128)(2,1)S(1)}, u32[]{:S(2)}, u32[]{:S(2)}) collective-permute-start(bf16[1088,128]{1,0:T(8,128)(2,1)S(1)} %get-tuple-element.24), channel_id=1, source_target_pairs={{0,1},{1,0},{2,3},{3,2},{4,5},{5,4},{6,7},{7,6},{8,9},{9,8},{10,11... | collective-permute-start | bytes 835592 | tf_op jit(solution)/shard_map/ppermute | solution.py:199
  6.1 4.2 %collective-permute-start = (bf16[1088,128]{1,0:T(8,128)(2,1)S(1)}, bf16[1088,128]{1,0:T(8,128)(2,1)S(1)}, u32[]{:S(2)}, u32[]{:S(2)}) collective-permute-start(bf16[1088,128]{1,0:T(8,128)(2,1)S(1)} %get-tuple-element.22), channel_id=1, source_target_pairs={{0,1},{1,0},{2,3},{3,2},{4,5},{5,4},{6,7},{7,6},{8,9},{9,8},{10,11... | collective-permute-start | bytes 835592 | tf_op jit(solution)/shard_map/ppermute | solution.py:199
  7.4 9.9 %collective-permute-start.2 = (bf16[1088,128]{1,0:T(8,128)(2,1)S(1)}, bf16[1088,128]{1,0:T(8,128)(2,1)S(1)}, u32[]{:S(2)}, u32[]{:S(2)}) collective-permute-start(bf16[1088,128]{1,0:T(8,128)(2,1)S(1)} %add_parts.2), channel_id=1, source_target_pairs={{0,2},{1,3},{2,0},{3,1},{4,6},{5,7},{6,4},{7,5},{8,10},{9,11},{10,... | collective-permute-start | bytes 835592 | tf_op jit(solution)/shard_map/ppermute | solution.py:199
  17.4 7.0 %collective-permute-start.3 = (bf16[272,128]{1,0:T(8,128)(2,1)S(1)}, bf16[272,128]{1,0:T(8,128)(2,1)S(1)}, u32[]{:S(2)}, u32[]{:S(2)}) collective-permute-start(bf16[272,128]{1,0:T(8,128)(2,1)S(1)} %get-tuple-element.26), channel_id=1, source_target_pairs={{0,12},{1,13},{2,14},{3,15},{4,8},{5,9},{6,10},{7,11},{8,4},{9,5},... | collective-permute-start | bytes 208904 | tf_op jit(solution)/shard_map/ppermute | solution.py:199
  21.3 5.5 %collective-permute-start.4 = (bf16[272,128]{1,0:T(8,128)(2,1)S(1)}, bf16[272,128]{1,0:T(8,128)(2,1)S(1)}, u32[]{:S(2)}, u32[]{:S(2)}) collective-permute-start(bf16[272,128]{1,0:T(8,128)(2,1)S(1)} %get-tuple-element.27), channel_id=1, source_target_pairs={{0,8},{1,9},{2,10},{3,11},{4,12},{5,13},{6,14},{7,15},{8,0},{9,1},... | collective-permute-start | bytes 208904 | tf_op jit(solution)/shard_map/ppermute | solution.py:199
  21.3 5.6 %collective-permute-start.5 = (bf16[272,128]{1,0:T(8,128)(2,1)S(1)}, bf16[272,128]{1,0:T(8,128)(2,1)S(1)}, u32[]{:S(2)}, u32[]{:S(2)}) collective-permute-start(bf16[272,128]{1,0:T(8,128)(2,1)S(1)} %get-tuple-element.28), channel_id=1, source_target_pairs={{0,4},{1,5},{2,6},{3,7},{4,0},{5,1},{6,2},{7,3},{8,12},{9,13},{10,... | collective-permute-start | bytes 208904 | tf_op jit(solution)/shard_map/ppermute | solution.py:199
  27.2 3.6 %copy-start.7 = (f32[12]{0:T(128)S(1)}, f32[12]{0:T(128)}, u32[]{:S(2)}) copy-start(f32[12]{0:T(128)} %basis_width.1) | copy-start | bytes 148
  27.2 5.4 %collective-permute-start.6 = (bf16[256,128]{1,0:T(8,128)(2,1)S(1)}, bf16[256,128]{1,0:T(8,128)(2,1)S(1)}, u32[]{:S(2)}, u32[]{:S(2)}) collective-permute-start(bf16[256,128]{1,0:T(8,128)(2,1)S(1)} %get-tuple-element.33.refs_0_), channel_id=1, source_target_pairs={{0,4},{1,5},{2,6},{3,7},{4,0},{5,1},{6,2},{7,3},{8,12},{9,13},{10,... | collective-permute-start | bytes 196616 | tf_op jit(solution)/shard_map/ppermute | solution.py:199
  28.1 6.2 %collective-permute-start.8 = (bf16[256,128]{1,0:T(8,128)(2,1)S(1)}, bf16[256,128]{1,0:T(8,128)(2,1)S(1)}, u32[]{:S(2)}, u32[]{:S(2)}) collective-permute-start(bf16[256,128]{1,0:T(8,128)(2,1)S(1)} %get-tuple-element.33.refs_0_), channel_id=1, source_target_pairs={{0,12},{1,13},{2,14},{3,15},{4,8},{5,9},{6,10},{7,11},{8,4},{9,5},... | collective-permute-start | bytes 196616 | tf_op jit(solution)/shard_map/ppermute | solution.py:199
  30.4 5.8 %collective-permute-start.7 = (bf16[256,128]{1,0:T(8,128)(2,1)S(1)}, bf16[256,128]{1,0:T(8,128)(2,1)S(1)}, u32[]{:S(2)}, u32[]{:S(2)}) collective-permute-start(bf16[256,128]{1,0:T(8,128)(2,1)S(1)} %get-tuple-element.33.refs_0_), channel_id=1, source_target_pairs={{0,8},{1,9},{2,10},{3,11},{4,12},{5,13},{6,14},{7,15},{8,0},{9,1},... | collective-permute-start | bytes 196616 | tf_op jit(solution)/shard_map/ppermute | solution.py:199
  32.6 5.8 %collective-permute-start.9 = (bf16[512,128]{1,0:T(8,128)(2,1)S(1)}, bf16[512,128]{1,0:T(8,128)(2,1)S(1)}, u32[]{:S(2)}, u32[]{:S(2)}) collective-permute-start(bf16[512,128]{1,0:T(8,128)(2,1)S(1)} %join.4.refs_0_), channel_id=1, source_target_pairs={{0,2},{1,3},{2,0},{3,1},{4,6},{5,7},{6,4},{7,5},{8,10},{9,11},{10,... | collective-permute-start | bytes 393224 | tf_op jit(solution)/shard_map/ppermute | solution.py:199
  36.2 5.0 %collective-permute-start.10 = (bf16[512,128]{1,0:T(8,128)(2,1)S(1)}, bf16[512,128]{1,0:T(8,128)(2,1)S(1)}, u32[]{:S(2)}, u32[]{:S(2)}) collective-permute-start(bf16[512,128]{1,0:T(8,128)(2,1)S(1)} %join.5.refs_1_), channel_id=1, source_target_pairs={{0,2},{1,3},{2,0},{3,1},{4,6},{5,7},{6,4},{7,5},{8,10},{9,11},{10,... | collective-permute-start | bytes 393224 | tf_op jit(solution)/shard_map/ppermute | solution.py:199
  37.8 3.5 %collective-permute-start.11 = (bf16[1024,128]{1,0:T(8,128)(2,1)S(1)}, bf16[1024,128]{1,0:T(8,128)(2,1)S(1)}, u32[]{:S(2)}, u32[]{:S(2)}) collective-permute-start(bf16[1024,128]{1,0:T(8,128)(2,1)S(1)} %join.6.refs_0_), channel_id=1, source_target_pairs={{0,1},{1,0},{2,3},{3,2},{4,5},{5,4},{6,7},{7,6},{8,9},{9,8},{10,11... | collective-permute-start | bytes 786440 | tf_op jit(solution)/shard_map/ppermute | solution.py:199
  41.3 1.6 %collective-permute-start.12 = (bf16[1024,128]{1,0:T(8,128)(2,1)S(1)}, bf16[1024,128]{1,0:T(8,128)(2,1)S(1)}, u32[]{:S(2)}, u32[]{:S(2)}) collective-permute-start(bf16[1024,128]{1,0:T(8,128)(2,1)S(1)} %join.7.refs_1_), channel_id=1, source_target_pairs={{0,1},{1,0},{2,3},{3,2},{4,5},{5,4},{6,7},{7,6},{8,9},{9,8},{10,11... | collective-permute-start | bytes 786440 | tf_op jit(solution)/shard_map/ppermute | solution.py:199

commit v10 on v9

--- a/solution.py
+++ b/solution.py
@@ -232,8 +232,8 @@
     low = join(own, *[far[away] for away in range(1, count)])
     low_side = swap(low, peers, 2)
     line = join(low, high)
-    side = join(low_side, high_side)
-    return line, side, swap(line, peers, 1), swap(side, peers, 1)
+    high_far = swap(high_side, peers, 1)
+    return line, low_side, high_side, swap(line, peers, 1), swap(low_side, peers, 1), high_far
 
 
 def summed_terms(terms, here):
@@ -357,13 +357,14 @@
     scales,
     *refs,
 ):
-    pieces, (template, out, table, window, blurred, matched) = refs[:4], refs[4:]
+    pieces, (template, out, table, window, blurred, matched) = refs[:6], refs[6:]
     groups = pl.cdiv(most, GROUP)
     high = GROUP * TALL
-    length = pieces[0].shape[0]
-    for i, piece in enumerate(pieces):
-        table[i * length : (i + 1) * length, :] = piece[...]
-    table[4 * length :, :] = jnp.zeros((BH, BW), jnp.bfloat16)
+    start = 0
+    for piece in pieces:
+        table[start : start + piece.shape[0], :] = piece[...]
+        start += piece.shape[0]
+    table[start:, :] = jnp.zeros((BH, BW), jnp.bfloat16)
     matched[...] = jnp.zeros_like(matched)
     template[...] = coadd[...].astype(jnp.bfloat16)
     if most % GROUP:
@@ -522,7 +523,7 @@
             jax.ShapeDtypeStruct((BOXES, BW), jnp.bfloat16),
             jax.ShapeDtypeStruct((BOXES, BW), jnp.float32),
         ],
-        in_specs=[VMEM] * 4 + [SMEM] * 2 + [VMEM] * 4,
+        in_specs=[VMEM] * 4 + [SMEM] * 2 + [VMEM] * 6,
         out_specs=[VMEM] * 2,
         scratch_shapes=[
             pltpu.VMEM(((peers * PS + 1) * BH, BW), jnp.bfloat16),

time: 51.4 us -> 51.2 us (level)
    ppermute x13 -> x14, waiting for transfers between devices: 19.9 us -> 19.7 us  [swap(): return lax.ppermute(x, 'visit', [(i, i ^ bit) for i in range(axis_size)])]
    ppermute x13 -> x14, starting transfers between devices: 15 us -> 14.9 us  [swap(): return lax.ppermute(x, 'visit', [(i, i ^ bit) for i in range(axis_size)])]
  transfers between devices with their start and end apart: 13 -> 14, of which waited for: 10 -> 10; matrix products, arithmetic and copies ran while one was open for 0% -> 0% of each run, Pallas kernels for 4% -> 4%
where the time goes in v10:
time: 51.2 us; the launch traced here: 51 us
  waiting for transfers between devices  19.7 us (38%)
  starting transfers between devices  14.9 us (29%)
  Pallas kernels  13.3 us (26%)
  local copies, waits for them, and re-layouts  1.73 us (3%)
  between operations  1.42 us (3%)
    ppermute x14, waiting for transfers between devices, swap(): return lax.ppermute(x, 'visit', [(i, i ^ bit) for i in range(axis_size)])  19.7 us
    ppermute x14, starting transfers between devices, swap(): return lax.ppermute(x, 'visit', [(i, i ^ bit) for i in range(axis_size)])  14.9 us
    pallas_call x1, Pallas kernels, shards(): pl.pallas_call(functools.partial(match_kernel, peers, bases, most, steps)...  8.4 us
    pallas_call x1, Pallas kernels, shards(): pl.pallas_call(functools.partial(warp_kernel, peers, bases), out_shape=[q...  2.5 us
    unnamed x16, local copies, waits for them, and re-layouts  1.73 us
    pallas_call x1, Pallas kernels, shards(): pl.pallas_call(gauss_kernel, out_shape=[jax.ShapeDtypeStruct((table_size,...  1.25 us
  transfers between devices with their start and end apart: 14, of which 10 were waited for; matrix products, arithmetic and copies ran while one was open for 0% of the time, Pallas kernels for 4%

profile of v10, /device:TPU:0, one launch (start us, length us, event | category | flops | bytes accessed | tf_op | source)
XLA Modules:
  0.0 51.0 jit_solution(2973694766149661356)
XLA Ops:
  1.3 0.6 %copy-done.4 = f32[1,2]{1,0:T(1,128)S(1)} copy-done((f32[1,2]{1,0:T(1,128)S(1)}, f32[1,2]{1,0:T(1,128)}, u32[]{:S(2)}) %copy-start.4) | copy-done | bytes 32
  1.9 0.0 copy-done.5
  2.0 1.0 %copy-done = bf16[1,256,1024]{2,1,0:T(8,128)(2,1)S(1)} copy-done((bf16[1,256,1024]{2,1,0:T(8,128)(2,1)S(1)}, bf16[1,256,1024]{2,1,0:T(8,128)(2,1)}, u32[]{:S(2)}) %copy-start) | copy-done | bytes 524312
  3.1 2.5 %warp.1 = (bf16[1088,128]{1,0:T(8,128)(2,1)S(1)}, bf16[1088,128]{1,0:T(8,128)(2,1)S(1)}, bf16[1088,128]{1,0:T(8,128)(2,1)S(1)}, bf16[1088,128]{1,0:T(8,128)(2,1)S(1)}) custom-call(s32[1]{0:T(128)} %bitcast.me_ref, bf16[256,1024]{1,0:T(8,128)(2,1)S(1)} %bitcast.7, s32[1,128]{1,0:T(1,128)S(1)} %bitcast.8, s32[1,128]{1,0:T(1,128)S(1)} %copy-done.2, ...), custom_call_target="tpu_custom_call" | custom-call | tf_op jit(solution)/shard_map/warp/pallas_call | solution.py:446
  5.6 0.5 %collective-permute-start.1 = (bf16[1088,128]{1,0:T(8,128)(2,1)S(1)}, bf16[1088,128]{1,0:T(8,128)(2,1)S(1)}, u32[]{:S(2)}, u32[]{:S(2)}) collective-permute-start(bf16[1088,128]{1,0:T(8,128)(2,1)S(1)} %get-tuple-element.24), channel_id=1, source_target_pairs={{0,1},{1,0},{2,3},{3,2},{4,5},{5,4},{6,7},{7,6},{8,9},{9,8},{10,11... | collective-permute-start | bytes 835592 | tf_op jit(solution)/shard_map/ppermute | solution.py:199
  6.1 0.1 collective-permute-start
  6.2 1.1 %collective-permute-done.1.refs_1_ = bf16[1088,128]{1,0:T(8,128)(2,1)S(1)} collective-permute-done((bf16[1088,128]{1,0:T(8,128)(2,1)S(1)}, bf16[1088,128]{1,0:T(8,128)(2,1)S(1)}, u32[]{:S(2)}, u32[]{:S(2)}) %collective-permute-start.1) | collective-permute-done | bytes 278560 | tf_op jit(solution)/shard_map/ppermute | solution.py:199
  7.3 0.1 add_parts.2
  7.4 3.0 %collective-permute-start.2 = (bf16[1088,128]{1,0:T(8,128)(2,1)S(1)}, bf16[1088,128]{1,0:T(8,128)(2,1)S(1)}, u32[]{:S(2)}, u32[]{:S(2)}) collective-permute-start(bf16[1088,128]{1,0:T(8,128)(2,1)S(1)} %add_parts.2), channel_id=1, source_target_pairs={{0,2},{1,3},{2,0},{3,1},{4,6},{5,7},{6,4},{7,5},{8,10},{9,11},{10,... | collective-permute-start | bytes 835592 | tf_op jit(solution)/shard_map/ppermute | solution.py:199
  10.3 7.0 %collective-permute-done.2.refs_2_ = bf16[1088,128]{1,0:T(8,128)(2,1)S(1)} collective-permute-done((bf16[1088,128]{1,0:T(8,128)(2,1)S(1)}, bf16[1088,128]{1,0:T(8,128)(2,1)S(1)}, u32[]{:S(2)}, u32[]{:S(2)}) %collective-permute-start.2) | collective-permute-done | bytes 278560 | tf_op jit(solution)/shard_map/ppermute | solution.py:199
  17.3 0.1 add_parts.3
  17.4 3.9 %collective-permute-start.3 = (bf16[272,128]{1,0:T(8,128)(2,1)S(1)}, bf16[272,128]{1,0:T(8,128)(2,1)S(1)}, u32[]{:S(2)}, u32[]{:S(2)}) collective-permute-start(bf16[272,128]{1,0:T(8,128)(2,1)S(1)} %get-tuple-element.26), channel_id=1, source_target_pairs={{0,12},{1,13},{2,14},{3,15},{4,8},{5,9},{6,10},{7,11},{8,4},{9,5},... | collective-permute-start | bytes 208904 | tf_op jit(solution)/shard_map/ppermute | solution.py:199
  21.3 0.6 %collective-permute-start.5 = (bf16[272,128]{1,0:T(8,128)(2,1)S(1)}, bf16[272,128]{1,0:T(8,128)(2,1)S(1)}, u32[]{:S(2)}, u32[]{:S(2)}) collective-permute-start(bf16[272,128]{1,0:T(8,128)(2,1)S(1)} %get-tuple-element.28), channel_id=1, source_target_pairs={{0,4},{1,5},{2,6},{3,7},{4,0},{5,1},{6,2},{7,3},{8,12},{9,13},{10,... | collective-permute-start | bytes 208904 | tf_op jit(solution)/shard_map/ppermute | solution.py:199
  21.9 2.5 %collective-permute-done.3.refs_1_ = bf16[272,128]{1,0:T(8,128)(2,1)S(1)} collective-permute-done((bf16[272,128]{1,0:T(8,128)(2,1)S(1)}, bf16[272,128]{1,0:T(8,128)(2,1)S(1)}, u32[]{:S(2)}, u32[]{:S(2)}) %collective-permute-start.3) | collective-permute-done | bytes 69664 | tf_op jit(solution)/shard_map/ppermute | solution.py:199
  24.4 2.4 %collective-permute-done.4.refs_2_ = bf16[272,128]{1,0:T(8,128)(2,1)S(1)} collective-permute-done((bf16[272,128]{1,0:T(8,128)(2,1)S(1)}, bf16[272,128]{1,0:T(8,128)(2,1)S(1)}, u32[]{:S(2)}, u32[]{:S(2)}) %collective-permute-start.4) | collective-permute-done | bytes 69664 | tf_op jit(solution)/shard_map/ppermute | solution.py:199
  26.8 0.1 collective-permute-done.5.refs_3_
  26.8 0.3 template.1
  27.2 0.9 %collective-permute-start.6 = (bf16[256,128]{1,0:T(8,128)(2,1)S(1)}, bf16[256,128]{1,0:T(8,128)(2,1)S(1)}, u32[]{:S(2)}, u32[]{:S(2)}) collective-permute-start(bf16[256,128]{1,0:T(8,128)(2,1)S(1)} %get-tuple-element.33.refs_0_), channel_id=1, source_target_pairs={{0,4},{1,5},{2,6},{3,7},{4,0},{5,1},{6,2},{7,3},{8,12},{9,13},{10,... | collective-permute-start | bytes 196616 | tf_op jit(solution)/shard_map/ppermute | solution.py:199
  28.1 2.3 %collective-permute-start.8 = (bf16[256,128]{1,0:T(8,128)(2,1)S(1)}, bf16[256,128]{1,0:T(8,128)(2,1)S(1)}, u32[]{:S(2)}, u32[]{:S(2)}) collective-permute-start(bf16[256,128]{1,0:T(8,128)(2,1)S(1)} %get-tuple-element.33.refs_0_), channel_id=1, source_target_pairs={{0,12},{1,13},{2,14},{3,15},{4,8},{5,9},{6,10},{7,11},{8,4},{9,5},... | collective-permute-start | bytes 196616 | tf_op jit(solution)/shard_map/ppermute | solution.py:199
  30.4 0.4 collective-permute-start.7
  30.7 1.3 %gauss_bands.1 = (bf16[12,256,128]{2,1,0:T(8,128)(2,1)S(1)}, bf16[12,128,256]{2,1,0:T(8,128)(2,1)S(1)}) custom-call(f32[12]{0:T(128)S(1)} %copy-done.7), custom_call_target="tpu_custom_call" | custom-call | tf_op jit(solution)/shard_map/gauss_bands/pallas_call | solution.py:480
  32.0 0.6 %plan.1 = (s32[32,128]{1,0:T(8,128)S(1)}, f32[16,128]{1,0:T(8,128)S(1)}) custom-call(s32[1]{0:T(128)} %bitcast.me_ref, bf16[272,128]{1,0:T(8,128)(2,1)S(1)} %get-tuple-element.25.refs_0_, bf16[272,128]{1,0:T(8,128)(2,1)S(1)} %collective-permute-done.3.refs_1_, bf16[272,128]{1,0:T(8,128)(2,1)S(1)} %collective-permute-done.4.refs_2_, ...), custom_call_target="tpu_custom_call" | custom-call | tf_op jit(solution)/shard_map/plan/pallas_call | solution.py:505
  32.6 1.6 %collective-permute-start.9 = (bf16[512,128]{1,0:T(8,128)(2,1)S(1)}, bf16[512,128]{1,0:T(8,128)(2,1)S(1)}, u32[]{:S(2)}, u32[]{:S(2)}) collective-permute-start(bf16[512,128]{1,0:T(8,128)(2,1)S(1)} %join.3.refs_0_), channel_id=1, source_target_pairs={{0,2},{1,3},{2,0},{3,1},{4,6},{5,7},{6,4},{7,5},{8,10},{9,11},{10,... | collective-permute-start | bytes 393224 | tf_op jit(solution)/shard_map/ppermute | solution.py:199
  34.2 0.1 collective-permute-done.8.refs_1_
  34.3 1.9 %collective-permute-done.7.refs_0_ = bf16[256,128]{1,0:T(8,128)(2,1)S(1)} collective-permute-done((bf16[256,128]{1,0:T(8,128)(2,1)S(1)}, bf16[256,128]{1,0:T(8,128)(2,1)S(1)}, u32[]{:S(2)}, u32[]{:S(2)}) %collective-permute-start.7) | collective-permute-done | bytes 65568 | tf_op jit(solution)/shard_map/ppermute | solution.py:199
  36.2 1.6 %collective-permute-start.10 = (bf16[512,128]{1,0:T(8,128)(2,1)S(1)}, bf16[512,128]{1,0:T(8,128)(2,1)S(1)}, u32[]{:S(2)}, u32[]{:S(2)}) collective-permute-start(bf16[512,128]{1,0:T(8,128)(2,1)S(1)} %join.4.refs_1_), channel_id=1, source_target_pairs={{0,2},{1,3},{2,0},{3,1},{4,6},{5,7},{6,4},{7,5},{8,10},{9,11},{10,... | collective-permute-start | bytes 393224 | tf_op jit(solution)/shard_map/ppermute | solution.py:199
  37.8 0.1 collective-permute-start.11
  37.9 0.5 collective-permute-done.9.refs_1_
  38.4 0.0 collective-permute-start.12
  38.4 2.9 %collective-permute-done.10.refs_2_ = bf16[512,128]{1,0:T(8,128)(2,1)S(1)} collective-permute-done((bf16[512,128]{1,0:T(8,128)(2,1)S(1)}, bf16[512,128]{1,0:T(8,128)(2,1)S(1)}, u32[]{:S(2)}, u32[]{:S(2)}) %collective-permute-start.10) | collective-permute-done | bytes 131104 | tf_op jit(solution)/shard_map/ppermute | solution.py:199
  41.3 1.3 %collective-permute-done.13.refs_5_ = bf16[512,128]{1,0:T(8,128)(2,1)S(1)} collective-permute-done((bf16[512,128]{1,0:T(8,128)(2,1)S(1)}, bf16[512,128]{1,0:T(8,128)(2,1)S(1)}, u32[]{:S(2)}, u32[]{:S(2)}) %collective-permute-start.13) | collective-permute-done | bytes 131104 | tf_op jit(solution)/shard_map/ppermute | solution.py:199
  42.6 8.4 %match.1 = (bf16[256,128]{1,0:T(8,128)(2,1)}, f32[256,128]{1,0:T(8,128)}) custom-call(bf16[12,256,128]{2,1,0:T(8,128)(2,1)S(1)} %get-tuple-element.19.refs_2_.across_bands, bf16[12,128,256]{2,1,0:T(8,128)(2,1)S(1)} %get-tuple-element.20.down_bands, f32[256,128]{1,0:T(8,128)S(1)} %get-tuple-element.29.coadd, f32[16,128]{1,0:T(8,128)S(1)} %get-tuple-element.30.weight_sum, ...), custom_call_target="tpu_custom_call" | custom-call | tf_op jit(solution)/shard_map/match/pallas_call | solution.py:520
  (22 shorter events, 0.1 us)
Async XLA Ops:
  1.3 0.7 %copy-start.4 = (f32[1,2]{1,0:T(1,128)S(1)}, f32[1,2]{1,0:T(1,128)}, u32[]{:S(2)}) copy-start(f32[1,2]{1,0:T(1,128)} %fraction_in.1) | copy-start | bytes 28
  1.3 0.7 %copy-start.5 = (s32[1,6]{1,0:T(1,128)S(1)}, s32[1,6]{1,0:T(1,128)}, u32[]{:S(2)}) copy-start(s32[1,6]{1,0:T(1,128)} %index_in.1) | copy-start | bytes 76
  1.3 0.7 %copy-start.6 = (f32[1,6]{1,0:T(1,128)S(1)}, f32[1,6]{1,0:T(1,128)}, u32[]{:S(2)}) copy-start(f32[1,6]{1,0:T(1,128)} %coef_in.1) | copy-start | bytes 76
  1.3 0.7 %copy-start.1 = (s32[1,128,1]{1,2,0:T(1,128)S(1)}, s32[1,128,1]{1,2,0:T(1,128)}, u32[]{:S(2)}) copy-start(s32[1,128,1]{1,2,0:T(1,128)} %param.13) | copy-start | bytes 1540
  1.3 0.7 %copy-start.2 = (s32[1,128]{1,0:T(1,128)S(1)}, s32[1,128]{1,0:T(1,128)}, u32[]{:S(2)}) copy-start(s32[1,128]{1,0:T(1,128)} %slot_in.1) | copy-start | bytes 1540
  1.3 0.7 %copy-start.3 = (s32[1,2]{1,0:T(1,128)S(1)}, s32[1,2]{1,0:T(1,128)}, u32[]{:S(2)}) copy-start(s32[1,2]{1,0:T(1,128)} %offset_in.1) | copy-start | bytes 28
  2.0 1.0 %copy-start = (bf16[1,256,1024]{2,1,0:T(8,128)(2,1)S(1)}, bf16[1,256,1024]{2,1,0:T(8,128)(2,1)}, u32[]{:S(2)}) copy-start(bf16[1,256,1024]{2,1,0:T(8,128)(2,1)} %param.9) | copy-start | bytes 1572868
  5.6 1.7 %collective-permute-start.1 = (bf16[1088,128]{1,0:T(8,128)(2,1)S(1)}, bf16[1088,128]{1,0:T(8,128)(2,1)S(1)}, u32[]{:S(2)}, u32[]{:S(2)}) collective-permute-start(bf16[1088,128]{1,0:T(8,128)(2,1)S(1)} %get-tuple-element.24), channel_id=1, source_target_pairs={{0,1},{1,0},{2,3},{3,2},{4,5},{5,4},{6,7},{7,6},{8,9},{9,8},{10,11... | collective-permute-start | bytes 835592 | tf_op jit(solution)/shard_map/ppermute | solution.py:199
  6.1 4.2 %collective-permute-start = (bf16[1088,128]{1,0:T(8,128)(2,1)S(1)}, bf16[1088,128]{1,0:T(8,128)(2,1)S(1)}, u32[]{:S(2)}, u32[]{:S(2)}) collective-permute-start(bf16[1088,128]{1,0:T(8,128)(2,1)S(1)} %get-tuple-element.22), channel_id=1, source_target_pairs={{0,1},{1,0},{2,3},{3,2},{4,5},{5,4},{6,7},{7,6},{8,9},{9,8},{10,11... | collective-permute-start | bytes 835592 | tf_op jit(solution)/shard_map/ppermute | solution.py:199
  7.4 9.9 %collective-permute-start.2 = (bf16[1088,128]{1,0:T(8,128)(2,1)S(1)}, bf16[1088,128]{1,0:T(8,128)(2,1)S(1)}, u32[]{:S(2)}, u32[]{:S(2)}) collective-permute-start(bf16[1088,128]{1,0:T(8,128)(2,1)S(1)} %add_parts.2), channel_id=1, source_target_pairs={{0,2},{1,3},{2,0},{3,1},{4,6},{5,7},{6,4},{7,5},{8,10},{9,11},{10,... | collective-permute-start | bytes 835592 | tf_op jit(solution)/shard_map/ppermute | solution.py:199
  17.4 7.0 %collective-permute-start.3 = (bf16[272,128]{1,0:T(8,128)(2,1)S(1)}, bf16[272,128]{1,0:T(8,128)(2,1)S(1)}, u32[]{:S(2)}, u32[]{:S(2)}) collective-permute-start(bf16[272,128]{1,0:T(8,128)(2,1)S(1)} %get-tuple-element.26), channel_id=1, source_target_pairs={{0,12},{1,13},{2,14},{3,15},{4,8},{5,9},{6,10},{7,11},{8,4},{9,5},... | collective-permute-start | bytes 208904 | tf_op jit(solution)/shard_map/ppermute | solution.py:199
  21.3 5.5 %collective-permute-start.4 = (bf16[272,128]{1,0:T(8,128)(2,1)S(1)}, bf16[272,128]{1,0:T(8,128)(2,1)S(1)}, u32[]{:S(2)}, u32[]{:S(2)}) collective-permute-start(bf16[272,128]{1,0:T(8,128)(2,1)S(1)} %get-tuple-element.27), channel_id=1, source_target_pairs={{0,8},{1,9},{2,10},{3,11},{4,12},{5,13},{6,14},{7,15},{8,0},{9,1},... | collective-permute-start | bytes 208904 | tf_op jit(solution)/shard_map/ppermute | solution.py:199
  21.3 5.6 %collective-permute-start.5 = (bf16[272,128]{1,0:T(8,128)(2,1)S(1)}, bf16[272,128]{1,0:T(8,128)(2,1)S(1)}, u32[]{:S(2)}, u32[]{:S(2)}) collective-permute-start(bf16[272,128]{1,0:T(8,128)(2,1)S(1)} %get-tuple-element.28), channel_id=1, source_target_pairs={{0,4},{1,5},{2,6},{3,7},{4,0},{5,1},{6,2},{7,3},{8,12},{9,13},{10,... | collective-permute-start | bytes 208904 | tf_op jit(solution)/shard_map/ppermute | solution.py:199
  27.2 3.6 %copy-start.7 = (f32[12]{0:T(128)S(1)}, f32[12]{0:T(128)}, u32[]{:S(2)}) copy-start(f32[12]{0:T(128)} %basis_width.1) | copy-start | bytes 148
  27.2 5.4 %collective-permute-start.6 = (bf16[256,128]{1,0:T(8,128)(2,1)S(1)}, bf16[256,128]{1,0:T(8,128)(2,1)S(1)}, u32[]{:S(2)}, u32[]{:S(2)}) collective-permute-start(bf16[256,128]{1,0:T(8,128)(2,1)S(1)} %get-tuple-element.33.refs_0_), channel_id=1, source_target_pairs={{0,4},{1,5},{2,6},{3,7},{4,0},{5,1},{6,2},{7,3},{8,12},{9,13},{10,... | collective-permute-start | bytes 196616 | tf_op jit(solution)/shard_map/ppermute | solution.py:199
  28.1 6.2 %collective-permute-start.8 = (bf16[256,128]{1,0:T(8,128)(2,1)S(1)}, bf16[256,128]{1,0:T(8,128)(2,1)S(1)}, u32[]{:S(2)}, u32[]{:S(2)}) collective-permute-start(bf16[256,128]{1,0:T(8,128)(2,1)S(1)} %get-tuple-element.33.refs_0_), channel_id=1, source_target_pairs={{0,12},{1,13},{2,14},{3,15},{4,8},{5,9},{6,10},{7,11},{8,4},{9,5},... | collective-permute-start | bytes 196616 | tf_op jit(solution)/shard_map/ppermute | solution.py:199
  30.4 5.8 %collective-permute-start.7 = (bf16[256,128]{1,0:T(8,128)(2,1)S(1)}, bf16[256,128]{1,0:T(8,128)(2,1)S(1)}, u32[]{:S(2)}, u32[]{:S(2)}) collective-permute-start(bf16[256,128]{1,0:T(8,128)(2,1)S(1)} %get-tuple-element.33.refs_0_), channel_id=1, source_target_pairs={{0,8},{1,9},{2,10},{3,11},{4,12},{5,13},{6,14},{7,15},{8,0},{9,1},... | collective-permute-start | bytes 196616 | tf_op jit(solution)/shard_map/ppermute | solution.py:199
  32.6 5.8 %collective-permute-start.9 = (bf16[512,128]{1,0:T(8,128)(2,1)S(1)}, bf16[512,128]{1,0:T(8,128)(2,1)S(1)}, u32[]{:S(2)}, u32[]{:S(2)}) collective-permute-start(bf16[512,128]{1,0:T(8,128)(2,1)S(1)} %join.3.refs_0_), channel_id=1, source_target_pairs={{0,2},{1,3},{2,0},{3,1},{4,6},{5,7},{6,4},{7,5},{8,10},{9,11},{10,... | collective-permute-start | bytes 393224 | tf_op jit(solution)/shard_map/ppermute | solution.py:199
  36.2 5.0 %collective-permute-start.10 = (bf16[512,128]{1,0:T(8,128)(2,1)S(1)}, bf16[512,128]{1,0:T(8,128)(2,1)S(1)}, u32[]{:S(2)}, u32[]{:S(2)}) collective-permute-start(bf16[512,128]{1,0:T(8,128)(2,1)S(1)} %join.4.refs_1_), channel_id=1, source_target_pairs={{0,2},{1,3},{2,0},{3,1},{4,6},{5,7},{6,4},{7,5},{8,10},{9,11},{10,... | collective-permute-start | bytes 393224 | tf_op jit(solution)/shard_map/ppermute | solution.py:199
  37.8 4.8 %collective-permute-start.11 = (bf16[1024,128]{1,0:T(8,128)(2,1)S(1)}, bf16[1024,128]{1,0:T(8,128)(2,1)S(1)}, u32[]{:S(2)}, u32[]{:S(2)}) collective-permute-start(bf16[1024,128]{1,0:T(8,128)(2,1)S(1)} %join.5.refs_0_), channel_id=1, source_target_pairs={{0,1},{1,0},{2,3},{3,2},{4,5},{5,4},{6,7},{7,6},{8,9},{9,8},{10,11... | collective-permute-start | bytes 786440 | tf_op jit(solution)/shard_map/ppermute | solution.py:199
  38.4 2.9 %collective-permute-start.12 = (bf16[512,128]{1,0:T(8,128)(2,1)S(1)}, bf16[512,128]{1,0:T(8,128)(2,1)S(1)}, u32[]{:S(2)}, u32[]{:S(2)}) collective-permute-start(bf16[512,128]{1,0:T(8,128)(2,1)S(1)} %collective-permute-done.9.refs_1_), channel_id=1, source_target_pairs={{0,1},{1,0},{2,3},{3,2},{4,5},{5,4},{6,7},{7,6},{8,9},{9,8},{10,11... | collective-permute-start | bytes 393224 | tf_op jit(solution)/shard_map/ppermute | solution.py:199
  41.3 1.3 %collective-permute-start.13 = (bf16[512,128]{1,0:T(8,128)(2,1)S(1)}, bf16[512,128]{1,0:T(8,128)(2,1)S(1)}, u32[]{:S(2)}, u32[]{:S(2)}) collective-permute-start(bf16[512,128]{1,0:T(8,128)(2,1)S(1)} %collective-permute-done.10.refs_2_), channel_id=1, source_target_pairs={{0,1},{1,0},{2,3},{3,2},{4,5},{5,4},{6,7},{7,6},{8,9},{9,8},{10,11... | collective-permute-start | bytes 393224 | tf_op jit(solution)/shard_map/ppermute | solution.py:199
